TPU v7x, 256 devices: a whole 4x4x8 slice. The times are simulated.
256 devices in a mesh: sta: 128 (over y_lo, x, z, core), win: 2 (over y_hi).
Axes of the slice: x: 4, y: 4 (y_hi: 2, y_lo: 2; y = y_hi * 2 + y_lo), z: 8, core: 2. Of those that a mesh axis runs over, the one named last changes fastest.
Arguments:
- raw_traces: bfloat16 [2, 32768, 4096], P('win', 'sta'), may hold values from -6 to 6
- fir_taps: bfloat16 [127], replicated, may hold values from -0.5 to 0.5
- source_slot: int32 [16, 2048], P('win', 'sta'), may hold values from 0 to 255, as said below
- present: int32 [16, 2048], P('win', 'sta'), may hold values 0 or 1
- lag_start: int32 [2048, 2048], P('sta'), may hold values from -2048 to 1920
Outputs:
- correlations: float32 [2048, 2048, 128], P('sta', 'win')
Inputs may be any that keep to these rules, and one draw needn't show every extreme that they name: `source_slot`: for each win index and each block of 16 stations on one sta index, the 128 entries are distinct; entry e names row e % 2 of the 2 rows that the file device with sta index e // 2 holds for this block. For every block, some file device holds 2 of its traces.
All inputs are finite; a program needn't handle non-finite values. No bound on the sum of `present` on one device may be relied on, other than what follows from the above.
Results may differ from a plain program's by a relative error of at most 0.0093.
Values may be sent and summed in bfloat16 or wider, within the bound.
No kernel may reach another device: no remote copies, remote signals or barrier semaphores. Data moves between devices by JAX's collectives and lax.ppermute only.
A program may use at most 128 MiB of HBM per device.

v0:
```python
import math

import jax
import jax.numpy as jnp
from jax import lax
from jax.sharding import PartitionSpec as P

L = 4096
TAPS = 127
FB = 64
BIN0 = 16
LAGW = 128


tile_len = 128
smooth_half = 4
floor_share = 0.25
spread_eps = 1e-06


def fir_matrix(fir_taps):
    half_taps = (TAPS - 1) // 2
    rows_in = jnp.arange(3 * tile_len, dtype=jnp.int32)[:, None]
    cols_out = jnp.arange(tile_len, dtype=jnp.int32)[None, :]
    offset = rows_in // tile_len - 1
    within = rows_in % tile_len
    tap_index = cols_out - within - offset * tile_len + half_taps
    tap_numbers = jnp.arange(TAPS, dtype=jnp.int32)
    matches = tap_index[:, :, None] == tap_numbers[None, None, :]
    picked = jnp.sum(jnp.where(matches, fir_taps.astype(jnp.float32)[None, None, :], 0.0), axis=2)
    return picked.astype(jnp.bfloat16)


def dft_table():
    sample = jnp.arange(L, dtype=jnp.int32)[:, None]
    bins = BIN0 + jnp.arange(FB, dtype=jnp.int32)[None, :]
    angle = (sample * bins % L).astype(jnp.float32) * (2.0 * math.pi / L)
    return jnp.concatenate([jnp.cos(angle), -jnp.sin(angle)], axis=1).astype(jnp.bfloat16)


def pick_rows(table, slot_list):
    selector = (slot_list[:, None] == jnp.arange(table.shape[0], dtype=jnp.int32)[None, :]).astype(
        table.dtype
    )
    return jnp.dot(selector, table, preferred_element_type=jnp.float32).astype(table.dtype)


def whiten(traces, fir_taps):
    row_count = traces.shape[0]
    tiles = L // tile_len
    blocked = traces.reshape(row_count, tiles, tile_len)
    padded = jnp.pad(blocked, ((0, 0), (1, 1), (0, 0)))
    windowed = jnp.concatenate([padded[:, :-2], padded[:, 1:-1], padded[:, 2:]], axis=2)
    filtered = jnp.dot(
        windowed.reshape(row_count * tiles, 3 * tile_len),
        fir_matrix(fir_taps),
        preferred_element_type=jnp.float32,
    )
    filtered = filtered.reshape(row_count, L).astype(jnp.bfloat16)
    spectrum = jnp.dot(filtered, dft_table(), preferred_element_type=jnp.float32)
    real_part = spectrum[:, :FB]
    imag_part = spectrum[:, FB:]
    magnitude = jnp.sqrt(real_part * real_part + imag_part * imag_part)
    padded_mag = jnp.pad(magnitude, ((0, 0), (smooth_half, smooth_half)))
    running = padded_mag[:, 0:FB]
    for shift_by in range(1, 2 * smooth_half + 1):
        running = running + padded_mag[:, shift_by : shift_by + FB]
    bins = jnp.arange(FB, dtype=jnp.int32)
    counts = (
        jnp.minimum(bins + smooth_half, FB - 1) - jnp.maximum(bins - smooth_half, 0) + 1
    ).astype(jnp.float32)
    amplitude = running / counts[None, :]
    spread = jnp.sqrt(jnp.mean(magnitude * magnitude, axis=1, keepdims=True) + spread_eps)
    divisor = jnp.maximum(amplitude, floor_share * spread)
    return jnp.concatenate([real_part / divisor, imag_part / divisor], axis=1).astype(jnp.bfloat16)


def lag_transform(cross_sum, lag_first, scale_factor):
    bins = BIN0 + jnp.arange(FB, dtype=jnp.int32)
    phase_int = lag_first[..., None] * bins % L
    alpha_angle = phase_int.astype(jnp.float32) * (2.0 * math.pi / L)
    cos_alpha = jnp.cos(alpha_angle)
    sin_alpha = jnp.sin(alpha_angle)
    cross_re = cross_sum[..., :FB]
    cross_im = cross_sum[..., FB:]
    rotated = jnp.concatenate(
        [cross_re * cos_alpha - cross_im * sin_alpha, cross_re * sin_alpha + cross_im * cos_alpha],
        axis=-1,
    )
    lag_index = jnp.arange(LAGW, dtype=jnp.int32)
    beta_angle = (bins[:, None] * lag_index[None, :] % L).astype(jnp.float32) * (2.0 * math.pi / L)
    lag_table = jnp.concatenate([jnp.cos(beta_angle), -jnp.sin(beta_angle)], axis=0)
    flat_rows = rotated.reshape(-1, 2 * FB)
    lag_values = jnp.dot(
        flat_rows, lag_table, precision=lax.Precision.HIGHEST, preferred_element_type=jnp.float32
    )
    return (lag_values * scale_factor).reshape(cross_sum.shape[0], cross_sum.shape[1], LAGW)


def make_accumulate(block_spectra, piece_rows):
    owned = block_spectra.shape[1]
    own_rows = jnp.concatenate([block_spectra[..., :FB], block_spectra[..., FB:]], axis=1)
    row_count = piece_rows.shape[1]
    other_rows = jnp.concatenate([piece_rows[..., :FB], piece_rows[..., FB:]], axis=1)
    product = jnp.einsum("wif,wjf->ijf", own_rows, other_rows, preferred_element_type=jnp.float32)
    real_part = product[:owned, :row_count] + product[owned:, row_count:]
    imag_part = product[owned:, :row_count] - product[:owned, row_count:]
    block_sum = jnp.concatenate([real_part, imag_part], axis=2)
    return block_sum


def per_device(raw_traces, fir_taps, source_slot, present, lag_start):
    local_raw = raw_traces[0]
    win_size = lax.axis_size("win")
    windows_here, owned = source_slot.shape
    flat_slots = source_slot.reshape(-1)
    keep_mask = present.reshape(-1, 1).astype(jnp.bfloat16)
    received = lax.all_to_all(local_raw, "sta", split_axis=0, concat_axis=0, tiled=True)
    traces = pick_rows(received, flat_slots)
    spectra = whiten(traces, fir_taps)
    spectra = (spectra * keep_mask).reshape(windows_here, owned, 2 * FB)
    scale_factor = 1.0 / math.sqrt(FB * windows_here * win_size)
    cross_sum = make_accumulate(spectra, lax.all_gather(spectra, "sta", axis=1, tiled=True))
    lag_values = lag_transform(cross_sum, lag_start, scale_factor)
    correlations = lax.psum_scatter(lag_values, "win", scatter_dimension=1, tiled=True)
    return correlations


def solution(mesh):
    placed = (P("win", "sta", None), P(), P("win", "sta"), P("win", "sta"), P("sta", None))
    return jax.shard_map(
        per_device, mesh=mesh, in_specs=placed, out_specs=P("sta", "win", None), check_vma=False
    )
```

profile of v0, /device:TPU:1, one launch (start us, length us, event | category | flops | bytes accessed | tf_op | source)
XLA Modules:
  0.0 626.0 jit_solution(1351621436093601959)
XLA Ops:
  6.5 4.4 all_to_all.8
  11.0 14.8 %all-to-all-start = ((bf16[128,2,4096]{2,1,0:T(2,128)(2,1)}), bf16[128,2,4096]{2,1,0:T(2,128)(2,1)S(1)}, u32[]{:S(2)}, u32[]{:S(2)}) async-start(bf16[128,2,4096]{2,1,0:T(2,128)(2,1)} %all_to_all.8), calls=%async_computation | async-start | bytes 4194304 | tf_op jit(solution)/shard_map/all_to_all | solution.py:118
  26.0 0.2 subtract_add_fusion
  26.1 2.5 select_reduce_fusion
  28.7 4.9 cosine_convert_fusion
  33.6 43.0 %all-to-all-done = bf16[128,2,4096]{2,1,0:T(2,128)(2,1)S(1)} async-done(((bf16[128,2,4096]{2,1,0:T(2,128)(2,1)}), bf16[128,2,4096]{2,1,0:T(2,128)(2,1)S(1)}, u32[]{:S(2)}, u32[]{:S(2)}) %all-to-all-start) | async-done | bytes 2097184 | tf_op jit(solution)/shard_map/all_to_all | solution.py:118
  76.6 2.2 all_to_all.10
  78.8 2.1 convolution_convert_fusion.1
  80.9 0.5 concatenate.36
  81.4 0.2 copy.30
  81.6 1.0 pad_slice_fusion.1
  82.7 1.0 convolution_convert_fusion
  83.7 0.5 convert_element_type.55
  84.2 0.4 fusion.16
  84.7 0.1 divide_convert_fusion.1
  84.8 0.1 copy.23
  84.9 0.1 copy.22
  85.1 0.1 pad_maximum_fusion.1
  85.2 0.2 copy.24
  85.4 0.8 copy.25
  86.2 0.2 reduce-scatter.2.cloned.1.call-start
  86.4 0.2 fusion.47
  86.7 212.8 %all-gather.2.cloned.1.call-done = bf16[8,2048,128]{2,0,1:T(8,128)(2,1)} async-done(((bf16[8,16,128]{2,0,1:T(8,128)(2,1)}), bf16[8,2048,128]{2,0,1:T(8,128)(2,1)}) %all-gather.2.cloned.1.call-update) | async-done | bytes 4194320 | tf_op jit(solution)/shard_map/all_gather | solution.py:123
  299.5 7.3 %fusion.65 = (bf16[8,2048,64]{2,0,1:T(8,128)(2,1)}, bf16[8,2048,64]{2,0,1:T(8,128)(2,1)}) fusion(bf16[8,2048,128]{2,0,1:T(8,128)(2,1)} %all-gather.2.cloned.1.call-done), kind=kLoop, calls=%fused_computation.116 | loop fusion | bytes 8388608 | tf_op jit(solution)/shard_map/slice | solution.py:104
  306.8 5.8 copy.28
  312.6 6.8 %copy.29 = bf16[8,2048,64]{1,0,2:T(8,128)(2,1)} copy(bf16[8,2048,64]{2,0,1:T(8,128)(2,1)} %get-tuple-element.12) | data formatting | bytes 4194304
  319.4 19.5 %convolution_bitcast_fusion = f32[32,4096,64]{1,0,2:T(8,128)} fusion(bf16[8,2048,64]{1,0,2:T(8,128)(2,1)} %copy.29, bf16[8,2048,64]{1,0,2:T(8,128)(2,1)S(1)} %copy.28, bf16[8,16,64]{1,0,2:T(8,128)(2,1)S(1)} %get-tuple-element.16, bf16[8,16,64]{1,0,2:T(8,128)(2,1)S(1)} %get-tuple-element.15), kind=kOutput, calls=%fused_computation.7 | convolution fusion | flops 142671872 | bytes 37781504 | tf_op jit(solution)/shard_map/wif,wjf->ijf/dot_general | solution.py:105
  338.9 38.1 %multiply_subtract_fusion = (f32[16,2048,64]{1,0,2:T(8,128)S(1)}, f32[16,2048,64]{1,0,2:T(8,128)S(1)}) fusion(s32[64]{0:T(128)S(1)} %iota_add_fusion.2, s32[16,2048]{1,0:T(8,128)S(1)} %copy-done, f32[32,4096,64]{1,0,2:T(8,128)} %convolution_bitcast_fusion), kind=kLoop, calls=%fused_computation.16 | loop fusion | flops 46137344 | bytes 50462976 | tf_op jit(solution)/shard_map/sub | solution.py:87
  377.1 2.4 pad_maximum_fusion
  379.4 14.1 %copy.31 = f32[16,8,16,2048]{3,1,2,0:T(8,128)S(1)} copy(f32[16,8,16,2048]{3,2,1,0:T(8,128)S(1)} %bitcast.19) | data formatting | bytes 33554432
  393.6 29.8 %convolution_multiply_fusion = f32[32768,128]{1,0:T(8,128)} fusion(f32[32768,128]{0,1:T(8,128)S(1)} %bitcast.18, f32[64,128]{1,0:T(8,128)S(1)} %get-tuple-element.18, f32[64,128]{1,0:T(8,128)S(1)} %get-tuple-element.17), kind=kOutput, calls=%fused_computation | convolution fusion | flops 6446661632 | bytes 33619968 | tf_op jit(solution)/shard_map/dot_general | solution.py:94
  423.5 195.7 %reduce-scatter.2.cloned.1.call-done = f32[16,1024,128]{2,1,0:T(8,128)} async-done(((f32[16,2048,128]{2,1,0:T(8,128)}), f32[16,1024,128]{2,1,0:T(8,128)}) %reduce-scatter.2.cloned.1.call-update) | async-done | bytes 8388624 | tf_op jit(solution)/shard_map/reduce_scatter | solution.py:125
  (22 shorter events, 0.3 us)
Async XLA Ops:
  6.5 19.3 %copy-start.1 = (s32[8,16]{1,0:T(8,128)S(1)}, s32[8,16]{1,0:T(8,128)}, u32[]{:S(2)}) copy-start(s32[8,16]{1,0:T(8,128)} %param.7) | copy-start | bytes 1540
  6.5 19.4 %copy-start.3 = (bf16[127]{0:T(256)(128)(2,1)S(1)}, bf16[127]{0:T(256)(128)(2,1)}, u32[]{:S(2)}) copy-start(bf16[127]{0:T(256)(128)(2,1)} %param.6) | copy-start | bytes 766
  6.5 19.4 %copy-start.2 = (s32[8,16]{1,0:T(8,128)S(1)}, s32[8,16]{1,0:T(8,128)}, u32[]{:S(2)}) copy-start(s32[8,16]{1,0:T(8,128)} %param.8) | copy-start | bytes 1540
  11.0 65.6 %all-to-all-start = ((bf16[128,2,4096]{2,1,0:T(2,128)(2,1)}), bf16[128,2,4096]{2,1,0:T(2,128)(2,1)S(1)}, u32[]{:S(2)}, u32[]{:S(2)}) async-start(bf16[128,2,4096]{2,1,0:T(2,128)(2,1)} %all_to_all.8), calls=%async_computation | async-start | bytes 4194304 | tf_op jit(solution)/shard_map/all_to_all | solution.py:118
  25.7 273.7 %all-gather.2.cloned.1.call-start = ((), (), s32[]{:S(2)}) async-start(), calls=%async_computation.2 | async-start | bytes 4227072 | tf_op jit(solution)/shard_map/all_gather | solution.py:123
  86.2 533.0 %reduce-scatter.2.cloned.1.call-start = ((), (), s32[]{:S(2)}) async-start(), calls=%async_computation.3 | async-start | bytes 25165824 | tf_op jit(solution)/shard_map/reduce_scatter | solution.py:125
  319.4 19.5 %copy-start = (s32[16,2048]{1,0:T(8,128)S(1)}, s32[16,2048]{1,0:T(8,128)}, u32[]{:S(2)}) copy-start(s32[16,2048]{1,0:T(8,128)} %param.9) | copy-start | bytes 393220
Sparse Core Ops, SparseCore 0:
  86.3 213.1 all-gather.1
  423.6 195.5 reduce-scatter.1
where the time goes:
time: 626 us
  waiting for transfers between devices  452 us (72%)
  matrix products  52.8 us (8%)
  other arithmetic  48.6 us (8%)
  local copies, waits for them, and re-layouts  44.3 us (7%)
  starting transfers between devices  15 us (2%)
  between operations  13.6 us (2%)
    all_gather x1, waiting for transfers between devices, per_device(): lax.all_gather(spectra, 'sta', axis=1, tiled=True)  213 us
    reduce_scatter x1, waiting for transfers between devices, per_device(): lax.psum_scatter(lag_values, 'win', scatter_dimension=1, tiled=True)  196 us
    all_to_all x1, waiting for transfers between devices, per_device(): lax.all_to_all(local_raw, 'sta', split_axis=0, concat_axis=0, tiled=True)  43 us
    sub x1, other arithmetic, lag_transform(): cross_re * cos_alpha - cross_im * sin_alpha  38.1 us
    dot_general x1, matrix products, lag_transform(): jnp.dot(flat_rows, lag_table, precision=lax.Precision.HIGHEST, preferred_...  29.8 us
    unnamed x12, local copies, waits for them, and re-layouts  27.1 us
    dot_general x1, matrix products, make_accumulate(): jnp.einsum('wif,wjf->ijf', own_rows, other_rows, preferred_element_type=j...  19.5 us
    all_to_all x1, starting transfers between devices, per_device(): lax.all_to_all(local_raw, 'sta', split_axis=0, concat_axis=0, tiled=True)  14.8 us
  transfers between devices with their start and end apart: 3, of which 3 were waited for; matrix products, arithmetic and copies ran while one was open for 1% of the time, Pallas kernels for 0%

commit v1 on v0

v1 whole, which is shorter than its diff:
```python
import functools
import math

import jax
import jax.numpy as jnp
import ml_dtypes
import numpy as np
from jax import lax
from jax.experimental import pallas as pl
from jax.experimental.pallas import tpu as pltpu
from jax.sharding import Mesh, PartitionSpec as P

L = 4096
TAPS = 127
FB = 64
BIN0 = 16
LAGW = 128
STD = 16
WDEV = 8
HALF = 1024

smooth_half = 4
floor_share = 0.25
spread_eps = 1e-06

column = np.arange(128)
column_bin = column // 16 * 8 + column % 8
column_im = column // 8 % 2

STA = ("ylo", "x", "z", "core")


def unit_angle(product):
    return ((product % L).astype(np.float32) * np.float32(2.0 * math.pi / L)).astype(np.float64)


def dft_table():
    angle = unit_angle(np.arange(L)[:, None] * (BIN0 + column_bin)[None, :])
    table = np.where(column_im == 0, np.cos(angle), -np.sin(angle))
    return table.astype(np.float32).astype(ml_dtypes.bfloat16)


def lag_table():
    angle = unit_angle((BIN0 + column_bin)[:, None] * np.arange(LAGW)[None, :])
    table = np.where(column_im[:, None] == 0, np.cos(angle), -np.sin(angle))
    return (table / math.sqrt(FB * 16)).astype(np.float32).astype(ml_dtypes.bfloat16)


def band_table():
    near = np.abs(column_bin[:, None] - column_bin[None, :]) <= smooth_half
    counts = (
        np.minimum(column_bin + smooth_half, FB - 1) - np.maximum(column_bin - smooth_half, 0) + 1
    )
    band = np.where(near & (column_im[:, None] == 0), 1.0, 0.0).astype(np.float32)
    return band, (1.0 / counts).astype(np.float32)[None, :]


def swap_parts(values):
    lane = lax.broadcasted_iota(jnp.int32, values.shape, 1)
    first = (lane // 8) % 2 == 0
    width = values.shape[1]
    return jnp.where(first, pltpu.roll(values, width - 8, 1), pltpu.roll(values, 8, 1))


def whiten_kernel(taps_ref, raw_ref, basis_ref, band_ref, inverse_ref, out_ref):
    taps = jnp.broadcast_to(taps_ref[...], (128, 512))
    chunks = []
    for chunk in range(4):
        first_shift = 128 * (chunk - 1) - 63
        moved = pltpu.roll(taps, first_shift % 512, 1, stride=1, stride_axis=0)
        chunks.append(moved[:, :256].astype(jnp.bfloat16))
    fir = jnp.concatenate(chunks, axis=0)
    spectrum = jnp.zeros((256, 128), jnp.float32)
    for tile in range(L // 256):
        first, last = 256 * tile - 128, 256 * tile + 384
        low, high = max(first, 0), min(last, L)
        filtered = jnp.dot(
            raw_ref[:, low:high],
            fir[low - first : 512 - (last - high)],
            preferred_element_type=jnp.float32,
        ).astype(jnp.bfloat16)
        spectrum += jnp.dot(
            filtered,
            basis_ref[256 * tile : 256 * (tile + 1), :],
            preferred_element_type=jnp.float32,
        )
    square = spectrum * spectrum
    magnitude = jnp.sqrt(square + swap_parts(square))
    amplitude = (
        jnp.dot(
            magnitude,
            band_ref[...],
            precision=lax.Precision.HIGHEST,
            preferred_element_type=jnp.float32,
        )
        * inverse_ref[...]
    )
    spread = jnp.sqrt(jnp.sum(square, axis=1, keepdims=True) * (1.0 / FB) + spread_eps)
    divisor = jnp.maximum(amplitude, floor_share * spread)
    out_ref[...] = (spectrum / divisor).astype(jnp.bfloat16)


def whiten(taps, raw):
    band, inverse = band_table()
    return pl.pallas_call(
        whiten_kernel,
        out_shape=jax.ShapeDtypeStruct((raw.shape[0], 128), jnp.bfloat16),
        compiler_params=pltpu.CompilerParams(vmem_limit_bytes=32 * 1024 * 1024),
        name="whiten",
    )(taps, raw, jnp.asarray(dft_table()), jnp.asarray(band), jnp.asarray(inverse))


def select_kernel(slot_ref, present_ref, rows_ref, out_ref):
    entry = lax.broadcasted_iota(jnp.int32, (128, 256), 1)
    selector = (slot_ref[...] == entry).astype(jnp.bfloat16)
    chosen = jnp.dot(selector, rows_ref[...], preferred_element_type=jnp.float32)
    chosen = chosen * present_ref[...].astype(jnp.float32)
    lane = lax.broadcasted_iota(jnp.int32, (STD, 128), 1) // 16
    for group in range(8):
        packed = jnp.zeros((STD, 128), jnp.float32)
        for window in range(WDEV):
            rows = chosen[window * STD : (window + 1) * STD]
            moved = pltpu.roll(rows, (window - group) * 16 % 128, 1) if window != group else rows
            packed = jnp.where(lane == window, moved, packed)
        out_ref[:, group * 128 : (group + 1) * 128] = packed.astype(jnp.bfloat16)


def select(slots, present, rows):
    return pl.pallas_call(
        select_kernel,
        out_shape=jax.ShapeDtypeStruct((STD, 1024), jnp.bfloat16),
        name="select",
    )(slots.reshape(-1, 1), present.reshape(-1, 1), rows)


cos_terms = (0.999999211, -19.7389804, 64.9286574, -85.2716215, 58.7904921, -21.0711056)
sin_terms = (6.28318492, -41.3415892, 81.5999433, -76.6144725, 41.3428824, -12.4712435)


def cos_sin(steps):
    turn = steps * (1.0 / L)
    turn = turn - jnp.round(turn)
    square = turn * turn
    cosine = jnp.full_like(square, cos_terms[-1])
    sine = jnp.full_like(square, sin_terms[-1])
    for cos_term, sin_term in zip(cos_terms[-2::-1], sin_terms[-2::-1]):
        cosine = cosine * square + cos_term
        sine = sine * square + sin_term
    return cosine, sine * turn


def correlate_kernel(piece_rows, place_ref, lag_ref, own_ref, table_ref, *rest):
    pieces = rest[: len(piece_rows)]
    out_ref, partners, weights, cross, sems = rest[len(piece_rows) :]
    step = pl.program_id(0)
    x, z, core = place_ref[0], place_ref[1], place_ref[2]

    def copy(number, source_x, target_x):
        first_x, _, z_back, core_back = piece_rows[number]
        z_at = lax.rem(z - z_back + 8, 8)
        core_at = lax.rem(core + core_back, 2)
        row = pl.multiple_of(z_at * 32 + core_at * 16, 16)
        return pltpu.make_async_copy(
            pieces[number].at[source_x - first_x],
            partners.at[target_x, :, pl.ds(row, 16), :],
            sems.at[target_x, z_back * 2 + core_back],
        )

    @pl.when(step == 0)
    def _():
        for number, (first_x, last_x, _, _) in enumerate(piece_rows):
            for source_x in range(first_x, last_x):
                copy(number, source_x, lax.rem(x - source_x + 4, 4)).start()
        own_lane = lax.broadcasted_iota(jnp.int32, (8, 256), 1)
        same_bin = own_lane % 8 == lax.broadcasted_iota(jnp.int32, (8, 256), 0)
        first = (lax.broadcasted_iota(jnp.int32, (STD, 256), 1) // 8) % 2 == 0
        for group in range(8):
            lanes = slice(group * 128, (group + 1) * 128)
            own = jnp.concatenate([own_ref[0, :, lanes], own_ref[1, :, lanes]], axis=1)
            own = own.astype(jnp.float32)
            swapped = swap_parts(own)
            swapped = jnp.where(first, swapped, -swapped)
            rows = []
            for station in range(STD):
                for part in (own, swapped):
                    row = jnp.broadcast_to(part[station : station + 1], (8, 256))
                    rows.append(jnp.where(same_bin, row, 0.0))
            weights[group] = jnp.concatenate(rows, axis=0).astype(jnp.bfloat16)

    seen = set()
    for number, (first_x, _, z_back, core_back) in enumerate(piece_rows):
        if (z_back, core_back) not in seen:
            seen.add((z_back, core_back))
            copy(number, first_x, step).wait()

    for group in range(8):
        lanes = slice(group * 128, (group + 1) * 128)
        partner = jnp.concatenate([partners[step, 0, :, lanes], partners[step, 1, :, lanes]], axis=1)
        cross[group] = lax.dot_general(
            weights[group], partner, (((1,), (1,)), ((), ())), preferred_element_type=jnp.float32
        )

    bins = (lax.broadcasted_iota(jnp.int32, (8, 128), 0) + BIN0).astype(jnp.float32)

    def one_station(station, carry):
        top = pl.multiple_of(station * 16, 16)
        for side in range(2):
            columns = slice(side * 128, (side + 1) * 128)
            lag = lag_ref[station, :, columns].astype(jnp.float32)
            lag = jnp.broadcast_to(lag, (8, 128))
            cosine, sine = cos_sin(lag * bins)
            cos_next, sin_next = cos_sin(lag * 8.0)
            rotated = []
            for group in range(8):
                real = cross[group, pl.ds(top, 8), columns]
                imag = cross[group, pl.ds(top + 8, 8), columns]
                rotated.append(real * cosine - imag * sine)
                rotated.append(real * sine + imag * cosine)
                if group < 7:
                    cosine, sine = (
                        cosine * cos_next - sine * sin_next,
                        cosine * sin_next + sine * cos_next,
                    )
            rotated = jnp.concatenate(rotated, axis=0).astype(jnp.bfloat16)
            out_ref[station, columns, :] = lax.dot_general(
                rotated,
                table_ref[...],
                (((0,), (0,)), ((), ())),
                preferred_element_type=jnp.float32,
            )
        return carry

    lax.fori_loop(0, STD, one_station, 0, unroll=4)


def correlate(place, lag, own, pieces, piece_rows):
    grid_spec = pltpu.PrefetchScalarGridSpec(
        num_scalar_prefetch=1,
        grid=(4,),
        in_specs=[
            pl.BlockSpec((STD, 1, 256), lambda q, place: (0, 0, q)),
            pl.BlockSpec((2, STD, 1024), lambda q, place: (0, 0, 0)),
            pl.BlockSpec((128, 128), lambda q, place: (0, 0)),
        ]
        + [pl.BlockSpec(memory_space=pl.ANY)] * len(pieces),
        out_specs=pl.BlockSpec((STD, 256, LAGW), lambda q, place: (0, q, 0)),
        scratch_shapes=[
            pltpu.VMEM((4, 2, 256, 1024), jnp.bfloat16),
            pltpu.VMEM((8, 256, 256), jnp.bfloat16),
            pltpu.VMEM((8, 256, 256), jnp.float32),
            pltpu.SemaphoreType.DMA((4, 16)),
        ],
    )
    return pl.pallas_call(
        functools.partial(correlate_kernel, piece_rows),
        grid_spec=grid_spec,
        out_shape=jax.ShapeDtypeStruct((STD, HALF, LAGW), jnp.float32),
        compiler_params=pltpu.CompilerParams(
            vmem_limit_bytes=40 * 1024 * 1024, dimension_semantics=("arbitrary",)
        ),
        name="correlate",
    )(place, lag.reshape(STD, 1, HALF), own, jnp.asarray(lag_table()), *pieces)


def shift(value, axis, size, by):
    return lax.ppermute(value, axis, [(at, (at + by) % size) for at in range(size)])


def per_device(raw_traces, fir_taps, source_slot, present, lag_start):
    ylo, yhi = lax.axis_index("ylo"), lax.axis_index("yhi")
    place = jnp.stack([lax.axis_index("x"), lax.axis_index("z"), lax.axis_index("core")])
    lag = lax.dynamic_slice_in_dim(lag_start, yhi * HALF, HALF, 1)

    taps = jnp.pad(fir_taps.astype(jnp.float32), (0, 512 - TAPS)).reshape(1, 512)
    white = whiten(taps, raw_traces[0])
    received = lax.all_to_all(white, STA, split_axis=0, concat_axis=0, tiled=True)
    mine = select(source_slot, present, received)

    ring = lax.ppermute(mine, ("ylo", "yhi"), [(0, 2), (2, 3), (3, 1), (1, 0)])
    middle = lax.ppermute(mine, ("ylo", "yhi"), [(1, 2), (2, 1)])
    other = shift(mine, "yhi", 2, 1)
    y = 2 * yhi + ylo
    early = jnp.where(y == 0, mine, jnp.where(y == 2, middle, ring))
    late = jnp.where(y == 3, mine, jnp.where(y == 1, middle, ring))
    own = jnp.stack([jnp.where(yhi == 0, mine, other), jnp.where(yhi == 0, other, mine)])

    block = jnp.stack([early, late])
    line = jnp.stack([block] + [shift(block, "x", 4, by) for by in (1, 2, 3)])
    pieces, piece_rows = [line], [(0, 4, 0)]
    up = down = line
    for hop in (1, 2, 3):
        up, down = shift(up, "z", 8, 1), shift(down, "z", 8, -1)
        pieces += [up, down]
        piece_rows += [(0, 4, hop), (0, 4, 8 - hop)]
    pieces += [shift(up[:2], "z", 8, 1), shift(down[2:], "z", 8, -1)]
    piece_rows += [(0, 2, 4), (2, 4, 4)]
    theirs = [shift(piece, "core", 2, 1) for piece in pieces]
    rows = tuple(row + (0,) for row in piece_rows) + tuple(row + (1,) for row in piece_rows)
    return correlate(place, lag, own, pieces + theirs, rows)


def solution(mesh):
    fine = Mesh(mesh.devices.reshape(2, 4, 8, 2, 2), STA + ("yhi",))
    placed = (P("yhi", STA, None), P(), P("yhi", STA), P("yhi", STA), P(STA, None))
    return jax.shard_map(
        per_device, mesh=fine, in_specs=placed, out_specs=P(STA, "yhi", None), check_vma=False
    )
```

time: 626 us -> 109 us (0.17)
  waiting for transfers between devices: 452 us -> 25.1 us
  matrix products: 52.8 us -> 0 us
  other arithmetic: 48.6 us -> 2.99 us
  starting transfers between devices: 15 us -> 48.1 us
  local copies, waits for them, and re-layouts: 44.3 us -> 11.3 us
  Pallas kernels: 0 us -> 21 us
  between operations: 13.6 us -> 0.27 us
    all_gather x1 -> x0, waiting for transfers between devices: 213 us -> none  [per_device(): lax.all_gather(spectra, 'sta', axis=1, tiled=True)]
    reduce_scatter x1 -> x0, waiting for transfers between devices: 196 us -> none  [per_device(): lax.psum_scatter(lag_values, 'win', scatter_dimension=1, tiled=True)]
    dot_general x5 -> x0, matrix products: 52.8 us -> none  [the longest x1 29.8 us: lag_transform(): jnp.dot(flat_rows, lag_table, precision=lax.Precision.HIGHEST, preferred_...]
    sub x1 -> x0, other arithmetic: 38.1 us -> none  [lag_transform(): cross_re * cos_alpha - cross_im * sin_alpha]
    all_to_all x1, waiting for transfers between devices: 43 us -> 7.85 us  [per_device(): lax.all_to_all(white, STA, split_axis=0, concat_axis=0, tiled=True)]
    ppermute x0 -> x23, starting transfers between devices: none -> 33.3 us  [the longest x21 29 us: shift(): lax.ppermute(value, axis, [(at, (at + by) % size) for at in range(size)])]
    unnamed x12 -> x14, local copies, waits for them, and re-layouts: 27.1 us -> 5.68 us
    pallas_call x0 -> x3, Pallas kernels: none -> 21 us  [the longest x1 14 us: correlate(): pl.pallas_call(functools.partial(correlate_kernel, piece_rows), grid_spec...]
  transfers between devices with their start and end apart: 3 -> 24, of which waited for: 3 -> 11; matrix products, arithmetic and copies ran while one was open for 1% -> 6% of each run, Pallas kernels for 0% -> 0%
where the time goes in v1:
time: 109 us
  starting transfers between devices  48.1 us (44%)
  waiting for transfers between devices  25.1 us (23%)
  Pallas kernels  21 us (19%)
  local copies, waits for them, and re-layouts  11.3 us (10%)
  other arithmetic  2.99 us (3%)
    ppermute x21, starting transfers between devices, shift(): lax.ppermute(value, axis, [(at, (at + by) % size) for at in range(size)])  29 us
    ppermute x21, waiting for transfers between devices, shift(): lax.ppermute(value, axis, [(at, (at + by) % size) for at in range(size)])  15.9 us
    all_to_all x1, starting transfers between devices, per_device(): lax.all_to_all(white, STA, split_axis=0, concat_axis=0, tiled=True)  14.8 us
    pallas_call x1, Pallas kernels, correlate(): pl.pallas_call(functools.partial(correlate_kernel, piece_rows), grid_spec...  14 us
    all_to_all x1, waiting for transfers between devices, per_device(): lax.all_to_all(white, STA, split_axis=0, concat_axis=0, tiled=True)  7.85 us
    unnamed x14, local copies, waits for them, and re-layouts  5.68 us
    pallas_call x1, Pallas kernels, whiten(): pl.pallas_call(whiten_kernel, out_shape=jax.ShapeDtypeStruct((raw.shape[0...  5.15 us
    ppermute x1, starting transfers between devices, per_device(): ring = lax.ppermute(mine, ('ylo', 'yhi'), [(0, 2), (2, 3), (3, 1), (1, 0)])  3.62 us
  transfers between devices with their start and end apart: 24, of which 11 were waited for; matrix products, arithmetic and copies ran while one was open for 6% of the time, Pallas kernels for 0%

profile of v1, /device:TPU:1, one launch (start us, length us, event | category | flops | bytes accessed | tf_op | source)
XLA Modules:
  0.0 108.7 jit_solution(15958846536143594045)
XLA Ops:
  0.7 1.6 %copy-done.1 = bf16[1,256,4096]{2,1,0:T(8,128)(2,1)S(1)} copy-done((bf16[1,256,4096]{2,1,0:T(8,128)(2,1)S(1)}, bf16[1,256,4096]{2,1,0:T(8,128)(2,1)}, u32[]{:S(2)}) %copy-start.1) | copy-done | bytes 2097176
  2.3 1.2 %copy-done.2 = bf16[4096,128]{1,0:T(8,128)(2,1)S(1)} copy-done((bf16[4096,128]{1,0:T(8,128)(2,1)S(1)}, bf16[4096,128]{1,0:T(8,128)(2,1)}, u32[]{:S(2)}) %copy-start.2) | copy-done | bytes 1048600
  3.5 0.8 copy-done.3
  5.0 5.1 %whiten.1 = bf16[256,128]{1,0:T(8,128)(2,1)} custom-call(f32[1,512]{1,0:T(1,128)S(1)} %bitcast.21, bf16[256,4096]{1,0:T(8,128)(2,1)S(1)} %bitcast.20, bf16[4096,128]{1,0:T(8,128)(2,1)S(1)} %copy-done.2, f32[128,128]{1,0:T(8,128)S(1)} %copy-done.3, f32[1,128]{1,0:T(1,128)S(1)} %copy-done.5), custom_call_target="tpu_custom_call" | custom-call | tf_op jit(solution)/shard_map/whiten/pallas_call | solution.py:105
  10.2 14.8 %all-to-all-start = ((bf16[128,2,128]{2,1,0:T(2,128)(2,1)}), bf16[128,2,128]{2,1,0:T(2,128)(2,1)S(1)}, u32[]{:S(2)}, u32[]{:S(2)}) async-start(bf16[128,2,128]{2,1,0:T(2,128)(2,1)} %bitcast.5), calls=%async_computation | async-start | bytes 131072 | tf_op jit(solution)/shard_map/all_to_all | solution.py:276
  24.9 1.4 %reshape.23.slot_ref = s32[128,1]{1,0:T(8,128)} reshape(s32[8,16]{1,0:T(8,128)} %param.11) | data formatting | bytes 1024 | tf_op jit(solution)/shard_map/reshape | solution.py:133
  26.3 1.4 %reshape.24.present_ref = s32[128,1]{1,0:T(8,128)} reshape(s32[8,16]{1,0:T(8,128)} %param.12) | data formatting | bytes 1024 | tf_op jit(solution)/shard_map/reshape | solution.py:133
  27.7 7.8 %all-to-all-done = bf16[128,2,128]{2,1,0:T(2,128)(2,1)S(1)} async-done(((bf16[128,2,128]{2,1,0:T(2,128)(2,1)}), bf16[128,2,128]{2,1,0:T(2,128)(2,1)S(1)}, u32[]{:S(2)}, u32[]{:S(2)}) %all-to-all-start) | async-done | bytes 65568 | tf_op jit(solution)/shard_map/all_to_all | solution.py:276
  36.2 1.8 %select.2 = bf16[16,1024]{1,0:T(8,128)(2,1)} custom-call(s32[128,1]{1,0:T(8,128)} %reshape.23.slot_ref, s32[128,1]{1,0:T(8,128)} %reshape.24.present_ref, bf16[256,128]{1,0:T(8,128)(2,1)} %bitcast.22), custom_call_target="tpu_custom_call" | custom-call | tf_op jit(solution)/shard_map/select/pallas_call | solution.py:129
  38.7 3.6 %collective-permute-start.2 = (bf16[16,1024]{1,0:T(8,128)(2,1)}, bf16[16,1024]{1,0:T(8,128)(2,1)S(1)}, u32[]{:S(2)}, u32[]{:S(2)}) collective-permute-start(bf16[16,1024]{1,0:T(8,128)(2,1)} %select.2), channel_id=1, source_target_pairs={{0,128},{128,129},{129,1},{1,0},{2,130},{130,131},{131,3},{3,2},{4... | collective-permute-start | bytes 98312 | tf_op jit(solution)/shard_map/ppermute | solution.py:279
  42.8 1.4 %collective-permute-done.2 = bf16[16,1024]{1,0:T(8,128)(2,1)S(1)} collective-permute-done((bf16[16,1024]{1,0:T(8,128)(2,1)}, bf16[16,1024]{1,0:T(8,128)(2,1)S(1)}, u32[]{:S(2)}, u32[]{:S(2)}) %collective-permute-start.2) | collective-permute-done | bytes 32800 | tf_op jit(solution)/shard_map/ppermute | solution.py:279
  44.2 2.6 %collective-permute-done = bf16[16,1024]{1,0:T(8,128)(2,1)S(1)} collective-permute-done((bf16[16,1024]{1,0:T(8,128)(2,1)}, bf16[16,1024]{1,0:T(8,128)(2,1)S(1)}, u32[]{:S(2)}, u32[]{:S(2)}) %collective-permute-start) | collective-permute-done | bytes 32800 | tf_op jit(solution)/shard_map/ppermute | solution.py:266
  46.8 1.4 %select_bitcast_fusion.1 = (bf16[1,16,1024]{2,1,0:T(8,128)(2,1)S(1)}, bf16[1,16,1024]{2,1,0:T(8,128)(2,1)S(1)}, bf16[1,16,1024]{2,1,0:T(8,128)(2,1)}, bf16[1,16,1024]{2,1,0:T(8,128)(2,1)}) fusion(bf16[16,1024]{1,0:T(8,128)(2,1)} %select.2, bf16[16,1024]{1,0:T(8,128)(2,1)S(1)} %collective-permute-done.1, bf16[16,1024]{1,0:T(8,128)(2,1)S(1)} %collective-permute-done.2, ...), kind=kLoop, calls=%fused_computation.4 | loop fusion | flops 98304 | bytes 262149 | tf_op jit(solution)/shard_map/stack | solution.py:287
  48.2 1.3 %collective-permute-start.4 = (bf16[2,16,1024]{2,1,0:T(8,128)(2,1)S(1)}, bf16[2,16,1024]{2,1,0:T(8,128)(2,1)S(1)}, u32[]{:S(2)}, u32[]{:S(2)}) collective-permute-start(bf16[2,16,1024]{2,1,0:T(8,128)(2,1)S(1)} %get-tuple-element.8), channel_id=1, source_target_pairs={{0,64},{32,96},{64,0},{96,32},{1,65},{33,97},{65,1},{97,33},{2,66}... | collective-permute-start | bytes 196616 | tf_op jit(solution)/shard_map/ppermute | solution.py:266
  49.7 2.5 %collective-permute-start.5 = (bf16[2,16,1024]{2,1,0:T(8,128)(2,1)S(1)}, bf16[2,16,1024]{2,1,0:T(8,128)(2,1)S(1)}, u32[]{:S(2)}, u32[]{:S(2)}) collective-permute-start(bf16[2,16,1024]{2,1,0:T(8,128)(2,1)S(1)} %get-tuple-element.8), channel_id=1, source_target_pairs={{0,96},{32,0},{64,32},{96,64},{1,97},{33,1},{65,33},{97,65},{2,98}... | collective-permute-start | bytes 196616 | tf_op jit(solution)/shard_map/ppermute | solution.py:266
  52.1 0.8 collective-permute-done.4
  52.9 0.9 collective-permute-done.3
  54.2 1.5 %collective-permute-start.6 = (bf16[4,2,16,1024]{3,2,1,0:T(8,128)(2,1)S(1)}, bf16[4,2,16,1024]{3,2,1,0:T(8,128)(2,1)S(1)}, u32[]{:S(2)}, u32[]{:S(2)}) collective-permute-start(bf16[4,2,16,1024]{3,2,1,0:T(8,128)(2,1)S(1)} %pad_maximum_fusion.rest_0_), channel_id=1, source_target_pairs={{0,4},{4,8},{8,12},{12,16},{16,20},{20,24},{24,28},{28,0},{1,5},{5... | collective-permute-start | bytes 786440 | tf_op jit(solution)/shard_map/ppermute | solution.py:266
  55.6 3.8 %collective-permute-done.7.rest_2_ = bf16[4,2,16,1024]{3,2,1,0:T(8,128)(2,1)S(1)} collective-permute-done((bf16[4,2,16,1024]{3,2,1,0:T(8,128)(2,1)S(1)}, bf16[4,2,16,1024]{3,2,1,0:T(8,128)(2,1)S(1)}, u32[]{:S(2)}, u32[]{:S(2)}) %collective-permute-start.7) | collective-permute-done | bytes 262176 | tf_op jit(solution)/shard_map/ppermute | solution.py:266
  59.4 1.2 %collective-permute-start.9 = (bf16[4,2,16,1024]{3,2,1,0:T(8,128)(2,1)S(1)}, bf16[4,2,16,1024]{3,2,1,0:T(8,128)(2,1)S(1)}, u32[]{:S(2)}, u32[]{:S(2)}) collective-permute-start(bf16[4,2,16,1024]{3,2,1,0:T(8,128)(2,1)S(1)} %collective-permute-done.7.rest_2_), channel_id=1, source_target_pairs={{0,28},{4,0},{8,4},{12,8},{16,12},{20,16},{24,20},{28,24},{1,29},{... | collective-permute-start | bytes 786440 | tf_op jit(solution)/shard_map/ppermute | solution.py:266
  60.9 5.5 %collective-permute-done.9.rest_4_ = bf16[4,2,16,1024]{3,2,1,0:T(8,128)(2,1)S(1)} collective-permute-done((bf16[4,2,16,1024]{3,2,1,0:T(8,128)(2,1)S(1)}, bf16[4,2,16,1024]{3,2,1,0:T(8,128)(2,1)S(1)}, u32[]{:S(2)}, u32[]{:S(2)}) %collective-permute-start.9) | collective-permute-done | bytes 262176 | tf_op jit(solution)/shard_map/ppermute | solution.py:266
  66.4 1.4 %collective-permute-start.11 = (bf16[4,2,16,1024]{3,2,1,0:T(8,128)(2,1)S(1)}, bf16[4,2,16,1024]{3,2,1,0:T(8,128)(2,1)S(1)}, u32[]{:S(2)}, u32[]{:S(2)}) collective-permute-start(bf16[4,2,16,1024]{3,2,1,0:T(8,128)(2,1)S(1)} %collective-permute-done.9.rest_4_), channel_id=1, source_target_pairs={{0,28},{4,0},{8,4},{12,8},{16,12},{20,16},{24,20},{28,24},{1,29},{... | collective-permute-start | bytes 786440 | tf_op jit(solution)/shard_map/ppermute | solution.py:266
  68.0 9.0 %collective-permute-start.14 = (bf16[4,2,16,1024]{3,2,1,0:T(8,128)(2,1)S(1)}, bf16[4,2,16,1024]{3,2,1,0:T(8,128)(2,1)S(1)}, u32[]{:S(2)}, u32[]{:S(2)}) collective-permute-start(bf16[4,2,16,1024]{3,2,1,0:T(8,128)(2,1)S(1)} %pad_maximum_fusion.rest_0_), channel_id=1, source_target_pairs={{0,2},{2,0},{1,3},{3,1},{4,6},{6,4},{5,7},{7,5},{8,10},{10,8},{9,1... | collective-permute-start | bytes 786440 | tf_op jit(solution)/shard_map/ppermute | solution.py:266
  77.6 3.2 %collective-permute-start.18 = (bf16[4,2,16,1024]{3,2,1,0:T(8,128)(2,1)S(1)}, bf16[4,2,16,1024]{3,2,1,0:T(8,128)(2,1)S(1)}, u32[]{:S(2)}, u32[]{:S(2)}) collective-permute-start(bf16[4,2,16,1024]{3,2,1,0:T(8,128)(2,1)S(1)} %collective-permute-done.9.rest_4_), channel_id=1, source_target_pairs={{0,2},{2,0},{1,3},{3,1},{4,6},{6,4},{5,7},{7,5},{8,10},{10,8},{9,1... | collective-permute-start | bytes 786440 | tf_op jit(solution)/shard_map/ppermute | solution.py:266
  81.5 2.5 %collective-permute-start.13 = (bf16[2,2,16,1024]{3,2,1,0:T(8,128)(2,1)}, bf16[2,2,16,1024]{3,2,1,0:T(8,128)(2,1)}, u32[]{:S(2)}, u32[]{:S(2)}) collective-permute-start(bf16[2,2,16,1024]{3,2,1,0:T(8,128)(2,1)} %slice.9), channel_id=1, source_target_pairs={{0,28},{4,0},{8,4},{12,8},{16,12},{20,16},{24,20},{28,24},{1,29},{... | collective-permute-start | bytes 393224 | tf_op jit(solution)/shard_map/ppermute | solution.py:266
  84.6 2.1 %collective-permute-start.17 = (bf16[4,2,16,1024]{3,2,1,0:T(8,128)(2,1)S(1)}, bf16[4,2,16,1024]{3,2,1,0:T(8,128)(2,1)S(1)}, u32[]{:S(2)}, u32[]{:S(2)}) collective-permute-start(bf16[4,2,16,1024]{3,2,1,0:T(8,128)(2,1)S(1)} %collective-permute-done.8.rest_3_), channel_id=1, source_target_pairs={{0,2},{2,0},{1,3},{3,1},{4,6},{6,4},{5,7},{7,5},{8,10},{10,8},{9,1... | collective-permute-start | bytes 786440 | tf_op jit(solution)/shard_map/ppermute | solution.py:266
  87.8 1.4 %collective-permute-start.22 = (bf16[2,2,16,1024]{3,2,1,0:T(8,128)(2,1)}, bf16[2,2,16,1024]{3,2,1,0:T(8,128)(2,1)S(1)}, u32[]{:S(2)}, u32[]{:S(2)}) collective-permute-start(bf16[2,2,16,1024]{3,2,1,0:T(8,128)(2,1)} %collective-permute-done.13.rest_8_), channel_id=1, source_target_pairs={{0,2},{2,0},{1,3},{3,1},{4,6},{6,4},{5,7},{7,5},{8,10},{10,8},{9,1... | collective-permute-start | bytes 393224 | tf_op jit(solution)/shard_map/ppermute | solution.py:266
  89.2 1.7 %collective-permute-done.12.rest_7_ = bf16[2,2,16,1024]{3,2,1,0:T(8,128)(2,1)} collective-permute-done((bf16[2,2,16,1024]{3,2,1,0:T(8,128)(2,1)}, bf16[2,2,16,1024]{3,2,1,0:T(8,128)(2,1)}, u32[]{:S(2)}, u32[]{:S(2)}) %collective-permute-start.12) | collective-permute-done | bytes 131104 | tf_op jit(solution)/shard_map/ppermute | solution.py:266
  90.9 1.1 %collective-permute-start.21 = (bf16[2,2,16,1024]{3,2,1,0:T(8,128)(2,1)}, bf16[2,2,16,1024]{3,2,1,0:T(8,128)(2,1)S(1)}, u32[]{:S(2)}, u32[]{:S(2)}) collective-permute-start(bf16[2,2,16,1024]{3,2,1,0:T(8,128)(2,1)} %collective-permute-done.12.rest_7_), channel_id=1, source_target_pairs={{0,2},{2,0},{1,3},{3,1},{4,6},{6,4},{5,7},{7,5},{8,10},{10,8},{9,1... | collective-permute-start | bytes 393224 | tf_op jit(solution)/shard_map/ppermute | solution.py:266
  92.1 0.9 reshape.16.lag_ref
  93.0 0.8 pad_maximum_fusion.1.own_ref
  94.6 14.0 %correlate.1 = f32[16,1024,128]{2,1,0:T(8,128)} custom-call(s32[3]{0:T(128)S(1)} %pad_add_fusion.place_ref, s32[16,1,1024]{2,1,0:T(1,128)S(1)} %reshape.16.lag_ref, bf16[2,16,1024]{2,1,0:T(8,128)(2,1)S(1)} %pad_maximum_fusion.1.own_ref, bf16[128,128]{1,0:T(8,128)(2,1)S(1)} %copy-done.4, bf16[4,2,16,1024]{3,2,1,0:T(8,128)(2,1)S(1)} %pad_maximum_fusion.rest_0_, ...), custom_call_target="tpu_custom_call" | custom-call | tf_op jit(solution)/shard_map/correlate/pallas_call | solution.py:254
  (45 shorter events, 8.0 us)
Async XLA Ops:
  0.0 87.2 %copy-start = (s32[16,2048]{1,0:T(8,128)S(1)}, s32[16,2048]{1,0:T(8,128)}, u32[]{:S(2)}) copy-start(s32[16,2048]{1,0:T(8,128)} %param.13) | copy-start | bytes 393220
  0.7 1.6 %copy-start.1 = (bf16[1,256,4096]{2,1,0:T(8,128)(2,1)S(1)}, bf16[1,256,4096]{2,1,0:T(8,128)(2,1)}, u32[]{:S(2)}) copy-start(bf16[1,256,4096]{2,1,0:T(8,128)(2,1)} %param.9) | copy-start | bytes 6291460
  2.3 1.2 %copy-start.2 = (bf16[4096,128]{1,0:T(8,128)(2,1)S(1)}, bf16[4096,128]{1,0:T(8,128)(2,1)}, u32[]{:S(2)}) copy-start(bf16[4096,128]{1,0:T(8,128)(2,1)} %constant.43.clone.basis_ref) | copy-start | bytes 3145732
  3.5 0.8 copy-start.3
  4.4 0.7 copy-start.5
  10.2 25.4 %all-to-all-start = ((bf16[128,2,128]{2,1,0:T(2,128)(2,1)}), bf16[128,2,128]{2,1,0:T(2,128)(2,1)S(1)}, u32[]{:S(2)}, u32[]{:S(2)}) async-start(bf16[128,2,128]{2,1,0:T(2,128)(2,1)} %bitcast.5), calls=%async_computation | async-start | bytes 131072 | tf_op jit(solution)/shard_map/all_to_all | solution.py:276
  35.6 0.6 copy-start.6
  38.0 4.7 %collective-permute-start.1 = (bf16[16,1024]{1,0:T(8,128)(2,1)}, bf16[16,1024]{1,0:T(8,128)(2,1)S(1)}, u32[]{:S(2)}, u32[]{:S(2)}) collective-permute-start(bf16[16,1024]{1,0:T(8,128)(2,1)} %select.2), channel_id=1, source_target_pairs={{1,128},{128,1},{3,130},{130,3},{5,132},{132,5},{7,134},{134,7},{9... | collective-permute-start | bytes 98312 | tf_op jit(solution)/shard_map/ppermute | solution.py:280
  38.7 5.5 %collective-permute-start.2 = (bf16[16,1024]{1,0:T(8,128)(2,1)}, bf16[16,1024]{1,0:T(8,128)(2,1)S(1)}, u32[]{:S(2)}, u32[]{:S(2)}) collective-permute-start(bf16[16,1024]{1,0:T(8,128)(2,1)} %select.2), channel_id=1, source_target_pairs={{0,128},{128,129},{129,1},{1,0},{2,130},{130,131},{131,3},{3,2},{4... | collective-permute-start | bytes 98312 | tf_op jit(solution)/shard_map/ppermute | solution.py:279
  42.3 4.5 %collective-permute-start = (bf16[16,1024]{1,0:T(8,128)(2,1)}, bf16[16,1024]{1,0:T(8,128)(2,1)S(1)}, u32[]{:S(2)}, u32[]{:S(2)}) collective-permute-start(bf16[16,1024]{1,0:T(8,128)(2,1)} %select.2), channel_id=1, source_target_pairs={{0,1},{1,0},{2,3},{3,2},{4,5},{5,4},{6,7},{7,6},{8,9},{9,8},{10,11... | collective-permute-start | bytes 98312 | tf_op jit(solution)/shard_map/ppermute | solution.py:266
  48.2 4.7 %collective-permute-start.4 = (bf16[2,16,1024]{2,1,0:T(8,128)(2,1)S(1)}, bf16[2,16,1024]{2,1,0:T(8,128)(2,1)S(1)}, u32[]{:S(2)}, u32[]{:S(2)}) collective-permute-start(bf16[2,16,1024]{2,1,0:T(8,128)(2,1)S(1)} %get-tuple-element.8), channel_id=1, source_target_pairs={{0,64},{32,96},{64,0},{96,32},{1,65},{33,97},{65,1},{97,33},{2,66}... | collective-permute-start | bytes 196616 | tf_op jit(solution)/shard_map/ppermute | solution.py:266
  49.5 4.3 %collective-permute-start.3 = (bf16[2,16,1024]{2,1,0:T(8,128)(2,1)S(1)}, bf16[2,16,1024]{2,1,0:T(8,128)(2,1)S(1)}, u32[]{:S(2)}, u32[]{:S(2)}) collective-permute-start(bf16[2,16,1024]{2,1,0:T(8,128)(2,1)S(1)} %get-tuple-element.8), channel_id=1, source_target_pairs={{0,32},{32,64},{64,96},{96,0},{1,33},{33,65},{65,97},{97,1},{2,34}... | collective-permute-start | bytes 196616 | tf_op jit(solution)/shard_map/ppermute | solution.py:266
  49.7 4.4 %collective-permute-start.5 = (bf16[2,16,1024]{2,1,0:T(8,128)(2,1)S(1)}, bf16[2,16,1024]{2,1,0:T(8,128)(2,1)S(1)}, u32[]{:S(2)}, u32[]{:S(2)}) collective-permute-start(bf16[2,16,1024]{2,1,0:T(8,128)(2,1)S(1)} %get-tuple-element.8), channel_id=1, source_target_pairs={{0,96},{32,0},{64,32},{96,64},{1,97},{33,1},{65,33},{97,65},{2,98}... | collective-permute-start | bytes 196616 | tf_op jit(solution)/shard_map/ppermute | solution.py:266
  54.1 5.3 %collective-permute-start.7 = (bf16[4,2,16,1024]{3,2,1,0:T(8,128)(2,1)S(1)}, bf16[4,2,16,1024]{3,2,1,0:T(8,128)(2,1)S(1)}, u32[]{:S(2)}, u32[]{:S(2)}) collective-permute-start(bf16[4,2,16,1024]{3,2,1,0:T(8,128)(2,1)S(1)} %pad_maximum_fusion.rest_0_), channel_id=1, source_target_pairs={{0,28},{4,0},{8,4},{12,8},{16,12},{20,16},{24,20},{28,24},{1,29},{... | collective-permute-start | bytes 786440 | tf_op jit(solution)/shard_map/ppermute | solution.py:266
  54.2 6.5 %collective-permute-start.6 = (bf16[4,2,16,1024]{3,2,1,0:T(8,128)(2,1)S(1)}, bf16[4,2,16,1024]{3,2,1,0:T(8,128)(2,1)S(1)}, u32[]{:S(2)}, u32[]{:S(2)}) collective-permute-start(bf16[4,2,16,1024]{3,2,1,0:T(8,128)(2,1)S(1)} %pad_maximum_fusion.rest_0_), channel_id=1, source_target_pairs={{0,4},{4,8},{8,12},{12,16},{16,20},{20,24},{24,28},{28,0},{1,5},{5... | collective-permute-start | bytes 786440 | tf_op jit(solution)/shard_map/ppermute | solution.py:266
  59.4 7.0 %collective-permute-start.9 = (bf16[4,2,16,1024]{3,2,1,0:T(8,128)(2,1)S(1)}, bf16[4,2,16,1024]{3,2,1,0:T(8,128)(2,1)S(1)}, u32[]{:S(2)}, u32[]{:S(2)}) collective-permute-start(bf16[4,2,16,1024]{3,2,1,0:T(8,128)(2,1)S(1)} %collective-permute-done.7.rest_2_), channel_id=1, source_target_pairs={{0,28},{4,0},{8,4},{12,8},{16,12},{20,16},{24,20},{28,24},{1,29},{... | collective-permute-start | bytes 786440 | tf_op jit(solution)/shard_map/ppermute | solution.py:266
  60.7 7.3 %collective-permute-start.8 = (bf16[4,2,16,1024]{3,2,1,0:T(8,128)(2,1)S(1)}, bf16[4,2,16,1024]{3,2,1,0:T(8,128)(2,1)S(1)}, u32[]{:S(2)}, u32[]{:S(2)}) collective-permute-start(bf16[4,2,16,1024]{3,2,1,0:T(8,128)(2,1)S(1)} %collective-permute-done.6.rest_1_), channel_id=1, source_target_pairs={{0,4},{4,8},{8,12},{12,16},{16,20},{20,24},{24,28},{28,0},{1,5},{5... | collective-permute-start | bytes 786440 | tf_op jit(solution)/shard_map/ppermute | solution.py:266
  66.4 11.2 %collective-permute-start.11 = (bf16[4,2,16,1024]{3,2,1,0:T(8,128)(2,1)S(1)}, bf16[4,2,16,1024]{3,2,1,0:T(8,128)(2,1)S(1)}, u32[]{:S(2)}, u32[]{:S(2)}) collective-permute-start(bf16[4,2,16,1024]{3,2,1,0:T(8,128)(2,1)S(1)} %collective-permute-done.9.rest_4_), channel_id=1, source_target_pairs={{0,28},{4,0},{8,4},{12,8},{16,12},{20,16},{24,20},{28,24},{1,29},{... | collective-permute-start | bytes 786440 | tf_op jit(solution)/shard_map/ppermute | solution.py:266
  68.0 13.4 %collective-permute-start.10 = (bf16[4,2,16,1024]{3,2,1,0:T(8,128)(2,1)S(1)}, bf16[4,2,16,1024]{3,2,1,0:T(8,128)(2,1)S(1)}, u32[]{:S(2)}, u32[]{:S(2)}) collective-permute-start(bf16[4,2,16,1024]{3,2,1,0:T(8,128)(2,1)S(1)} %collective-permute-done.8.rest_3_), channel_id=1, source_target_pairs={{0,4},{4,8},{8,12},{12,16},{16,20},{20,24},{24,28},{28,0},{1,5},{5... | collective-permute-start | bytes 786440 | tf_op jit(solution)/shard_map/ppermute | solution.py:266
  68.0 16.5 %collective-permute-start.14 = (bf16[4,2,16,1024]{3,2,1,0:T(8,128)(2,1)S(1)}, bf16[4,2,16,1024]{3,2,1,0:T(8,128)(2,1)S(1)}, u32[]{:S(2)}, u32[]{:S(2)}) collective-permute-start(bf16[4,2,16,1024]{3,2,1,0:T(8,128)(2,1)S(1)} %pad_maximum_fusion.rest_0_), channel_id=1, source_target_pairs={{0,2},{2,0},{1,3},{3,1},{4,6},{6,4},{5,7},{7,5},{8,10},{10,8},{9,1... | collective-permute-start | bytes 786440 | tf_op jit(solution)/shard_map/ppermute | solution.py:266
  77.0 7.5 %collective-permute-start.16 = (bf16[4,2,16,1024]{3,2,1,0:T(8,128)(2,1)S(1)}, bf16[4,2,16,1024]{3,2,1,0:T(8,128)(2,1)S(1)}, u32[]{:S(2)}, u32[]{:S(2)}) collective-permute-start(bf16[4,2,16,1024]{3,2,1,0:T(8,128)(2,1)S(1)} %collective-permute-done.7.rest_2_), channel_id=1, source_target_pairs={{0,2},{2,0},{1,3},{3,1},{4,6},{6,4},{5,7},{7,5},{8,10},{10,8},{9,1... | collective-permute-start | bytes 786440 | tf_op jit(solution)/shard_map/ppermute | solution.py:266
  77.0 9.6 %collective-permute-start.15 = (bf16[4,2,16,1024]{3,2,1,0:T(8,128)(2,1)S(1)}, bf16[4,2,16,1024]{3,2,1,0:T(8,128)(2,1)S(1)}, u32[]{:S(2)}, u32[]{:S(2)}) collective-permute-start(bf16[4,2,16,1024]{3,2,1,0:T(8,128)(2,1)S(1)} %collective-permute-done.6.rest_1_), channel_id=1, source_target_pairs={{0,2},{2,0},{1,3},{3,1},{4,6},{6,4},{5,7},{7,5},{8,10},{10,8},{9,1... | collective-permute-start | bytes 786440 | tf_op jit(solution)/shard_map/ppermute | solution.py:266
  77.6 9.2 %collective-permute-start.18 = (bf16[4,2,16,1024]{3,2,1,0:T(8,128)(2,1)S(1)}, bf16[4,2,16,1024]{3,2,1,0:T(8,128)(2,1)S(1)}, u32[]{:S(2)}, u32[]{:S(2)}) collective-permute-start(bf16[4,2,16,1024]{3,2,1,0:T(8,128)(2,1)S(1)} %collective-permute-done.9.rest_4_), channel_id=1, source_target_pairs={{0,2},{2,0},{1,3},{3,1},{4,6},{6,4},{5,7},{7,5},{8,10},{10,8},{9,1... | collective-permute-start | bytes 786440 | tf_op jit(solution)/shard_map/ppermute | solution.py:266
  81.5 6.3 %collective-permute-start.13 = (bf16[2,2,16,1024]{3,2,1,0:T(8,128)(2,1)}, bf16[2,2,16,1024]{3,2,1,0:T(8,128)(2,1)}, u32[]{:S(2)}, u32[]{:S(2)}) collective-permute-start(bf16[2,2,16,1024]{3,2,1,0:T(8,128)(2,1)} %slice.9), channel_id=1, source_target_pairs={{0,28},{4,0},{8,4},{12,8},{16,12},{20,16},{24,20},{28,24},{1,29},{... | collective-permute-start | bytes 393224 | tf_op jit(solution)/shard_map/ppermute | solution.py:266
  84.6 6.3 %collective-permute-start.12 = (bf16[2,2,16,1024]{3,2,1,0:T(8,128)(2,1)}, bf16[2,2,16,1024]{3,2,1,0:T(8,128)(2,1)}, u32[]{:S(2)}, u32[]{:S(2)}) collective-permute-start(bf16[2,2,16,1024]{3,2,1,0:T(8,128)(2,1)} %slice.8), channel_id=1, source_target_pairs={{0,4},{4,8},{8,12},{12,16},{16,20},{20,24},{24,28},{28,0},{1,5},{5... | collective-permute-start | bytes 393224 | tf_op jit(solution)/shard_map/ppermute | solution.py:266
  84.6 9.2 %collective-permute-start.17 = (bf16[4,2,16,1024]{3,2,1,0:T(8,128)(2,1)S(1)}, bf16[4,2,16,1024]{3,2,1,0:T(8,128)(2,1)S(1)}, u32[]{:S(2)}, u32[]{:S(2)}) collective-permute-start(bf16[4,2,16,1024]{3,2,1,0:T(8,128)(2,1)S(1)} %collective-permute-done.8.rest_3_), channel_id=1, source_target_pairs={{0,2},{2,0},{1,3},{3,1},{4,6},{6,4},{5,7},{7,5},{8,10},{10,8},{9,1... | collective-permute-start | bytes 786440 | tf_op jit(solution)/shard_map/ppermute | solution.py:266
  86.6 7.2 %collective-permute-start.20 = (bf16[4,2,16,1024]{3,2,1,0:T(8,128)(2,1)S(1)}, bf16[4,2,16,1024]{3,2,1,0:T(8,128)(2,1)S(1)}, u32[]{:S(2)}, u32[]{:S(2)}) collective-permute-start(bf16[4,2,16,1024]{3,2,1,0:T(8,128)(2,1)S(1)} %collective-permute-done.11.rest_6_), channel_id=1, source_target_pairs={{0,2},{2,0},{1,3},{3,1},{4,6},{6,4},{5,7},{7,5},{8,10},{10,8},{9,1... | collective-permute-start | bytes 786440 | tf_op jit(solution)/shard_map/ppermute | solution.py:266
  86.7 7.1 %collective-permute-start.19 = (bf16[4,2,16,1024]{3,2,1,0:T(8,128)(2,1)S(1)}, bf16[4,2,16,1024]{3,2,1,0:T(8,128)(2,1)}, u32[]{:S(2)}, u32[]{:S(2)}) collective-permute-start(bf16[4,2,16,1024]{3,2,1,0:T(8,128)(2,1)S(1)} %collective-permute-done.10.rest_5_), channel_id=1, source_target_pairs={{0,2},{2,0},{1,3},{3,1},{4,6},{6,4},{5,7},{7,5},{8,10},{10,8},{9,1... | collective-permute-start | bytes 786440 | tf_op jit(solution)/shard_map/ppermute | solution.py:266
  87.8 6.0 %collective-permute-start.22 = (bf16[2,2,16,1024]{3,2,1,0:T(8,128)(2,1)}, bf16[2,2,16,1024]{3,2,1,0:T(8,128)(2,1)S(1)}, u32[]{:S(2)}, u32[]{:S(2)}) collective-permute-start(bf16[2,2,16,1024]{3,2,1,0:T(8,128)(2,1)} %collective-permute-done.13.rest_8_), channel_id=1, source_target_pairs={{0,2},{2,0},{1,3},{3,1},{4,6},{6,4},{5,7},{7,5},{8,10},{10,8},{9,1... | collective-permute-start | bytes 393224 | tf_op jit(solution)/shard_map/ppermute | solution.py:266
  90.9 2.9 %collective-permute-start.21 = (bf16[2,2,16,1024]{3,2,1,0:T(8,128)(2,1)}, bf16[2,2,16,1024]{3,2,1,0:T(8,128)(2,1)S(1)}, u32[]{:S(2)}, u32[]{:S(2)}) collective-permute-start(bf16[2,2,16,1024]{3,2,1,0:T(8,128)(2,1)} %collective-permute-done.12.rest_7_), channel_id=1, source_target_pairs={{0,2},{2,0},{1,3},{3,1},{4,6},{6,4},{5,7},{7,5},{8,10},{10,8},{9,1... | collective-permute-start | bytes 393224 | tf_op jit(solution)/shard_map/ppermute | solution.py:266
  93.8 0.8 copy-start.4

commit v2 on v1

v2 whole, which is shorter than its diff:
```python
import functools
import math

import jax
import jax.numpy as jnp
import ml_dtypes
import numpy as np
from jax import lax
from jax.experimental import pallas as pl
from jax.experimental.pallas import tpu as pltpu
from jax.sharding import Mesh, PartitionSpec as P

L = 4096
TAPS = 127
FB = 64
BIN0 = 16
LAGW = 128
STD = 16
WDEV = 8
HALF = 1024

smooth_half = 4
floor_share = 0.25
spread_eps = 1e-06

column = np.arange(128)
column_bin = column // 16 * 8 + column % 8
column_im = column // 8 % 2

STA = ("ylo", "x", "z", "core")


def unit_angle(product):
    return ((product % L).astype(np.float32) * np.float32(2.0 * math.pi / L)).astype(np.float64)


def dft_table():
    angle = unit_angle(np.arange(L)[:, None] * (BIN0 + column_bin)[None, :])
    table = np.where(column_im == 0, np.cos(angle), -np.sin(angle))
    return table.astype(np.float32).astype(ml_dtypes.bfloat16)


def lag_table():
    angle = unit_angle((BIN0 + column_bin)[:, None] * np.arange(LAGW)[None, :])
    table = np.where(column_im[:, None] == 0, np.cos(angle), -np.sin(angle))
    return (table / math.sqrt(FB * 16)).astype(np.float32).astype(ml_dtypes.bfloat16)


def band_table():
    near = np.abs(column_bin[:, None] - column_bin[None, :]) <= smooth_half
    counts = (
        np.minimum(column_bin + smooth_half, FB - 1) - np.maximum(column_bin - smooth_half, 0) + 1
    )
    band = np.where(near & (column_im[:, None] == 0), 1.0, 0.0).astype(np.float32)
    return band, (1.0 / counts).astype(np.float32)[None, :]


def swap_parts(values):
    lane = lax.broadcasted_iota(jnp.int32, values.shape, 1)
    first = (lane // 8) % 2 == 0
    width = values.shape[1]
    return jnp.where(first, pltpu.roll(values, width - 8, 1), pltpu.roll(values, 8, 1))


def whiten_kernel(taps_ref, raw_hbm, basis_hbm, band_ref, inverse_ref, out_ref, raw_ref, basis_ref, wide, sems):
    raw_copies = []
    for chunk in range(4):
        columns = slice(chunk * 1024, (chunk + 1) * 1024)
        raw_copies.append(
            pltpu.make_async_copy(raw_hbm.at[:, columns], raw_ref.at[:, columns], sems.at[chunk])
        )
    basis_copy = pltpu.make_async_copy(basis_hbm, basis_ref, sems.at[4])
    raw_copies[0].start()
    raw_copies[1].start()
    basis_copy.start()
    raw_copies[2].start()
    raw_copies[3].start()

    wide[...] = jnp.zeros((1, 512), jnp.float32)
    wide[:, :TAPS] = taps_ref[...].astype(jnp.float32)
    taps = jnp.broadcast_to(wide[...], (128, 512))
    chunks = []
    for chunk in range(4):
        first_shift = 128 * (chunk - 1) - 63
        moved = pltpu.roll(taps, first_shift % 512, 1, stride=1, stride_axis=0)
        chunks.append(moved[:, :256].astype(jnp.bfloat16))
    fir = jnp.concatenate(chunks, axis=0)
    spectrum = jnp.zeros((256, 128), jnp.float32)
    arrived = 0
    for tile in range(L // 256):
        first, last = 256 * tile - 128, 256 * tile + 384
        low, high = max(first, 0), min(last, L)
        while arrived * 1024 < high:
            raw_copies[arrived].wait()
            arrived += 1
        if tile == 0:
            basis_copy.wait()
        filtered = jnp.dot(
            raw_ref[:, low:high],
            fir[low - first : 512 - (last - high)],
            preferred_element_type=jnp.float32,
        ).astype(jnp.bfloat16)
        spectrum += jnp.dot(
            filtered,
            basis_ref[256 * tile : 256 * (tile + 1), :],
            preferred_element_type=jnp.float32,
        )
    square = spectrum * spectrum
    magnitude = jnp.sqrt(square + swap_parts(square))
    amplitude = (
        jnp.dot(
            magnitude,
            band_ref[...],
            precision=lax.Precision.HIGHEST,
            preferred_element_type=jnp.float32,
        )
        * inverse_ref[...]
    )
    spread = jnp.sqrt(jnp.sum(square, axis=1, keepdims=True) * (1.0 / FB) + spread_eps)
    divisor = jnp.maximum(amplitude, floor_share * spread)
    out_ref[...] = (spectrum / divisor).astype(jnp.bfloat16)


def whiten(taps, raw):
    band, inverse = band_table()
    return pl.pallas_call(
        whiten_kernel,
        out_shape=jax.ShapeDtypeStruct((256, 128), jnp.bfloat16),
        in_specs=[
            pl.BlockSpec(memory_space=pltpu.VMEM),
            pl.BlockSpec(memory_space=pl.ANY),
            pl.BlockSpec(memory_space=pl.ANY),
            pl.BlockSpec(memory_space=pltpu.VMEM),
            pl.BlockSpec(memory_space=pltpu.VMEM),
        ],
        scratch_shapes=[
            pltpu.VMEM((256, L), jnp.bfloat16),
            pltpu.VMEM((L, 128), jnp.bfloat16),
            pltpu.VMEM((1, 512), jnp.float32),
            pltpu.SemaphoreType.DMA((5,)),
        ],
        compiler_params=pltpu.CompilerParams(vmem_limit_bytes=56 * 1024 * 1024),
        name="whiten",
    )(taps, raw, jnp.asarray(dft_table()), jnp.asarray(band), jnp.asarray(inverse))


def select_kernel(slot_ref, present_ref, rows_ref, out_ref):
    entry = lax.broadcasted_iota(jnp.int32, (128, 256), 1)
    selector = (slot_ref[...] == entry).astype(jnp.bfloat16)
    chosen = jnp.dot(selector, rows_ref[...], preferred_element_type=jnp.float32)
    chosen = chosen * present_ref[...].astype(jnp.float32)
    lane = lax.broadcasted_iota(jnp.int32, (STD, 128), 1) // 16
    for group in range(8):
        packed = jnp.zeros((STD, 128), jnp.float32)
        for window in range(WDEV):
            rows = chosen[window * STD : (window + 1) * STD]
            moved = pltpu.roll(rows, (window - group) * 16 % 128, 1) if window != group else rows
            packed = jnp.where(lane == window, moved, packed)
        out_ref[:, group * 128 : (group + 1) * 128] = packed.astype(jnp.bfloat16)


def select(slots, present, rows):
    return pl.pallas_call(
        select_kernel,
        out_shape=jax.ShapeDtypeStruct((STD, 1024), jnp.bfloat16),
        name="select",
    )(slots.reshape(-1, 1), present.reshape(-1, 1), rows)


cos_terms = (0.999999211, -19.7389804, 64.9286574, -85.2716215, 58.7904921, -21.0711056)
sin_terms = (6.28318492, -41.3415892, 81.5999433, -76.6144725, 41.3428824, -12.4712435)


def cos_sin(steps):
    turn = steps * (1.0 / L)
    turn = turn - jnp.round(turn)
    square = turn * turn
    cosine = jnp.full_like(square, cos_terms[-1])
    sine = jnp.full_like(square, sin_terms[-1])
    for cos_term, sin_term in zip(cos_terms[-2::-1], sin_terms[-2::-1]):
        cosine = cosine * square + cos_term
        sine = sine * square + sin_term
    return cosine, sine * turn


def phase_kernel(place_ref, lag_ref, out_ref):
    x, core = place_ref[0], place_ref[1]
    lane = lax.broadcasted_iota(jnp.int32, (STD, 128), 1)
    bins = (lax.broadcasted_iota(jnp.int32, (8, 128), 0) + BIN0).astype(jnp.float32)
    for z in range(8):
        tile = jnp.zeros((STD, 128), jnp.int32)
        for x_at in range(4):
            first = (x_at * 256 + z * 32) // 128 * 128
            part = lag_ref[:, first : first + 128]
            by = (x_at - z % 4) * 32 % 128
            tile = jnp.where(lane // 32 == x_at, pltpu.roll(part, by, 1) if by else part, tile)
        tile = pltpu.roll(tile, lax.rem(128 - 32 * x, 128), 1)
        crossed = jnp.where((lane // 16) % 2 == 0, pltpu.roll(tile, 112, 1), pltpu.roll(tile, 16, 1))
        lag = jnp.where(core == 1, crossed, tile).astype(jnp.float32)
        out_ref[z, 256:272, :], out_ref[z, 272:288, :] = cos_sin(lag * 8.0)
        for station in range(STD):
            low, high = station * 8, station * 8 + 8
            steps = jnp.broadcast_to(lag[station : station + 1], (8, 128)) * bins
            out_ref[z, low:high, :], out_ref[z, 128 + low : 128 + high, :] = cos_sin(steps)


def phases(place, lag):
    return pl.pallas_call(
        phase_kernel,
        in_specs=[pl.BlockSpec(memory_space=pltpu.SMEM), pl.BlockSpec(memory_space=pltpu.VMEM)],
        out_shape=jax.ShapeDtypeStruct((8, 288, 128), jnp.float32),
        cost_estimate=pl.CostEstimate(flops=1 << 20, bytes_accessed=1 << 16, transcendentals=0),
        name="phases",
    )(place, lag)


def weight_kernel(yhi_ref, mine_ref, other_ref, table_ref, out_ref):
    out_ref[8, :128, :128] = table_ref[...]
    mine_first = yhi_ref[0] == 0
    own_lane = lax.broadcasted_iota(jnp.int32, (8, 256), 1)
    same_bin = own_lane % 8 == lax.broadcasted_iota(jnp.int32, (8, 256), 0)
    first = (lax.broadcasted_iota(jnp.int32, (STD, 256), 1) // 8) % 2 == 0
    for group in range(8):
        lanes = slice(group * 128, (group + 1) * 128)
        mine = mine_ref[:, lanes].astype(jnp.float32)
        other = other_ref[:, lanes].astype(jnp.float32)
        early = jnp.where(mine_first, mine, other)
        own = jnp.concatenate([early, jnp.where(mine_first, other, mine)], axis=1)
        swapped = swap_parts(own)
        swapped = jnp.where(first, swapped, -swapped)
        rows = []
        for station in range(STD):
            for part in (own, swapped):
                row = jnp.broadcast_to(part[station : station + 1], (8, 256))
                rows.append(jnp.where(same_bin, row, 0.0))
        out_ref[group] = jnp.concatenate(rows, axis=0).astype(jnp.bfloat16)


def pair_weights(yhi, mine, other):
    return pl.pallas_call(
        weight_kernel,
        in_specs=[
            pl.BlockSpec(memory_space=pltpu.SMEM),
            pl.BlockSpec(memory_space=pltpu.VMEM),
            pl.BlockSpec(memory_space=pltpu.VMEM),
            pl.BlockSpec(memory_space=pltpu.VMEM),
        ],
        out_shape=jax.ShapeDtypeStruct((9, 256, 256), jnp.bfloat16),
        cost_estimate=pl.CostEstimate(flops=1 << 20, bytes_accessed=1 << 16, transcendentals=0),
        name="pair_weights",
    )(yhi, mine, other, jnp.asarray(lag_table()))


def correlate_kernel(layout, place_ref, weight_ref, turn_ref, *rest):
    count = sum(len(parts) for parts in layout)
    mine, theirs = rest[:count], rest[count : 2 * count]
    out_ref, cross = rest[-2:]
    step = pl.program_id(0)
    x, core = place_ref[0], place_ref[1]

    @pl.when(step == 0)
    def _():
        for group in range(8):
            lanes = slice(group * 128, (group + 1) * 128)
            halves = []
            for half in range(2):
                blocks = []
                for parts in layout:
                    for number, rows in parts:
                        for row in range(rows):
                            blocks.append(mine[number][row, half, :, lanes])
                            blocks.append(theirs[number][row, half, :, lanes])
                halves.append(jnp.concatenate(blocks, axis=0))
            product = lax.dot_general(
                weight_ref[group],
                jnp.concatenate(halves, axis=1),
                (((1,), (1,)), ((), ())),
                preferred_element_type=jnp.float32,
            )
            for at in range(len(layout)):
                cross[at, group] = product[:, at * 128 : (at + 1) * 128]

    for station in range(STD):
        top = station * 16
        cosine = turn_ref[0, station * 8 : station * 8 + 8, :]
        sine = turn_ref[0, station * 8 + 128 : station * 8 + 136, :]
        cos_next = jnp.broadcast_to(turn_ref[0, station + 256 : station + 257, :], (8, 128))
        sin_next = jnp.broadcast_to(turn_ref[0, station + 272 : station + 273, :], (8, 128))
        rotated = []
        for group in range(8):
            real = cross[step, group, top : top + 8, :]
            imag = cross[step, group, top + 8 : top + 16, :]
            rotated.append(real * cosine - imag * sine)
            rotated.append(real * sine + imag * cosine)
            if group < 7:
                cosine, sine = (
                    cosine * cos_next - sine * sin_next,
                    cosine * sin_next + sine * cos_next,
                )
        rotated = jnp.concatenate(rotated, axis=0).astype(jnp.bfloat16)
        values = lax.dot_general(
            rotated, weight_ref[8, :128, :128], (((0,), (0,)), ((), ())), preferred_element_type=jnp.float32
        )
        for ahead in range(4):
            for other in range(2):
                row = pl.multiple_of(lax.rem(core + other, 2) * 16, 16)
                first = ahead * 32 + other * 16
                out_ref[station, lax.rem(x + ahead, 4), 0, pl.ds(row, 16), :] = values[
                    first : first + 16
                ]


def correlate(place, weights, turns, previous, hop, mine, theirs):
    cost = (1 << 31, 1 << 30, 1 << 28, 1 << 31, 1 << 30)[hop]
    layout, number = [], 0
    for parts in mine:
        layout.append([])
        for part in parts:
            layout[-1].append((number, part.shape[0]))
            number += 1
    steps = len(layout)

    def z_at(step, place):
        return lax.rem(place[2] + (8 - hop) + step * (2 * hop - 8), 8)

    whole = lambda shape: pl.BlockSpec(shape, lambda step, place: (0,) * len(shape))
    blocks = [part for parts in mine for part in parts] + [part for parts in theirs for part in parts]
    operands = [place, weights, turns, *blocks]
    in_specs = [whole((9, 256, 256))]
    in_specs += [pl.BlockSpec((1, 288, 128), lambda step, place: (z_at(step, place), 0, 0))]
    in_specs += [whole(block.shape) for block in blocks]
    aliases = {}
    if previous is not None:
        aliases = {len(operands): 0}
        operands.append(previous)
        in_specs.append(pl.BlockSpec(memory_space=pl.ANY))
    return pl.pallas_call(
        functools.partial(correlate_kernel, layout),
        grid_spec=pltpu.PrefetchScalarGridSpec(
            num_scalar_prefetch=1,
            grid=(steps,),
            in_specs=in_specs,
            out_specs=pl.BlockSpec(
                (STD, 4, 1, 32, LAGW), lambda step, place: (0, 0, z_at(step, place), 0, 0)
            ),
            scratch_shapes=[pltpu.VMEM((steps, 8, 256, 128), jnp.float32)],
        ),
        out_shape=jax.ShapeDtypeStruct((STD, 4, 8, 32, LAGW), jnp.float32),
        input_output_aliases=aliases,
        compiler_params=pltpu.CompilerParams(
            vmem_limit_bytes=24 * 1024 * 1024, dimension_semantics=("arbitrary",)
        ),
        cost_estimate=pl.CostEstimate(
            flops=cost, bytes_accessed=1 << 16, transcendentals=0
        ),
        name="correlate",
    )(*operands)


def shift(value, axis, size, by):
    return lax.ppermute(value, axis, [(at, (at + by) % size) for at in range(size)])


def per_device(raw_traces, fir_taps, source_slot, present, lag_start):
    ylo, yhi = lax.axis_index("ylo"), lax.axis_index("yhi")
    place = jnp.stack([lax.axis_index("x"), lax.axis_index("core"), lax.axis_index("z")])
    lag = lax.dynamic_slice_in_dim(lag_start, yhi * HALF, HALF, 1)
    white = whiten(fir_taps.reshape(1, TAPS), raw_traces[0])
    white, lag = lax.optimization_barrier((white, lag))
    received = lax.all_to_all(white, STA, split_axis=0, concat_axis=0, tiled=True)
    received, place, turns = lax.optimization_barrier((received, place, phases(place, lag)))
    mine = select(source_slot, present, received)

    ring = lax.ppermute(mine, ("ylo", "yhi"), [(0, 2), (2, 3), (3, 1), (1, 0)])
    middle = lax.ppermute(mine, ("ylo", "yhi"), [(1, 2), (2, 1)])
    y = 2 * yhi + ylo
    early = jnp.where(y == 0, mine, jnp.where(y == 2, middle, ring))
    late = jnp.where(y == 3, mine, jnp.where(y == 1, middle, ring))
    block = jnp.stack([early, late])
    block, mine = lax.optimization_barrier((block, mine))
    other = shift(mine, "yhi", 2, 1)
    blocks = [block] + [shift(block, "x", 4, -by) for by in (1, 2, 3)]
    blocks, other = lax.optimization_barrier((blocks, other))
    line = jnp.stack(blocks)
    weights = pair_weights(yhi.reshape(1), mine, other)

    across = lambda value: shift(value, "core", 2, 1)
    up = down = line
    hops = [[[line]]]
    for _ in range(3):
        up, down = shift(up, "z", 8, 1), shift(down, "z", 8, -1)
        hops.append([[up], [down]])
    hops.append([[shift(up[:2], "z", 8, 1), shift(down[2:], "z", 8, -1)]])
    out = None
    for hop, mine_here in enumerate(hops):
        ready = mine_here
        if hop in (1, 2):
            ready, out = lax.optimization_barrier((mine_here, out))
        theirs = [[across(part) for part in parts] for parts in ready]
        out = correlate(place, weights, turns, out, hop, mine_here, theirs)
    return out.reshape(STD, HALF, LAGW)


def solution(mesh):
    fine = Mesh(mesh.devices.reshape(2, 4, 8, 2, 2), STA + ("yhi",))
    placed = (P("yhi", STA, None), P(), P("yhi", STA), P("yhi", STA), P(STA, None))
    return jax.shard_map(
        per_device, mesh=fine, in_specs=placed, out_specs=P(STA, "yhi", None), check_vma=False
    )
```

time: 109 us -> 91.4 us (0.84)
  waiting for transfers between devices: 25.1 us -> 9.72 us
  Pallas kernels: 21 us -> 27.5 us
  starting transfers between devices: 48.1 us -> 44.1 us
  local copies, waits for them, and re-layouts: 11.3 us -> 8.06 us
  other arithmetic: 2.99 us -> 1.37 us
    ppermute x21, waiting for transfers between devices: 15.9 us -> 3.28 us  [shift(): lax.ppermute(value, axis, [(at, (at + by) % size) for at in range(size)])]
    pallas_call x2 -> x8, Pallas kernels: 19.1 us -> 25.6 us  [the longest x5 13 us: correlate(): pl.pallas_call(functools.partial(correlate_kernel, layout), grid_spec=plt...]
    ppermute x21, starting transfers between devices: 29 us -> 25 us  [shift(): lax.ppermute(value, axis, [(at, (at + by) % size) for at in range(size)])]
    all_to_all x1, waiting for transfers between devices: 7.85 us -> 4.59 us  [per_device(): lax.all_to_all(white, STA, split_axis=0, concat_axis=0, tiled=True)]
    slice x2, local copies, waits for them, and re-layouts: 1.32 us -> 0.02 us  [per_device(): hops.append([[shift(up[:2], 'z', 8, 1), shift(down[2:], 'z', 8, -1)]])]
    unnamed x14 -> x12, local copies, waits for them, and re-layouts: 5.68 us -> 4.62 us
  transfers between devices with their start and end apart: 24 -> 24, of which waited for: 11 -> 4; matrix products, arithmetic and copies ran while one was open for 6% -> 4% of each run, Pallas kernels for 0% -> 17%
where the time goes in v2:
time: 91.4 us; the launch traced here: 90.8 us
  starting transfers between devices  44.1 us (48%)
  Pallas kernels  27.5 us (30%)
  waiting for transfers between devices  9.72 us (11%)
  local copies, waits for them, and re-layouts  8.06 us (9%)
  other arithmetic  1.37 us (1%)
    ppermute x21, starting transfers between devices, shift(): lax.ppermute(value, axis, [(at, (at + by) % size) for at in range(size)])  25 us
    all_to_all x1, starting transfers between devices, per_device(): lax.all_to_all(white, STA, split_axis=0, concat_axis=0, tiled=True)  14.8 us
    pallas_call x5, Pallas kernels, correlate(): pl.pallas_call(functools.partial(correlate_kernel, layout), grid_spec=plt...  13 us
    pallas_call x1, Pallas kernels, whiten(): pl.pallas_call(whiten_kernel, out_shape=jax.ShapeDtypeStruct((256, 128),...  7.93 us
    unnamed x12, local copies, waits for them, and re-layouts  4.62 us
    all_to_all x1, waiting for transfers between devices, per_device(): lax.all_to_all(white, STA, split_axis=0, concat_axis=0, tiled=True)  4.59 us
    ppermute x1, starting transfers between devices, per_device(): ring = lax.ppermute(mine, ('ylo', 'yhi'), [(0, 2), (2, 3), (3, 1), (1, 0)])  3.62 us
    ppermute x21, waiting for transfers between devices, shift(): lax.ppermute(value, axis, [(at, (at + by) % size) for at in range(size)])  3.28 us
  transfers between devices with their start and end apart: 24, of which 4 were waited for; matrix products, arithmetic and copies ran while one was open for 4% of the time, Pallas kernels for 17%

profile of v2, /device:TPU:1, one launch (start us, length us, event | category | flops | bytes accessed | tf_op | source)
XLA Modules:
  0.0 90.8 jit_solution(365964390233218093)
XLA Ops:
  0.0 0.9 copy-done
  1.5 7.9 %whiten.1 = bf16[256,128]{1,0:T(8,128)(2,1)} custom-call(bf16[1,127]{1,0:T(2,128)(2,1)} %bitcast.24, bf16[256,4096]{1,0:T(8,128)(2,1)} %bitcast.17, bf16[4096,128]{1,0:T(8,128)(2,1)} %constant.40.clone.basis_hbm, f32[128,128]{1,0:T(8,128)} %constant.41.clone.band_ref, f32[1,128]{1,0:T(1,128)} %constant.42.clone.inverse_ref), custom_call_target="tpu_custom_call" | custom-call | tf_op jit(solution)/shard_map/whiten/pallas_call | solution.py:126
  9.5 14.8 %all-to-all-start = ((bf16[128,2,128]{2,1,0:T(2,128)(2,1)}), bf16[128,2,128]{2,1,0:T(2,128)(2,1)S(1)}, u32[]{:S(2)}, u32[]{:S(2)}) async-start(bf16[128,2,128]{2,1,0:T(2,128)(2,1)} %bitcast.19), calls=%async_computation | async-start | bytes 131072 | tf_op jit(solution)/shard_map/all_to_all | solution.py:370
  24.3 1.4 %reshape.22.slot_ref = s32[128,1]{1,0:T(8,128)} reshape(s32[8,16]{1,0:T(8,128)} %param.11) | data formatting | bytes 1024 | tf_op jit(solution)/shard_map/reshape | solution.py:167
  25.7 1.4 %reshape.23.present_ref = s32[128,1]{1,0:T(8,128)} reshape(s32[8,16]{1,0:T(8,128)} %param.12) | data formatting | bytes 1024 | tf_op jit(solution)/shard_map/reshape | solution.py:167
  27.6 2.6 %phases.1.turn_ref = f32[8,288,128]{2,1,0:T(8,128)} custom-call(s32[3]{0:T(128)} %pad_add_fusion.place_ref, s32[16,1024]{1,0:T(8,128)} %constant_dynamic-slice_fusion.lag_ref), custom_call_target="tpu_custom_call" | custom-call | flops 1048576 | bytes 65536 | tf_op jit(solution)/shard_map/phases/pallas_call | solution.py:208
  30.3 4.6 %all-to-all-done = bf16[128,2,128]{2,1,0:T(2,128)(2,1)S(1)} async-done(((bf16[128,2,128]{2,1,0:T(2,128)(2,1)}), bf16[128,2,128]{2,1,0:T(2,128)(2,1)S(1)}, u32[]{:S(2)}, u32[]{:S(2)}) %all-to-all-start) | async-done | bytes 65568 | tf_op jit(solution)/shard_map/all_to_all | solution.py:370
  35.5 1.8 %select.1.mine_ref = bf16[16,1024]{1,0:T(8,128)(2,1)} custom-call(s32[128,1]{1,0:T(8,128)} %reshape.22.slot_ref, s32[128,1]{1,0:T(8,128)} %reshape.23.present_ref, bf16[256,128]{1,0:T(8,128)(2,1)} %bitcast.18), custom_call_target="tpu_custom_call" | custom-call | tf_op jit(solution)/shard_map/select/pallas_call | solution.py:163
  38.0 3.6 %collective-permute-start.1 = (bf16[16,1024]{1,0:T(8,128)(2,1)}, bf16[16,1024]{1,0:T(8,128)(2,1)S(1)}, u32[]{:S(2)}, u32[]{:S(2)}) collective-permute-start(bf16[16,1024]{1,0:T(8,128)(2,1)} %select.1.mine_ref), channel_id=1, source_target_pairs={{0,128},{128,129},{129,1},{1,0},{2,130},{130,131},{131,3},{3,2},{4... | collective-permute-start | bytes 98312 | tf_op jit(solution)/shard_map/ppermute | solution.py:374
  41.6 1.8 %collective-permute-done.1 = bf16[16,1024]{1,0:T(8,128)(2,1)S(1)} collective-permute-done((bf16[16,1024]{1,0:T(8,128)(2,1)}, bf16[16,1024]{1,0:T(8,128)(2,1)S(1)}, u32[]{:S(2)}, u32[]{:S(2)}) %collective-permute-start.1) | collective-permute-done | bytes 32800 | tf_op jit(solution)/shard_map/ppermute | solution.py:374
  44.2 0.9 %collective-permute-start.2 = (bf16[2,16,1024]{2,1,0:T(8,128)(2,1)S(1)}, bf16[2,16,1024]{2,1,0:T(8,128)(2,1)S(1)}, u32[]{:S(2)}, u32[]{:S(2)}) collective-permute-start(bf16[2,16,1024]{2,1,0:T(8,128)(2,1)S(1)} %pad_maximum_fusion.1), channel_id=1, source_target_pairs={{0,96},{32,0},{64,32},{96,64},{1,97},{33,1},{65,33},{97,65},{2,98}... | collective-permute-start | bytes 196616 | tf_op jit(solution)/shard_map/ppermute | solution.py:361
  45.1 1.4 %collective-permute-start.3 = (bf16[2,16,1024]{2,1,0:T(8,128)(2,1)S(1)}, bf16[2,16,1024]{2,1,0:T(8,128)(2,1)S(1)}, u32[]{:S(2)}, u32[]{:S(2)}) collective-permute-start(bf16[2,16,1024]{2,1,0:T(8,128)(2,1)S(1)} %pad_maximum_fusion.1), channel_id=1, source_target_pairs={{0,64},{32,96},{64,0},{96,32},{1,65},{33,97},{65,1},{97,33},{2,66}... | collective-permute-start | bytes 196616 | tf_op jit(solution)/shard_map/ppermute | solution.py:361
  46.5 1.5 %collective-permute-start.5 = (bf16[16,1024]{1,0:T(8,128)(2,1)}, bf16[16,1024]{1,0:T(8,128)(2,1)S(1)}, u32[]{:S(2)}, u32[]{:S(2)}) collective-permute-start(bf16[16,1024]{1,0:T(8,128)(2,1)} %select.1.mine_ref), channel_id=1, source_target_pairs={{0,1},{1,0},{2,3},{3,2},{4,5},{5,4},{6,7},{7,6},{8,9},{9,8},{10,11... | collective-permute-start | bytes 98312 | tf_op jit(solution)/shard_map/ppermute | solution.py:361
  48.0 3.0 %collective-permute-done.5.other_ref = bf16[16,1024]{1,0:T(8,128)(2,1)S(1)} collective-permute-done((bf16[16,1024]{1,0:T(8,128)(2,1)}, bf16[16,1024]{1,0:T(8,128)(2,1)S(1)}, u32[]{:S(2)}, u32[]{:S(2)}) %collective-permute-start.5) | collective-permute-done | bytes 32800 | tf_op jit(solution)/shard_map/ppermute | solution.py:361
  51.5 1.1 %collective-permute-start.6 = (bf16[4,2,16,1024]{3,2,1,0:T(8,128)(2,1)S(1)}, bf16[4,2,16,1024]{3,2,1,0:T(8,128)(2,1)S(1)}, u32[]{:S(2)}, u32[]{:S(2)}) collective-permute-start(bf16[4,2,16,1024]{3,2,1,0:T(8,128)(2,1)S(1)} %pad_maximum_fusion.rest_0_), channel_id=1, source_target_pairs={{0,4},{4,8},{8,12},{12,16},{16,20},{20,24},{24,28},{28,0},{1,5},{5... | collective-permute-start | bytes 786440 | tf_op jit(solution)/shard_map/ppermute | solution.py:361
  52.6 3.9 %collective-permute-start.18 = (bf16[4,2,16,1024]{3,2,1,0:T(8,128)(2,1)S(1)}, bf16[4,2,16,1024]{3,2,1,0:T(8,128)(2,1)S(1)}, u32[]{:S(2)}, u32[]{:S(2)}) collective-permute-start(bf16[4,2,16,1024]{3,2,1,0:T(8,128)(2,1)S(1)} %pad_maximum_fusion.rest_0_), channel_id=1, source_target_pairs={{0,2},{2,0},{1,3},{3,1},{4,6},{6,4},{5,7},{7,5},{8,10},{10,8},{9,1... | collective-permute-start | bytes 786440 | tf_op jit(solution)/shard_map/ppermute | solution.py:361
  56.5 2.0 %pair_weights.1.weight_ref = bf16[9,256,256]{2,1,0:T(8,128)(2,1)} custom-call(s32[1]{0:T(128)} %bitcast.7.yhi_ref, bf16[16,1024]{1,0:T(8,128)(2,1)} %select.1.mine_ref, bf16[16,1024]{1,0:T(8,128)(2,1)} %copy-done.5, bf16[128,128]{1,0:T(8,128)(2,1)} %constant.43.clone.table_ref), custom_call_target="tpu_custom_call" | custom-call | flops 1048576 | bytes 65536 | tf_op jit(solution)/shard_map/pair_weights/pallas_call | solution.py:240
  58.6 1.6 %collective-permute-start.11 = (bf16[4,2,16,1024]{3,2,1,0:T(8,128)(2,1)S(1)}, bf16[4,2,16,1024]{3,2,1,0:T(8,128)(2,1)S(1)}, u32[]{:S(2)}, u32[]{:S(2)}) collective-permute-start(bf16[4,2,16,1024]{3,2,1,0:T(8,128)(2,1)S(1)} %collective-permute-done.10.rest_1_), channel_id=1, source_target_pairs={{0,28},{4,0},{8,4},{12,8},{16,12},{20,16},{24,20},{28,24},{1,29},{... | collective-permute-start | bytes 786440 | tf_op jit(solution)/shard_map/ppermute | solution.py:361
  60.2 1.3 %copy-done.1 = f32[8,288,128]{2,1,0:T(8,128)S(1)} copy-done((f32[8,288,128]{2,1,0:T(8,128)S(1)}, f32[8,288,128]{2,1,0:T(8,128)}, u32[]{:S(2)}) %copy-start.1) | copy-done | bytes 1179672
  61.5 1.3 %copy-done.2 = bf16[9,256,256]{2,1,0:T(8,128)(2,1)S(1)} copy-done((bf16[9,256,256]{2,1,0:T(8,128)(2,1)S(1)}, bf16[9,256,256]{2,1,0:T(8,128)(2,1)}, u32[]{:S(2)}) %copy-start.2) | copy-done | bytes 1179672
  63.3 2.2 %correlate.5.rest_4_ = f32[16,4,8,32,128]{4,3,2,1,0:T(8,128)} custom-call(s32[3]{0:T(128)S(1)} %copy-done.3, bf16[9,256,256]{2,1,0:T(8,128)(2,1)S(1)} %copy-done.2, f32[8,288,128]{2,1,0:T(8,128)S(1)} %copy-done.1, bf16[4,2,16,1024]{3,2,1,0:T(8,128)(2,1)S(1)} %pad_maximum_fusion.rest_0_, bf16[4,2,16,1024]{3,2,1,0:T(8,128)(2,1)S(1)} %collective-permute-done.18.rest_1_), custom_call_target="tpu_custom_call" | custom-call | flops 2147483648 | bytes 65536 | tf_op jit(solution)/shard_map/correlate/pallas_call | solution.py:337
  65.6 2.7 %collective-permute-start.19 = (bf16[4,2,16,1024]{3,2,1,0:T(8,128)(2,1)S(1)}, bf16[4,2,16,1024]{3,2,1,0:T(8,128)(2,1)S(1)}, u32[]{:S(2)}, u32[]{:S(2)}) collective-permute-start(bf16[4,2,16,1024]{3,2,1,0:T(8,128)(2,1)S(1)} %collective-permute-done.6.rest_0_), channel_id=1, source_target_pairs={{0,2},{2,0},{1,3},{3,1},{4,6},{6,4},{5,7},{7,5},{8,10},{10,8},{9,1... | collective-permute-start | bytes 786440 | tf_op jit(solution)/shard_map/ppermute | solution.py:361
  68.6 2.6 %collective-permute-start.12 = (bf16[4,2,16,1024]{3,2,1,0:T(8,128)(2,1)S(1)}, bf16[4,2,16,1024]{3,2,1,0:T(8,128)(2,1)S(1)}, u32[]{:S(2)}, u32[]{:S(2)}) collective-permute-start(bf16[4,2,16,1024]{3,2,1,0:T(8,128)(2,1)S(1)} %collective-permute-done.11.rest_1_), channel_id=1, source_target_pairs={{0,28},{4,0},{8,4},{12,8},{16,12},{20,16},{24,20},{28,24},{1,29},{... | collective-permute-start | bytes 786440 | tf_op jit(solution)/shard_map/ppermute | solution.py:361
  71.2 2.9 %correlate.6.rest_4_ = f32[16,4,8,32,128]{4,3,2,1,0:T(8,128)} custom-call(s32[3]{0:T(128)S(1)} %copy-done.3, bf16[9,256,256]{2,1,0:T(8,128)(2,1)S(1)} %copy-done.2, f32[8,288,128]{2,1,0:T(8,128)S(1)} %copy-done.1, bf16[4,2,16,1024]{3,2,1,0:T(8,128)(2,1)S(1)} %collective-permute-done.6.rest_0_, ...), custom_call_target="tpu_custom_call", output_to_operand_aliasing={{}: (7, {})} | custom-call | flops 1073741824 | bytes 65536 | tf_op jit(solution)/shard_map/correlate/pallas_call | solution.py:337
  74.1 2.4 %collective-permute-start.21 = (bf16[4,2,16,1024]{3,2,1,0:T(8,128)(2,1)S(1)}, bf16[4,2,16,1024]{3,2,1,0:T(8,128)(2,1)S(1)}, u32[]{:S(2)}, u32[]{:S(2)}) collective-permute-start(bf16[4,2,16,1024]{3,2,1,0:T(8,128)(2,1)S(1)} %collective-permute-done.7.rest_0_), channel_id=1, source_target_pairs={{0,2},{2,0},{1,3},{3,1},{4,6},{6,4},{5,7},{7,5},{8,10},{10,8},{9,1... | collective-permute-start | bytes 786440 | tf_op jit(solution)/shard_map/ppermute | solution.py:361
  76.5 1.9 %collective-permute-start.16 = (bf16[4,2,16,1024]{3,2,1,0:T(8,128)(2,1)S(1)}, bf16[4,2,16,1024]{3,2,1,0:T(8,128)(2,1)S(1)}, u32[]{:S(2)}, u32[]{:S(2)}) collective-permute-start(bf16[4,2,16,1024]{3,2,1,0:T(8,128)(2,1)S(1)} %collective-permute-done.8.rest_0_), channel_id=1, source_target_pairs={{0,2},{2,0},{1,3},{3,1},{4,6},{6,4},{5,7},{7,5},{8,10},{10,8},{9,1... | collective-permute-start | bytes 786440 | tf_op jit(solution)/shard_map/ppermute | solution.py:361
  78.4 1.2 %collective-permute-start.9 = (bf16[2,2,16,1024]{3,2,1,0:T(8,128)(2,1)S(1)}, bf16[2,2,16,1024]{3,2,1,0:T(8,128)(2,1)S(1)}, u32[]{:S(2)}, u32[]{:S(2)}) collective-permute-start(bf16[2,2,16,1024]{3,2,1,0:T(8,128)(2,1)S(1)} %slice.8), channel_id=1, source_target_pairs={{0,4},{4,8},{8,12},{12,16},{16,20},{20,24},{24,28},{28,0},{1,5},{5... | collective-permute-start | bytes 393224 | tf_op jit(solution)/shard_map/ppermute | solution.py:361
  79.6 1.8 %collective-permute-start.13 = (bf16[2,2,16,1024]{3,2,1,0:T(8,128)(2,1)S(1)}, bf16[2,2,16,1024]{3,2,1,0:T(8,128)(2,1)S(1)}, u32[]{:S(2)}, u32[]{:S(2)}) collective-permute-start(bf16[2,2,16,1024]{3,2,1,0:T(8,128)(2,1)S(1)} %slice.9), channel_id=1, source_target_pairs={{0,28},{4,0},{8,4},{12,8},{16,12},{20,16},{24,20},{28,24},{1,29},{... | collective-permute-start | bytes 393224 | tf_op jit(solution)/shard_map/ppermute | solution.py:361
  81.4 2.9 %correlate.7.rest_4_ = f32[16,4,8,32,128]{4,3,2,1,0:T(8,128)} custom-call(s32[3]{0:T(128)S(1)} %copy-done.3, bf16[9,256,256]{2,1,0:T(8,128)(2,1)S(1)} %copy-done.2, f32[8,288,128]{2,1,0:T(8,128)S(1)} %copy-done.1, bf16[4,2,16,1024]{3,2,1,0:T(8,128)(2,1)S(1)} %collective-permute-done.7.rest_0_, ...), custom_call_target="tpu_custom_call", output_to_operand_aliasing={{}: (7, {})} | custom-call | flops 268435456 | bytes 65536 | tf_op jit(solution)/shard_map/correlate/pallas_call | solution.py:337
  84.4 1.3 %collective-permute-start.14 = (bf16[2,2,16,1024]{3,2,1,0:T(8,128)(2,1)S(1)}, bf16[2,2,16,1024]{3,2,1,0:T(8,128)(2,1)S(1)}, u32[]{:S(2)}, u32[]{:S(2)}) collective-permute-start(bf16[2,2,16,1024]{3,2,1,0:T(8,128)(2,1)S(1)} %collective-permute-done.9.rest_0_), channel_id=1, source_target_pairs={{0,2},{2,0},{1,3},{3,1},{4,6},{6,4},{5,7},{7,5},{8,10},{10,8},{9,1... | collective-permute-start | bytes 393224 | tf_op jit(solution)/shard_map/ppermute | solution.py:361
  85.7 2.9 %correlate.8.rest_4_ = f32[16,4,8,32,128]{4,3,2,1,0:T(8,128)} custom-call(s32[3]{0:T(128)S(1)} %copy-done.3, bf16[9,256,256]{2,1,0:T(8,128)(2,1)S(1)} %copy-done.2, f32[8,288,128]{2,1,0:T(8,128)S(1)} %copy-done.1, bf16[4,2,16,1024]{3,2,1,0:T(8,128)(2,1)S(1)} %collective-permute-done.8.rest_0_, ...), custom_call_target="tpu_custom_call", output_to_operand_aliasing={{}: (7, {})} | custom-call | flops 2147483648 | bytes 65536 | tf_op jit(solution)/shard_map/correlate/pallas_call | solution.py:337
  88.6 2.2 %correlate.9 = f32[16,4,8,32,128]{4,3,2,1,0:T(8,128)} custom-call(s32[3]{0:T(128)S(1)} %copy-done.3, bf16[9,256,256]{2,1,0:T(8,128)(2,1)S(1)} %copy-done.2, f32[8,288,128]{2,1,0:T(8,128)S(1)} %copy-done.1, bf16[2,2,16,1024]{3,2,1,0:T(8,128)(2,1)S(1)} %collective-permute-done.9.rest_0_, ...), custom_call_target="tpu_custom_call", output_to_operand_aliasing={{}: (7, {})} | custom-call | flops 1073741824 | bytes 65536 | tf_op jit(solution)/shard_map/correlate/pallas_call | solution.py:337
  (46 shorter events, 5.0 us)
Async XLA Ops:
  0.0 0.9 copy-start
  9.5 25.4 %all-to-all-start = ((bf16[128,2,128]{2,1,0:T(2,128)(2,1)}), bf16[128,2,128]{2,1,0:T(2,128)(2,1)S(1)}, u32[]{:S(2)}, u32[]{:S(2)}) async-start(bf16[128,2,128]{2,1,0:T(2,128)(2,1)} %bitcast.19), calls=%async_computation | async-start | bytes 131072 | tf_op jit(solution)/shard_map/all_to_all | solution.py:370
  34.9 0.6 copy-start.4
  37.3 4.3 %collective-permute-start = (bf16[16,1024]{1,0:T(8,128)(2,1)}, bf16[16,1024]{1,0:T(8,128)(2,1)S(1)}, u32[]{:S(2)}, u32[]{:S(2)}) collective-permute-start(bf16[16,1024]{1,0:T(8,128)(2,1)} %select.1.mine_ref), channel_id=1, source_target_pairs={{1,128},{128,1},{3,130},{130,3},{5,132},{132,5},{7,134},{134,7},{9... | collective-permute-start | bytes 98312 | tf_op jit(solution)/shard_map/ppermute | solution.py:375
  38.0 5.5 %collective-permute-start.1 = (bf16[16,1024]{1,0:T(8,128)(2,1)}, bf16[16,1024]{1,0:T(8,128)(2,1)S(1)}, u32[]{:S(2)}, u32[]{:S(2)}) collective-permute-start(bf16[16,1024]{1,0:T(8,128)(2,1)} %select.1.mine_ref), channel_id=1, source_target_pairs={{0,128},{128,129},{129,1},{1,0},{2,130},{130,131},{131,3},{3,2},{4... | collective-permute-start | bytes 98312 | tf_op jit(solution)/shard_map/ppermute | solution.py:374
  44.2 6.8 %collective-permute-start.2 = (bf16[2,16,1024]{2,1,0:T(8,128)(2,1)S(1)}, bf16[2,16,1024]{2,1,0:T(8,128)(2,1)S(1)}, u32[]{:S(2)}, u32[]{:S(2)}) collective-permute-start(bf16[2,16,1024]{2,1,0:T(8,128)(2,1)S(1)} %pad_maximum_fusion.1), channel_id=1, source_target_pairs={{0,96},{32,0},{64,32},{96,64},{1,97},{33,1},{65,33},{97,65},{2,98}... | collective-permute-start | bytes 196616 | tf_op jit(solution)/shard_map/ppermute | solution.py:361
  45.1 5.9 %collective-permute-start.3 = (bf16[2,16,1024]{2,1,0:T(8,128)(2,1)S(1)}, bf16[2,16,1024]{2,1,0:T(8,128)(2,1)S(1)}, u32[]{:S(2)}, u32[]{:S(2)}) collective-permute-start(bf16[2,16,1024]{2,1,0:T(8,128)(2,1)S(1)} %pad_maximum_fusion.1), channel_id=1, source_target_pairs={{0,64},{32,96},{64,0},{96,32},{1,65},{33,97},{65,1},{97,33},{2,66}... | collective-permute-start | bytes 196616 | tf_op jit(solution)/shard_map/ppermute | solution.py:361
  46.5 4.5 %collective-permute-start.4 = (bf16[2,16,1024]{2,1,0:T(8,128)(2,1)S(1)}, bf16[2,16,1024]{2,1,0:T(8,128)(2,1)S(1)}, u32[]{:S(2)}, u32[]{:S(2)}) collective-permute-start(bf16[2,16,1024]{2,1,0:T(8,128)(2,1)S(1)} %pad_maximum_fusion.1), channel_id=1, source_target_pairs={{0,32},{32,64},{64,96},{96,0},{1,33},{33,65},{65,97},{97,1},{2,34}... | collective-permute-start | bytes 196616 | tf_op jit(solution)/shard_map/ppermute | solution.py:361
  46.5 4.5 %collective-permute-start.5 = (bf16[16,1024]{1,0:T(8,128)(2,1)}, bf16[16,1024]{1,0:T(8,128)(2,1)S(1)}, u32[]{:S(2)}, u32[]{:S(2)}) collective-permute-start(bf16[16,1024]{1,0:T(8,128)(2,1)} %select.1.mine_ref), channel_id=1, source_target_pairs={{0,1},{1,0},{2,3},{3,2},{4,5},{5,4},{6,7},{7,6},{8,9},{9,8},{10,11... | collective-permute-start | bytes 98312 | tf_op jit(solution)/shard_map/ppermute | solution.py:361
  51.0 5.5 %copy-start.5 = (bf16[16,1024]{1,0:T(8,128)(2,1)}, bf16[16,1024]{1,0:T(8,128)(2,1)S(1)}, u32[]{:S(2)}) copy-start(bf16[16,1024]{1,0:T(8,128)(2,1)S(1)} %collective-permute-done.5.other_ref) | copy-start | bytes 98308
  51.1 7.5 %collective-permute-start.10 = (bf16[4,2,16,1024]{3,2,1,0:T(8,128)(2,1)S(1)}, bf16[4,2,16,1024]{3,2,1,0:T(8,128)(2,1)S(1)}, u32[]{:S(2)}, u32[]{:S(2)}) collective-permute-start(bf16[4,2,16,1024]{3,2,1,0:T(8,128)(2,1)S(1)} %pad_maximum_fusion.rest_0_), channel_id=1, source_target_pairs={{0,28},{4,0},{8,4},{12,8},{16,12},{20,16},{24,20},{28,24},{1,29},{... | collective-permute-start | bytes 786440 | tf_op jit(solution)/shard_map/ppermute | solution.py:361
  51.5 8.7 %collective-permute-start.6 = (bf16[4,2,16,1024]{3,2,1,0:T(8,128)(2,1)S(1)}, bf16[4,2,16,1024]{3,2,1,0:T(8,128)(2,1)S(1)}, u32[]{:S(2)}, u32[]{:S(2)}) collective-permute-start(bf16[4,2,16,1024]{3,2,1,0:T(8,128)(2,1)S(1)} %pad_maximum_fusion.rest_0_), channel_id=1, source_target_pairs={{0,4},{4,8},{8,12},{12,16},{16,20},{20,24},{24,28},{28,0},{1,5},{5... | collective-permute-start | bytes 786440 | tf_op jit(solution)/shard_map/ppermute | solution.py:361
  52.6 7.6 %collective-permute-start.18 = (bf16[4,2,16,1024]{3,2,1,0:T(8,128)(2,1)S(1)}, bf16[4,2,16,1024]{3,2,1,0:T(8,128)(2,1)S(1)}, u32[]{:S(2)}, u32[]{:S(2)}) collective-permute-start(bf16[4,2,16,1024]{3,2,1,0:T(8,128)(2,1)S(1)} %pad_maximum_fusion.rest_0_), channel_id=1, source_target_pairs={{0,2},{2,0},{1,3},{3,1},{4,6},{6,4},{5,7},{7,5},{8,10},{10,8},{9,1... | collective-permute-start | bytes 786440 | tf_op jit(solution)/shard_map/ppermute | solution.py:361
  58.6 10.1 %collective-permute-start.11 = (bf16[4,2,16,1024]{3,2,1,0:T(8,128)(2,1)S(1)}, bf16[4,2,16,1024]{3,2,1,0:T(8,128)(2,1)S(1)}, u32[]{:S(2)}, u32[]{:S(2)}) collective-permute-start(bf16[4,2,16,1024]{3,2,1,0:T(8,128)(2,1)S(1)} %collective-permute-done.10.rest_1_), channel_id=1, source_target_pairs={{0,28},{4,0},{8,4},{12,8},{16,12},{20,16},{24,20},{28,24},{1,29},{... | collective-permute-start | bytes 786440 | tf_op jit(solution)/shard_map/ppermute | solution.py:361
  60.2 8.0 %collective-permute-start.7 = (bf16[4,2,16,1024]{3,2,1,0:T(8,128)(2,1)S(1)}, bf16[4,2,16,1024]{3,2,1,0:T(8,128)(2,1)S(1)}, u32[]{:S(2)}, u32[]{:S(2)}) collective-permute-start(bf16[4,2,16,1024]{3,2,1,0:T(8,128)(2,1)S(1)} %collective-permute-done.6.rest_0_), channel_id=1, source_target_pairs={{0,4},{4,8},{8,12},{12,16},{16,20},{20,24},{24,28},{28,0},{1,5},{5... | collective-permute-start | bytes 786440 | tf_op jit(solution)/shard_map/ppermute | solution.py:361
  60.2 1.3 %copy-start.1 = (f32[8,288,128]{2,1,0:T(8,128)S(1)}, f32[8,288,128]{2,1,0:T(8,128)}, u32[]{:S(2)}) copy-start(f32[8,288,128]{2,1,0:T(8,128)} %phases.1.turn_ref) | copy-start | bytes 3538948
  61.5 1.3 %copy-start.2 = (bf16[9,256,256]{2,1,0:T(8,128)(2,1)S(1)}, bf16[9,256,256]{2,1,0:T(8,128)(2,1)}, u32[]{:S(2)}) copy-start(bf16[9,256,256]{2,1,0:T(8,128)(2,1)} %pair_weights.1.weight_ref) | copy-start | bytes 3538948
  62.8 0.6 copy-start.3
  65.6 5.6 %collective-permute-start.19 = (bf16[4,2,16,1024]{3,2,1,0:T(8,128)(2,1)S(1)}, bf16[4,2,16,1024]{3,2,1,0:T(8,128)(2,1)S(1)}, u32[]{:S(2)}, u32[]{:S(2)}) collective-permute-start(bf16[4,2,16,1024]{3,2,1,0:T(8,128)(2,1)S(1)} %collective-permute-done.6.rest_0_), channel_id=1, source_target_pairs={{0,2},{2,0},{1,3},{3,1},{4,6},{6,4},{5,7},{7,5},{8,10},{10,8},{9,1... | collective-permute-start | bytes 786440 | tf_op jit(solution)/shard_map/ppermute | solution.py:361
  68.3 3.0 %collective-permute-start.20 = (bf16[4,2,16,1024]{3,2,1,0:T(8,128)(2,1)S(1)}, bf16[4,2,16,1024]{3,2,1,0:T(8,128)(2,1)S(1)}, u32[]{:S(2)}, u32[]{:S(2)}) collective-permute-start(bf16[4,2,16,1024]{3,2,1,0:T(8,128)(2,1)S(1)} %collective-permute-done.10.rest_1_), channel_id=1, source_target_pairs={{0,2},{2,0},{1,3},{3,1},{4,6},{6,4},{5,7},{7,5},{8,10},{10,8},{9,1... | collective-permute-start | bytes 786440 | tf_op jit(solution)/shard_map/ppermute | solution.py:361
  68.3 8.3 %collective-permute-start.8 = (bf16[4,2,16,1024]{3,2,1,0:T(8,128)(2,1)S(1)}, bf16[4,2,16,1024]{3,2,1,0:T(8,128)(2,1)S(1)}, u32[]{:S(2)}, u32[]{:S(2)}) collective-permute-start(bf16[4,2,16,1024]{3,2,1,0:T(8,128)(2,1)S(1)} %collective-permute-done.7.rest_0_), channel_id=1, source_target_pairs={{0,4},{4,8},{8,12},{12,16},{16,20},{20,24},{24,28},{28,0},{1,5},{5... | collective-permute-start | bytes 786440 | tf_op jit(solution)/shard_map/ppermute | solution.py:361
  68.6 9.7 %collective-permute-start.12 = (bf16[4,2,16,1024]{3,2,1,0:T(8,128)(2,1)S(1)}, bf16[4,2,16,1024]{3,2,1,0:T(8,128)(2,1)S(1)}, u32[]{:S(2)}, u32[]{:S(2)}) collective-permute-start(bf16[4,2,16,1024]{3,2,1,0:T(8,128)(2,1)S(1)} %collective-permute-done.11.rest_1_), channel_id=1, source_target_pairs={{0,28},{4,0},{8,4},{12,8},{16,12},{20,16},{24,20},{28,24},{1,29},{... | collective-permute-start | bytes 786440 | tf_op jit(solution)/shard_map/ppermute | solution.py:361
  74.1 5.5 %collective-permute-start.21 = (bf16[4,2,16,1024]{3,2,1,0:T(8,128)(2,1)S(1)}, bf16[4,2,16,1024]{3,2,1,0:T(8,128)(2,1)S(1)}, u32[]{:S(2)}, u32[]{:S(2)}) collective-permute-start(bf16[4,2,16,1024]{3,2,1,0:T(8,128)(2,1)S(1)} %collective-permute-done.7.rest_0_), channel_id=1, source_target_pairs={{0,2},{2,0},{1,3},{3,1},{4,6},{6,4},{5,7},{7,5},{8,10},{10,8},{9,1... | collective-permute-start | bytes 786440 | tf_op jit(solution)/shard_map/ppermute | solution.py:361
  76.5 4.8 %collective-permute-start.22 = (bf16[4,2,16,1024]{3,2,1,0:T(8,128)(2,1)S(1)}, bf16[4,2,16,1024]{3,2,1,0:T(8,128)(2,1)S(1)}, u32[]{:S(2)}, u32[]{:S(2)}) collective-permute-start(bf16[4,2,16,1024]{3,2,1,0:T(8,128)(2,1)S(1)} %collective-permute-done.11.rest_1_), channel_id=1, source_target_pairs={{0,2},{2,0},{1,3},{3,1},{4,6},{6,4},{5,7},{7,5},{8,10},{10,8},{9,1... | collective-permute-start | bytes 786440 | tf_op jit(solution)/shard_map/ppermute | solution.py:361
  76.5 9.2 %collective-permute-start.16 = (bf16[4,2,16,1024]{3,2,1,0:T(8,128)(2,1)S(1)}, bf16[4,2,16,1024]{3,2,1,0:T(8,128)(2,1)S(1)}, u32[]{:S(2)}, u32[]{:S(2)}) collective-permute-start(bf16[4,2,16,1024]{3,2,1,0:T(8,128)(2,1)S(1)} %collective-permute-done.8.rest_0_), channel_id=1, source_target_pairs={{0,2},{2,0},{1,3},{3,1},{4,6},{6,4},{5,7},{7,5},{8,10},{10,8},{9,1... | collective-permute-start | bytes 786440 | tf_op jit(solution)/shard_map/ppermute | solution.py:361
  78.4 7.3 %collective-permute-start.17 = (bf16[4,2,16,1024]{3,2,1,0:T(8,128)(2,1)S(1)}, bf16[4,2,16,1024]{3,2,1,0:T(8,128)(2,1)S(1)}, u32[]{:S(2)}, u32[]{:S(2)}) collective-permute-start(bf16[4,2,16,1024]{3,2,1,0:T(8,128)(2,1)S(1)} %collective-permute-done.12.rest_1_), channel_id=1, source_target_pairs={{0,2},{2,0},{1,3},{3,1},{4,6},{6,4},{5,7},{7,5},{8,10},{10,8},{9,1... | collective-permute-start | bytes 786440 | tf_op jit(solution)/shard_map/ppermute | solution.py:361
  78.4 6.0 %collective-permute-start.9 = (bf16[2,2,16,1024]{3,2,1,0:T(8,128)(2,1)S(1)}, bf16[2,2,16,1024]{3,2,1,0:T(8,128)(2,1)S(1)}, u32[]{:S(2)}, u32[]{:S(2)}) collective-permute-start(bf16[2,2,16,1024]{3,2,1,0:T(8,128)(2,1)S(1)} %slice.8), channel_id=1, source_target_pairs={{0,4},{4,8},{8,12},{12,16},{16,20},{20,24},{24,28},{28,0},{1,5},{5... | collective-permute-start | bytes 393224 | tf_op jit(solution)/shard_map/ppermute | solution.py:361
  79.6 6.1 %collective-permute-start.13 = (bf16[2,2,16,1024]{3,2,1,0:T(8,128)(2,1)S(1)}, bf16[2,2,16,1024]{3,2,1,0:T(8,128)(2,1)S(1)}, u32[]{:S(2)}, u32[]{:S(2)}) collective-permute-start(bf16[2,2,16,1024]{3,2,1,0:T(8,128)(2,1)S(1)} %slice.9), channel_id=1, source_target_pairs={{0,28},{4,0},{8,4},{12,8},{16,12},{20,16},{24,20},{28,24},{1,29},{... | collective-permute-start | bytes 393224 | tf_op jit(solution)/shard_map/ppermute | solution.py:361
  84.4 4.2 %collective-permute-start.14 = (bf16[2,2,16,1024]{3,2,1,0:T(8,128)(2,1)S(1)}, bf16[2,2,16,1024]{3,2,1,0:T(8,128)(2,1)S(1)}, u32[]{:S(2)}, u32[]{:S(2)}) collective-permute-start(bf16[2,2,16,1024]{3,2,1,0:T(8,128)(2,1)S(1)} %collective-permute-done.9.rest_0_), channel_id=1, source_target_pairs={{0,2},{2,0},{1,3},{3,1},{4,6},{6,4},{5,7},{7,5},{8,10},{10,8},{9,1... | collective-permute-start | bytes 393224 | tf_op jit(solution)/shard_map/ppermute | solution.py:361
  85.7 2.9 %collective-permute-start.15 = (bf16[2,2,16,1024]{3,2,1,0:T(8,128)(2,1)S(1)}, bf16[2,2,16,1024]{3,2,1,0:T(8,128)(2,1)S(1)}, u32[]{:S(2)}, u32[]{:S(2)}) collective-permute-start(bf16[2,2,16,1024]{3,2,1,0:T(8,128)(2,1)S(1)} %collective-permute-done.13.rest_1_), channel_id=1, source_target_pairs={{0,2},{2,0},{1,3},{3,1},{4,6},{6,4},{5,7},{7,5},{8,10},{10,8},{9,1... | collective-permute-start | bytes 393224 | tf_op jit(solution)/shard_map/ppermute | solution.py:361

commit v3 on v2

--- a/solution.py
+++ b/solution.py
@@ -64,17 +64,16 @@
 
 def whiten_kernel(taps_ref, raw_hbm, basis_hbm, band_ref, inverse_ref, out_ref, raw_ref, basis_ref, wide, sems):
     raw_copies = []
-    for chunk in range(4):
-        columns = slice(chunk * 1024, (chunk + 1) * 1024)
+    for chunk in range(8):
+        columns = slice(chunk * 512, (chunk + 1) * 512)
         raw_copies.append(
             pltpu.make_async_copy(raw_hbm.at[:, columns], raw_ref.at[:, columns], sems.at[chunk])
         )
-    basis_copy = pltpu.make_async_copy(basis_hbm, basis_ref, sems.at[4])
-    raw_copies[0].start()
-    raw_copies[1].start()
-    basis_copy.start()
-    raw_copies[2].start()
-    raw_copies[3].start()
+    basis_copy = pltpu.make_async_copy(basis_hbm, basis_ref, sems.at[8])
+    for chunk, raw_copy in enumerate(raw_copies):
+        raw_copy.start()
+        if chunk == 3:
+            basis_copy.start()
 
     wide[...] = jnp.zeros((1, 512), jnp.float32)
     wide[:, :TAPS] = taps_ref[...].astype(jnp.float32)
@@ -85,26 +84,40 @@
         moved = pltpu.roll(taps, first_shift % 512, 1, stride=1, stride_axis=0)
         chunks.append(moved[:, :256].astype(jnp.bfloat16))
     fir = jnp.concatenate(chunks, axis=0)
+    fir_halves = fir[:256], fir[256:]
+    edge = jnp.zeros((256, 128), jnp.bfloat16)
     spectrum = jnp.zeros((256, 128), jnp.float32)
     arrived = 0
-    for tile in range(L // 256):
-        first, last = 256 * tile - 128, 256 * tile + 384
-        low, high = max(first, 0), min(last, L)
-        while arrived * 1024 < high:
+    for group in range(4):
+        tiles = range(group * 4, (group + 1) * 4)
+        while arrived < 8 and arrived * 512 < tiles[-1] * 256 + 384:
             raw_copies[arrived].wait()
             arrived += 1
-        if tile == 0:
+        filtered = jnp.zeros((256 * 4, 256), jnp.float32)
+        for half in range(2):
+            parts = []
+            for tile in tiles:
+                low = 256 * tile - 128 + 256 * half
+                if low < 0:
+                    parts.append(jnp.concatenate([edge, raw_ref[:, :128]], axis=1))
+                elif low + 256 > L:
+                    parts.append(jnp.concatenate([raw_ref[:, low:], edge], axis=1))
+                else:
+                    parts.append(raw_ref[:, low : low + 256])
+            filtered += jnp.dot(
+                jnp.concatenate(parts, axis=0),
+                fir_halves[half],
+                preferred_element_type=jnp.float32,
+            )
+        filtered = filtered.astype(jnp.bfloat16)
+        if group == 0:
             basis_copy.wait()
-        filtered = jnp.dot(
-            raw_ref[:, low:high],
-            fir[low - first : 512 - (last - high)],
-            preferred_element_type=jnp.float32,
-        ).astype(jnp.bfloat16)
-        spectrum += jnp.dot(
-            filtered,
-            basis_ref[256 * tile : 256 * (tile + 1), :],
-            preferred_element_type=jnp.float32,
-        )
+        for number, tile in enumerate(tiles):
+            spectrum += jnp.dot(
+                filtered[256 * number : 256 * (number + 1)],
+                basis_ref[256 * tile : 256 * (tile + 1), :],
+                preferred_element_type=jnp.float32,
+            )
     square = spectrum * spectrum
     magnitude = jnp.sqrt(square + swap_parts(square))
     amplitude = (
@@ -137,34 +150,42 @@
             pltpu.VMEM((256, L), jnp.bfloat16),
             pltpu.VMEM((L, 128), jnp.bfloat16),
             pltpu.VMEM((1, 512), jnp.float32),
-            pltpu.SemaphoreType.DMA((5,)),
+            pltpu.SemaphoreType.DMA((9,)),
         ],
         compiler_params=pltpu.CompilerParams(vmem_limit_bytes=56 * 1024 * 1024),
         name="whiten",
     )(taps, raw, jnp.asarray(dft_table()), jnp.asarray(band), jnp.asarray(inverse))
 
 
-def select_kernel(slot_ref, present_ref, rows_ref, out_ref):
-    entry = lax.broadcasted_iota(jnp.int32, (128, 256), 1)
-    selector = (slot_ref[...] == entry).astype(jnp.bfloat16)
-    chosen = jnp.dot(selector, rows_ref[...], preferred_element_type=jnp.float32)
-    chosen = chosen * present_ref[...].astype(jnp.float32)
+def select_kernel(slot_ref, rows_ref, out_ref):
+    slots = slot_ref[...]
+    entry = lax.broadcasted_iota(jnp.int32, (256, STD), 0)
+    stored = rows_ref[...]
+    chosen = []
+    for window in range(WDEV):
+        picked = jnp.where(entry == slots[window : window + 1, :], 1.0, 0.0).astype(jnp.bfloat16)
+        chosen.append(
+            lax.dot_general(
+                picked, stored, (((0,), (0,)), ((), ())), preferred_element_type=jnp.float32
+            )
+        )
     lane = lax.broadcasted_iota(jnp.int32, (STD, 128), 1) // 16
     for group in range(8):
         packed = jnp.zeros((STD, 128), jnp.float32)
         for window in range(WDEV):
-            rows = chosen[window * STD : (window + 1) * STD]
+            rows = chosen[window]
             moved = pltpu.roll(rows, (window - group) * 16 % 128, 1) if window != group else rows
             packed = jnp.where(lane == window, moved, packed)
         out_ref[:, group * 128 : (group + 1) * 128] = packed.astype(jnp.bfloat16)
 
 
-def select(slots, present, rows):
+def select(slots, rows):
     return pl.pallas_call(
         select_kernel,
         out_shape=jax.ShapeDtypeStruct((STD, 1024), jnp.bfloat16),
+        compiler_params=pltpu.CompilerParams(vmem_limit_bytes=4 * 1024 * 1024),
         name="select",
-    )(slots.reshape(-1, 1), present.reshape(-1, 1), rows)
+    )(slots, rows)
 
 
 cos_terms = (0.999999211, -19.7389804, 64.9286574, -85.2716215, 58.7904921, -21.0711056)
@@ -183,7 +204,8 @@
     return cosine, sine * turn
 
 
-def phase_kernel(place_ref, lag_ref, out_ref):
+def phase_kernel(place_ref, lag_ref, table_ref, out_ref, table_out_ref):
+    table_out_ref[...] = table_ref[...]
     x, core = place_ref[0], place_ref[1]
     lane = lax.broadcasted_iota(jnp.int32, (STD, 128), 1)
     bins = (lax.broadcasted_iota(jnp.int32, (8, 128), 0) + BIN0).astype(jnp.float32)
@@ -207,15 +229,29 @@
 def phases(place, lag):
     return pl.pallas_call(
         phase_kernel,
-        in_specs=[pl.BlockSpec(memory_space=pltpu.SMEM), pl.BlockSpec(memory_space=pltpu.VMEM)],
-        out_shape=jax.ShapeDtypeStruct((8, 288, 128), jnp.float32),
+        grid_spec=pltpu.PrefetchScalarGridSpec(
+            num_scalar_prefetch=1,
+            grid=(1,),
+            in_specs=[
+                pl.BlockSpec((STD, HALF), lambda step, place: (0, place[3])),
+                pl.BlockSpec((128, 128), lambda step, place: (0, 0)),
+            ],
+            out_specs=[
+                pl.BlockSpec((8, 288, 128), lambda step, place: (0, 0, 0)),
+                pl.BlockSpec((128, 128), lambda step, place: (0, 0)),
+            ],
+        ),
+        compiler_params=pltpu.CompilerParams(vmem_limit_bytes=8 * 1024 * 1024),
+        out_shape=[
+            jax.ShapeDtypeStruct((8, 288, 128), jnp.float32),
+            jax.ShapeDtypeStruct((128, 128), jnp.bfloat16),
+        ],
         cost_estimate=pl.CostEstimate(flops=1 << 20, bytes_accessed=1 << 16, transcendentals=0),
         name="phases",
-    )(place, lag)
-
-
-def weight_kernel(yhi_ref, mine_ref, other_ref, table_ref, out_ref):
-    out_ref[8, :128, :128] = table_ref[...]
+    )(place, lag, jnp.asarray(lag_table()))
+
+
+def weight_kernel(yhi_ref, mine_ref, other_ref, out_ref):
     mine_first = yhi_ref[0] == 0
     own_lane = lax.broadcasted_iota(jnp.int32, (8, 256), 1)
     same_bin = own_lane % 8 == lax.broadcasted_iota(jnp.int32, (8, 256), 0)
@@ -243,15 +279,15 @@
             pl.BlockSpec(memory_space=pltpu.SMEM),
             pl.BlockSpec(memory_space=pltpu.VMEM),
             pl.BlockSpec(memory_space=pltpu.VMEM),
-            pl.BlockSpec(memory_space=pltpu.VMEM),
         ],
-        out_shape=jax.ShapeDtypeStruct((9, 256, 256), jnp.bfloat16),
+        out_shape=jax.ShapeDtypeStruct((8, 256, 256), jnp.bfloat16),
+        compiler_params=pltpu.CompilerParams(vmem_limit_bytes=8 * 1024 * 1024),
         cost_estimate=pl.CostEstimate(flops=1 << 20, bytes_accessed=1 << 16, transcendentals=0),
         name="pair_weights",
-    )(yhi, mine, other, jnp.asarray(lag_table()))
-
-
-def correlate_kernel(layout, place_ref, weight_ref, turn_ref, *rest):
+    )(yhi, mine, other)
+
+
+def correlate_kernel(layout, place_ref, weight_ref, table_ref, turn_ref, *rest):
     count = sum(len(parts) for parts in layout)
     mine, theirs = rest[:count], rest[count : 2 * count]
     out_ref, cross = rest[-2:]
@@ -299,7 +335,7 @@
                 )
         rotated = jnp.concatenate(rotated, axis=0).astype(jnp.bfloat16)
         values = lax.dot_general(
-            rotated, weight_ref[8, :128, :128], (((0,), (0,)), ((), ())), preferred_element_type=jnp.float32
+            rotated, table_ref[...], (((0,), (0,)), ((), ())), preferred_element_type=jnp.float32
         )
         for ahead in range(4):
             for other in range(2):
@@ -310,7 +346,7 @@
                 ]
 
 
-def correlate(place, weights, turns, previous, hop, mine, theirs):
+def correlate(place, weights, table, turns, previous, hop, mine, theirs):
     cost = (1 << 31, 1 << 30, 1 << 28, 1 << 31, 1 << 30)[hop]
     layout, number = [], 0
     for parts in mine:
@@ -325,8 +361,8 @@
 
     whole = lambda shape: pl.BlockSpec(shape, lambda step, place: (0,) * len(shape))
     blocks = [part for parts in mine for part in parts] + [part for parts in theirs for part in parts]
-    operands = [place, weights, turns, *blocks]
-    in_specs = [whole((9, 256, 256))]
+    operands = [place, weights, table, turns, *blocks]
+    in_specs = [whole((8, 256, 256)), whole((128, 128))]
     in_specs += [pl.BlockSpec((1, 288, 128), lambda step, place: (z_at(step, place), 0, 0))]
     in_specs += [whole(block.shape) for block in blocks]
     aliases = {}
@@ -363,13 +399,15 @@
 
 def per_device(raw_traces, fir_taps, source_slot, present, lag_start):
     ylo, yhi = lax.axis_index("ylo"), lax.axis_index("yhi")
-    place = jnp.stack([lax.axis_index("x"), lax.axis_index("core"), lax.axis_index("z")])
-    lag = lax.dynamic_slice_in_dim(lag_start, yhi * HALF, HALF, 1)
+    place = jnp.stack([lax.axis_index(name) for name in ("x", "core", "z", "yhi")])
     white = whiten(fir_taps.reshape(1, TAPS), raw_traces[0])
-    white, lag = lax.optimization_barrier((white, lag))
+    white, lag = lax.optimization_barrier((white, lag_start))
     received = lax.all_to_all(white, STA, split_axis=0, concat_axis=0, tiled=True)
-    received, place, turns = lax.optimization_barrier((received, place, phases(place, lag)))
-    mine = select(source_slot, present, received)
+    slots = jnp.where(present != 0, source_slot, -1)
+    received, place, slots, turns, table = lax.optimization_barrier(
+        (received, place, slots, *phases(place, lag))
+    )
+    mine = select(slots, received)
 
     ring = lax.ppermute(mine, ("ylo", "yhi"), [(0, 2), (2, 3), (3, 1), (1, 0)])
     middle = lax.ppermute(mine, ("ylo", "yhi"), [(1, 2), (2, 1)])
@@ -397,7 +435,7 @@
         if hop in (1, 2):
             ready, out = lax.optimization_barrier((mine_here, out))
         theirs = [[across(part) for part in parts] for parts in ready]
-        out = correlate(place, weights, turns, out, hop, mine_here, theirs)
+        out = correlate(place, weights, table, turns, out, hop, mine_here, theirs)
     return out.reshape(STD, HALF, LAGW)
 
 

time: 91.4 us -> 84.6 us (0.926)
  local copies, waits for them, and re-layouts: 8.06 us -> 1.68 us
  Pallas kernels: 27.5 us -> 21.4 us
  starting transfers between devices: 44.1 us -> 48.4 us
  waiting for transfers between devices: 9.72 us -> 11.8 us
    ppermute x21, starting transfers between devices: 25 us -> 29.3 us  [shift(): lax.ppermute(value, axis, [(at, (at + by) % size) for at in range(size)])]
    unnamed x12 -> x4, local copies, waits for them, and re-layouts: 4.62 us -> 1.66 us
    reshape x2 -> x0, local copies, waits for them, and re-layouts: 2.79 us -> none  [the longest x1 1.4 us: select(): slots.reshape(-1, 1)]
    all_to_all x1, waiting for transfers between devices: 4.59 us -> 6.78 us  [per_device(): lax.all_to_all(white, STA, split_axis=0, concat_axis=0, tiled=True)]
    pallas_call x1, Pallas kernels: 2.03 us -> 0.23 us  [pair_weights(): pl.pallas_call(weight_kernel, in_specs=[pl.BlockSpec(memory_space=pltpu.S...]
    pallas_call x1, Pallas kernels: 1.84 us -> 0.37 us  [select(): pl.pallas_call(select_kernel, out_shape=jax.ShapeDtypeStruct((STD, 1024),...]
    pallas_call x1, Pallas kernels: 7.93 us -> 6.5 us  [whiten(): pl.pallas_call(whiten_kernel, out_shape=jax.ShapeDtypeStruct((256, 128),...]
    pallas_call x1, Pallas kernels: 2.65 us -> 1.32 us  [phases(): pl.pallas_call(phase_kernel, grid_spec=pltpu.PrefetchScalarGridSpec(num_s...]
  transfers between devices with their start and end apart: 24 -> 24, of which waited for: 4 -> 4; matrix products, arithmetic and copies ran while one was open for 4% -> 1% of each run, Pallas kernels for 17% -> 15%
where the time goes in v3:
time: 84.6 us; the launch traced here: 84.3 us
  starting transfers between devices  48.4 us (57%)
  Pallas kernels  21.4 us (25%)
  waiting for transfers between devices  11.8 us (14%)
  local copies, waits for them, and re-layouts  1.68 us (2%)
    ppermute x21, starting transfers between devices, shift(): lax.ppermute(value, axis, [(at, (at + by) % size) for at in range(size)])  29.3 us
    all_to_all x1, starting transfers between devices, per_device(): lax.all_to_all(white, STA, split_axis=0, concat_axis=0, tiled=True)  14.8 us
    pallas_call x5, Pallas kernels, correlate(): pl.pallas_call(functools.partial(correlate_kernel, layout), grid_spec=plt...  13 us
    all_to_all x1, waiting for transfers between devices, per_device(): lax.all_to_all(white, STA, split_axis=0, concat_axis=0, tiled=True)  6.78 us
    pallas_call x1, Pallas kernels, whiten(): pl.pallas_call(whiten_kernel, out_shape=jax.ShapeDtypeStruct((256, 128),...  6.5 us
    ppermute x1, starting transfers between devices, per_device(): ring = lax.ppermute(mine, ('ylo', 'yhi'), [(0, 2), (2, 3), (3, 1), (1, 0)])  3.62 us
    ppermute x21, waiting for transfers between devices, shift(): lax.ppermute(value, axis, [(at, (at + by) % size) for at in range(size)])  3.33 us
  transfers between devices with their start and end apart: 24, of which 4 were waited for; matrix products, arithmetic and copies ran while one was open for 1% of the time, Pallas kernels for 15%

profile of v3, /device:TPU:1, one launch (start us, length us, event | category | flops | bytes accessed | tf_op | source)
XLA Modules:
  0.0 84.3 jit_solution(17043840237572939387)
XLA Ops:
  0.0 6.5 %whiten.1 = bf16[256,128]{1,0:T(8,128)(2,1)} custom-call(bf16[1,127]{1,0:T(2,128)(2,1)} %bitcast.24, bf16[256,4096]{1,0:T(8,128)(2,1)} %bitcast.18, bf16[4096,128]{1,0:T(8,128)(2,1)} %constant.39.clone.basis_hbm, f32[128,128]{1,0:T(8,128)} %constant.40.clone.band_ref, f32[1,128]{1,0:T(1,128)} %constant.41.clone.inverse_ref), custom_call_target="tpu_custom_call" | custom-call | tf_op jit(solution)/shard_map/whiten/pallas_call | solution.py:139
  6.5 14.8 %all-to-all-start = ((bf16[128,2,128]{2,1,0:T(2,128)(2,1)}), bf16[128,2,128]{2,1,0:T(2,128)(2,1)S(1)}, u32[]{:S(2)}, u32[]{:S(2)}) async-start(bf16[128,2,128]{2,1,0:T(2,128)(2,1)} %bitcast.19), calls=%async_computation | async-start | bytes 131072 | tf_op jit(solution)/shard_map/all_to_all | solution.py:405
  21.4 0.9 %copy-done = s32[16,2048]{1,0:T(8,128)S(1)} copy-done((s32[16,2048]{1,0:T(8,128)S(1)}, s32[16,2048]{1,0:T(8,128)}, u32[]{:S(2)}) %copy-start) | copy-done | bytes 131096
  22.3 0.8 copy-done.1
  23.1 1.3 %phases.1 = (f32[8,288,128]{2,1,0:T(8,128)S(1)}, bf16[128,128]{1,0:T(8,128)(2,1)S(1)}) custom-call(s32[4]{0:T(128)S(1)} %pad_add_fusion.place_ref, s32[16,2048]{1,0:T(8,128)S(1)} %copy-done, bf16[128,128]{1,0:T(8,128)(2,1)S(1)} %copy-done.1), custom_call_target="tpu_custom_call" | custom-call | flops 1048576 | bytes 65536 | tf_op jit(solution)/shard_map/phases/pallas_call | solution.py:230
  24.4 0.7 compare_select_fusion.slot_ref
  25.1 6.8 %all-to-all-done = bf16[128,2,128]{2,1,0:T(2,128)(2,1)S(1)} async-done(((bf16[128,2,128]{2,1,0:T(2,128)(2,1)}), bf16[128,2,128]{2,1,0:T(2,128)(2,1)S(1)}, u32[]{:S(2)}, u32[]{:S(2)}) %all-to-all-start) | async-done | bytes 65568 | tf_op jit(solution)/shard_map/all_to_all | solution.py:405
  31.9 0.4 select.1.mine_ref
  32.3 0.7 collective-permute-start
  32.9 3.6 %collective-permute-start.1 = (bf16[16,1024]{1,0:T(8,128)(2,1)S(1)}, bf16[16,1024]{1,0:T(8,128)(2,1)S(1)}, u32[]{:S(2)}, u32[]{:S(2)}) collective-permute-start(bf16[16,1024]{1,0:T(8,128)(2,1)S(1)} %select.1.mine_ref), channel_id=1, source_target_pairs={{0,128},{128,129},{129,1},{1,0},{2,130},{130,131},{131,3},{3,2},{4... | collective-permute-start | bytes 98312 | tf_op jit(solution)/shard_map/ppermute | solution.py:412
  36.6 1.6 %collective-permute-done.1 = bf16[16,1024]{1,0:T(8,128)(2,1)S(1)} collective-permute-done((bf16[16,1024]{1,0:T(8,128)(2,1)S(1)}, bf16[16,1024]{1,0:T(8,128)(2,1)S(1)}, u32[]{:S(2)}, u32[]{:S(2)}) %collective-permute-start.1) | collective-permute-done | bytes 32800 | tf_op jit(solution)/shard_map/ppermute | solution.py:412
  38.2 0.9 %collective-permute-start.2 = (bf16[2,16,1024]{2,1,0:T(8,128)(2,1)S(1)}, bf16[2,16,1024]{2,1,0:T(8,128)(2,1)S(1)}, u32[]{:S(2)}, u32[]{:S(2)}) collective-permute-start(bf16[2,16,1024]{2,1,0:T(8,128)(2,1)S(1)} %pad_maximum_fusion.1), channel_id=1, source_target_pairs={{0,96},{32,0},{64,32},{96,64},{1,97},{33,1},{65,33},{97,65},{2,98}... | collective-permute-start | bytes 196616 | tf_op jit(solution)/shard_map/ppermute | solution.py:397
  39.1 1.4 %collective-permute-start.3 = (bf16[2,16,1024]{2,1,0:T(8,128)(2,1)S(1)}, bf16[2,16,1024]{2,1,0:T(8,128)(2,1)S(1)}, u32[]{:S(2)}, u32[]{:S(2)}) collective-permute-start(bf16[2,16,1024]{2,1,0:T(8,128)(2,1)S(1)} %pad_maximum_fusion.1), channel_id=1, source_target_pairs={{0,64},{32,96},{64,0},{96,32},{1,65},{33,97},{65,1},{97,33},{2,66}... | collective-permute-start | bytes 196616 | tf_op jit(solution)/shard_map/ppermute | solution.py:397
  40.5 1.5 %collective-permute-start.5 = (bf16[16,1024]{1,0:T(8,128)(2,1)S(1)}, bf16[16,1024]{1,0:T(8,128)(2,1)S(1)}, u32[]{:S(2)}, u32[]{:S(2)}) collective-permute-start(bf16[16,1024]{1,0:T(8,128)(2,1)S(1)} %select.1.mine_ref), channel_id=1, source_target_pairs={{0,1},{1,0},{2,3},{3,2},{4,5},{5,4},{6,7},{7,6},{8,9},{9,8},{10,11... | collective-permute-start | bytes 98312 | tf_op jit(solution)/shard_map/ppermute | solution.py:397
  41.9 2.8 %collective-permute-done.5.other_ref = bf16[16,1024]{1,0:T(8,128)(2,1)S(1)} collective-permute-done((bf16[16,1024]{1,0:T(8,128)(2,1)S(1)}, bf16[16,1024]{1,0:T(8,128)(2,1)S(1)}, u32[]{:S(2)}, u32[]{:S(2)}) %collective-permute-start.5) | collective-permute-done | bytes 32800 | tf_op jit(solution)/shard_map/ppermute | solution.py:397
  44.8 0.5 collective-permute-start.10
  45.3 1.1 %collective-permute-start.6 = (bf16[4,2,16,1024]{3,2,1,0:T(8,128)(2,1)S(1)}, bf16[4,2,16,1024]{3,2,1,0:T(8,128)(2,1)S(1)}, u32[]{:S(2)}, u32[]{:S(2)}) collective-permute-start(bf16[4,2,16,1024]{3,2,1,0:T(8,128)(2,1)S(1)} %pad_maximum_fusion.rest_0_), channel_id=1, source_target_pairs={{0,4},{4,8},{8,12},{12,16},{16,20},{20,24},{24,28},{28,0},{1,5},{5... | collective-permute-start | bytes 786440 | tf_op jit(solution)/shard_map/ppermute | solution.py:397
  46.4 3.9 %collective-permute-start.18 = (bf16[4,2,16,1024]{3,2,1,0:T(8,128)(2,1)S(1)}, bf16[4,2,16,1024]{3,2,1,0:T(8,128)(2,1)S(1)}, u32[]{:S(2)}, u32[]{:S(2)}) collective-permute-start(bf16[4,2,16,1024]{3,2,1,0:T(8,128)(2,1)S(1)} %pad_maximum_fusion.rest_0_), channel_id=1, source_target_pairs={{0,2},{2,0},{1,3},{3,1},{4,6},{6,4},{5,7},{7,5},{8,10},{10,8},{9,1... | collective-permute-start | bytes 786440 | tf_op jit(solution)/shard_map/ppermute | solution.py:397
  50.5 1.8 %collective-permute-start.11 = (bf16[4,2,16,1024]{3,2,1,0:T(8,128)(2,1)S(1)}, bf16[4,2,16,1024]{3,2,1,0:T(8,128)(2,1)S(1)}, u32[]{:S(2)}, u32[]{:S(2)}) collective-permute-start(bf16[4,2,16,1024]{3,2,1,0:T(8,128)(2,1)S(1)} %collective-permute-done.10.rest_1_), channel_id=1, source_target_pairs={{0,28},{4,0},{8,4},{12,8},{16,12},{20,16},{24,20},{28,24},{1,29},{... | collective-permute-start | bytes 786440 | tf_op jit(solution)/shard_map/ppermute | solution.py:397
  52.4 2.2 %correlate.5.rest_4_ = f32[16,4,8,32,128]{4,3,2,1,0:T(8,128)} custom-call(s32[4]{0:T(128)S(1)} %pad_add_fusion.place_ref, bf16[8,256,256]{2,1,0:T(8,128)(2,1)S(1)} %pair_weights.1.weight_ref, bf16[128,128]{1,0:T(8,128)(2,1)S(1)} %get-tuple-element.37.table_ref, f32[8,288,128]{2,1,0:T(8,128)S(1)} %get-tuple-element.38.turn_ref, ...), custom_call_target="tpu_custom_call" | custom-call | flops 2147483648 | bytes 65536 | tf_op jit(solution)/shard_map/correlate/pallas_call | solution.py:373
  54.6 5.1 %collective-permute-start.19 = (bf16[4,2,16,1024]{3,2,1,0:T(8,128)(2,1)S(1)}, bf16[4,2,16,1024]{3,2,1,0:T(8,128)(2,1)S(1)}, u32[]{:S(2)}, u32[]{:S(2)}) collective-permute-start(bf16[4,2,16,1024]{3,2,1,0:T(8,128)(2,1)S(1)} %collective-permute-done.6.rest_0_), channel_id=1, source_target_pairs={{0,2},{2,0},{1,3},{3,1},{4,6},{6,4},{5,7},{7,5},{8,10},{10,8},{9,1... | collective-permute-start | bytes 786440 | tf_op jit(solution)/shard_map/ppermute | solution.py:397
  59.7 0.5 collective-permute-start.8
  60.2 2.2 %collective-permute-start.12 = (bf16[4,2,16,1024]{3,2,1,0:T(8,128)(2,1)S(1)}, bf16[4,2,16,1024]{3,2,1,0:T(8,128)(2,1)S(1)}, u32[]{:S(2)}, u32[]{:S(2)}) collective-permute-start(bf16[4,2,16,1024]{3,2,1,0:T(8,128)(2,1)S(1)} %collective-permute-done.11.rest_1_), channel_id=1, source_target_pairs={{0,28},{4,0},{8,4},{12,8},{16,12},{20,16},{24,20},{28,24},{1,29},{... | collective-permute-start | bytes 786440 | tf_op jit(solution)/shard_map/ppermute | solution.py:397
  62.4 2.9 %correlate.6.rest_4_ = f32[16,4,8,32,128]{4,3,2,1,0:T(8,128)} custom-call(s32[4]{0:T(128)S(1)} %pad_add_fusion.place_ref, bf16[8,256,256]{2,1,0:T(8,128)(2,1)S(1)} %pair_weights.1.weight_ref, bf16[128,128]{1,0:T(8,128)(2,1)S(1)} %get-tuple-element.37.table_ref, f32[8,288,128]{2,1,0:T(8,128)S(1)} %get-tuple-element.38.turn_ref, ...), custom_call_target="tpu_custom_call", output_to_operand_aliasing={{}: (8, {})} | custom-call | flops 1073741824 | bytes 65536 | tf_op jit(solution)/shard_map/correlate/pallas_call | solution.py:373
  65.2 4.9 %collective-permute-start.21 = (bf16[4,2,16,1024]{3,2,1,0:T(8,128)(2,1)S(1)}, bf16[4,2,16,1024]{3,2,1,0:T(8,128)(2,1)S(1)}, u32[]{:S(2)}, u32[]{:S(2)}) collective-permute-start(bf16[4,2,16,1024]{3,2,1,0:T(8,128)(2,1)S(1)} %collective-permute-done.7.rest_0_), channel_id=1, source_target_pairs={{0,2},{2,0},{1,3},{3,1},{4,6},{6,4},{5,7},{7,5},{8,10},{10,8},{9,1... | collective-permute-start | bytes 786440 | tf_op jit(solution)/shard_map/ppermute | solution.py:397
  70.2 1.5 %collective-permute-start.16 = (bf16[4,2,16,1024]{3,2,1,0:T(8,128)(2,1)S(1)}, bf16[4,2,16,1024]{3,2,1,0:T(8,128)(2,1)S(1)}, u32[]{:S(2)}, u32[]{:S(2)}) collective-permute-start(bf16[4,2,16,1024]{3,2,1,0:T(8,128)(2,1)S(1)} %collective-permute-done.8.rest_0_), channel_id=1, source_target_pairs={{0,2},{2,0},{1,3},{3,1},{4,6},{6,4},{5,7},{7,5},{8,10},{10,8},{9,1... | collective-permute-start | bytes 786440 | tf_op jit(solution)/shard_map/ppermute | solution.py:397
  71.8 3.0 %collective-permute-start.13 = (bf16[2,2,16,1024]{3,2,1,0:T(8,128)(2,1)S(1)}, bf16[2,2,16,1024]{3,2,1,0:T(8,128)(2,1)S(1)}, u32[]{:S(2)}, u32[]{:S(2)}) collective-permute-start(bf16[2,2,16,1024]{3,2,1,0:T(8,128)(2,1)S(1)} %slice.9), channel_id=1, source_target_pairs={{0,28},{4,0},{8,4},{12,8},{16,12},{20,16},{24,20},{28,24},{1,29},{... | collective-permute-start | bytes 393224 | tf_op jit(solution)/shard_map/ppermute | solution.py:397
  74.8 2.9 %correlate.7.rest_4_ = f32[16,4,8,32,128]{4,3,2,1,0:T(8,128)} custom-call(s32[4]{0:T(128)S(1)} %pad_add_fusion.place_ref, bf16[8,256,256]{2,1,0:T(8,128)(2,1)S(1)} %pair_weights.1.weight_ref, bf16[128,128]{1,0:T(8,128)(2,1)S(1)} %get-tuple-element.37.table_ref, f32[8,288,128]{2,1,0:T(8,128)S(1)} %get-tuple-element.38.turn_ref, ...), custom_call_target="tpu_custom_call", output_to_operand_aliasing={{}: (8, {})} | custom-call | flops 268435456 | bytes 65536 | tf_op jit(solution)/shard_map/correlate/pallas_call | solution.py:373
  77.7 0.4 collective-permute-done.9.rest_0_
  78.1 1.0 %collective-permute-start.14 = (bf16[2,2,16,1024]{3,2,1,0:T(8,128)(2,1)S(1)}, bf16[2,2,16,1024]{3,2,1,0:T(8,128)(2,1)S(1)}, u32[]{:S(2)}, u32[]{:S(2)}) collective-permute-start(bf16[2,2,16,1024]{3,2,1,0:T(8,128)(2,1)S(1)} %collective-permute-done.9.rest_0_), channel_id=1, source_target_pairs={{0,2},{2,0},{1,3},{3,1},{4,6},{6,4},{5,7},{7,5},{8,10},{10,8},{9,1... | collective-permute-start | bytes 393224 | tf_op jit(solution)/shard_map/ppermute | solution.py:397
  79.2 2.9 %correlate.8.rest_4_ = f32[16,4,8,32,128]{4,3,2,1,0:T(8,128)} custom-call(s32[4]{0:T(128)S(1)} %pad_add_fusion.place_ref, bf16[8,256,256]{2,1,0:T(8,128)(2,1)S(1)} %pair_weights.1.weight_ref, bf16[128,128]{1,0:T(8,128)(2,1)S(1)} %get-tuple-element.37.table_ref, f32[8,288,128]{2,1,0:T(8,128)S(1)} %get-tuple-element.38.turn_ref, ...), custom_call_target="tpu_custom_call", output_to_operand_aliasing={{}: (8, {})} | custom-call | flops 2147483648 | bytes 65536 | tf_op jit(solution)/shard_map/correlate/pallas_call | solution.py:373
  82.0 2.2 %correlate.9 = f32[16,4,8,32,128]{4,3,2,1,0:T(8,128)} custom-call(s32[4]{0:T(128)S(1)} %pad_add_fusion.place_ref, bf16[8,256,256]{2,1,0:T(8,128)(2,1)S(1)} %pair_weights.1.weight_ref, bf16[128,128]{1,0:T(8,128)(2,1)S(1)} %get-tuple-element.37.table_ref, f32[8,288,128]{2,1,0:T(8,128)S(1)} %get-tuple-element.38.turn_ref, ...), custom_call_target="tpu_custom_call", output_to_operand_aliasing={{}: (8, {})} | custom-call | flops 1073741824 | bytes 65536 | tf_op jit(solution)/shard_map/correlate/pallas_call | solution.py:373
  (36 shorter events, 0.6 us)
Async XLA Ops:
  6.5 25.4 %all-to-all-start = ((bf16[128,2,128]{2,1,0:T(2,128)(2,1)}), bf16[128,2,128]{2,1,0:T(2,128)(2,1)S(1)}, u32[]{:S(2)}, u32[]{:S(2)}) async-start(bf16[128,2,128]{2,1,0:T(2,128)(2,1)} %bitcast.19), calls=%async_computation | async-start | bytes 131072 | tf_op jit(solution)/shard_map/all_to_all | solution.py:405
  21.4 0.9 %copy-start = (s32[16,2048]{1,0:T(8,128)S(1)}, s32[16,2048]{1,0:T(8,128)}, u32[]{:S(2)}) copy-start(s32[16,2048]{1,0:T(8,128)} %lag_ref) | copy-start | bytes 393220
  22.3 0.8 copy-start.1
  32.3 4.3 %collective-permute-start = (bf16[16,1024]{1,0:T(8,128)(2,1)S(1)}, bf16[16,1024]{1,0:T(8,128)(2,1)S(1)}, u32[]{:S(2)}, u32[]{:S(2)}) collective-permute-start(bf16[16,1024]{1,0:T(8,128)(2,1)S(1)} %select.1.mine_ref), channel_id=1, source_target_pairs={{1,128},{128,1},{3,130},{130,3},{5,132},{132,5},{7,134},{134,7},{9... | collective-permute-start | bytes 98312 | tf_op jit(solution)/shard_map/ppermute | solution.py:413
  32.9 5.3 %collective-permute-start.1 = (bf16[16,1024]{1,0:T(8,128)(2,1)S(1)}, bf16[16,1024]{1,0:T(8,128)(2,1)S(1)}, u32[]{:S(2)}, u32[]{:S(2)}) collective-permute-start(bf16[16,1024]{1,0:T(8,128)(2,1)S(1)} %select.1.mine_ref), channel_id=1, source_target_pairs={{0,128},{128,129},{129,1},{1,0},{2,130},{130,131},{131,3},{3,2},{4... | collective-permute-start | bytes 98312 | tf_op jit(solution)/shard_map/ppermute | solution.py:412
  38.2 6.5 %collective-permute-start.2 = (bf16[2,16,1024]{2,1,0:T(8,128)(2,1)S(1)}, bf16[2,16,1024]{2,1,0:T(8,128)(2,1)S(1)}, u32[]{:S(2)}, u32[]{:S(2)}) collective-permute-start(bf16[2,16,1024]{2,1,0:T(8,128)(2,1)S(1)} %pad_maximum_fusion.1), channel_id=1, source_target_pairs={{0,96},{32,0},{64,32},{96,64},{1,97},{33,1},{65,33},{97,65},{2,98}... | collective-permute-start | bytes 196616 | tf_op jit(solution)/shard_map/ppermute | solution.py:397
  39.1 5.6 %collective-permute-start.3 = (bf16[2,16,1024]{2,1,0:T(8,128)(2,1)S(1)}, bf16[2,16,1024]{2,1,0:T(8,128)(2,1)S(1)}, u32[]{:S(2)}, u32[]{:S(2)}) collective-permute-start(bf16[2,16,1024]{2,1,0:T(8,128)(2,1)S(1)} %pad_maximum_fusion.1), channel_id=1, source_target_pairs={{0,64},{32,96},{64,0},{96,32},{1,65},{33,97},{65,1},{97,33},{2,66}... | collective-permute-start | bytes 196616 | tf_op jit(solution)/shard_map/ppermute | solution.py:397
  40.5 4.3 %collective-permute-start.4 = (bf16[2,16,1024]{2,1,0:T(8,128)(2,1)S(1)}, bf16[2,16,1024]{2,1,0:T(8,128)(2,1)S(1)}, u32[]{:S(2)}, u32[]{:S(2)}) collective-permute-start(bf16[2,16,1024]{2,1,0:T(8,128)(2,1)S(1)} %pad_maximum_fusion.1), channel_id=1, source_target_pairs={{0,32},{32,64},{64,96},{96,0},{1,33},{33,65},{65,97},{97,1},{2,34}... | collective-permute-start | bytes 196616 | tf_op jit(solution)/shard_map/ppermute | solution.py:397
  40.5 4.3 %collective-permute-start.5 = (bf16[16,1024]{1,0:T(8,128)(2,1)S(1)}, bf16[16,1024]{1,0:T(8,128)(2,1)S(1)}, u32[]{:S(2)}, u32[]{:S(2)}) collective-permute-start(bf16[16,1024]{1,0:T(8,128)(2,1)S(1)} %select.1.mine_ref), channel_id=1, source_target_pairs={{0,1},{1,0},{2,3},{3,2},{4,5},{5,4},{6,7},{7,6},{8,9},{9,8},{10,11... | collective-permute-start | bytes 98312 | tf_op jit(solution)/shard_map/ppermute | solution.py:397
  44.8 5.6 %collective-permute-start.10 = (bf16[4,2,16,1024]{3,2,1,0:T(8,128)(2,1)S(1)}, bf16[4,2,16,1024]{3,2,1,0:T(8,128)(2,1)S(1)}, u32[]{:S(2)}, u32[]{:S(2)}) collective-permute-start(bf16[4,2,16,1024]{3,2,1,0:T(8,128)(2,1)S(1)} %pad_maximum_fusion.rest_0_), channel_id=1, source_target_pairs={{0,28},{4,0},{8,4},{12,8},{16,12},{20,16},{24,20},{28,24},{1,29},{... | collective-permute-start | bytes 786440 | tf_op jit(solution)/shard_map/ppermute | solution.py:397
  45.3 7.0 %collective-permute-start.6 = (bf16[4,2,16,1024]{3,2,1,0:T(8,128)(2,1)S(1)}, bf16[4,2,16,1024]{3,2,1,0:T(8,128)(2,1)S(1)}, u32[]{:S(2)}, u32[]{:S(2)}) collective-permute-start(bf16[4,2,16,1024]{3,2,1,0:T(8,128)(2,1)S(1)} %pad_maximum_fusion.rest_0_), channel_id=1, source_target_pairs={{0,4},{4,8},{8,12},{12,16},{16,20},{20,24},{24,28},{28,0},{1,5},{5... | collective-permute-start | bytes 786440 | tf_op jit(solution)/shard_map/ppermute | solution.py:397
  46.4 6.0 %collective-permute-start.18 = (bf16[4,2,16,1024]{3,2,1,0:T(8,128)(2,1)S(1)}, bf16[4,2,16,1024]{3,2,1,0:T(8,128)(2,1)S(1)}, u32[]{:S(2)}, u32[]{:S(2)}) collective-permute-start(bf16[4,2,16,1024]{3,2,1,0:T(8,128)(2,1)S(1)} %pad_maximum_fusion.rest_0_), channel_id=1, source_target_pairs={{0,2},{2,0},{1,3},{3,1},{4,6},{6,4},{5,7},{7,5},{8,10},{10,8},{9,1... | collective-permute-start | bytes 786440 | tf_op jit(solution)/shard_map/ppermute | solution.py:397
  50.5 9.7 %collective-permute-start.11 = (bf16[4,2,16,1024]{3,2,1,0:T(8,128)(2,1)S(1)}, bf16[4,2,16,1024]{3,2,1,0:T(8,128)(2,1)S(1)}, u32[]{:S(2)}, u32[]{:S(2)}) collective-permute-start(bf16[4,2,16,1024]{3,2,1,0:T(8,128)(2,1)S(1)} %collective-permute-done.10.rest_1_), channel_id=1, source_target_pairs={{0,28},{4,0},{8,4},{12,8},{16,12},{20,16},{24,20},{28,24},{1,29},{... | collective-permute-start | bytes 786440 | tf_op jit(solution)/shard_map/ppermute | solution.py:397
  52.3 7.3 %collective-permute-start.7 = (bf16[4,2,16,1024]{3,2,1,0:T(8,128)(2,1)S(1)}, bf16[4,2,16,1024]{3,2,1,0:T(8,128)(2,1)S(1)}, u32[]{:S(2)}, u32[]{:S(2)}) collective-permute-start(bf16[4,2,16,1024]{3,2,1,0:T(8,128)(2,1)S(1)} %collective-permute-done.6.rest_0_), channel_id=1, source_target_pairs={{0,4},{4,8},{8,12},{12,16},{16,20},{20,24},{24,28},{28,0},{1,5},{5... | collective-permute-start | bytes 786440 | tf_op jit(solution)/shard_map/ppermute | solution.py:397
  54.6 7.8 %collective-permute-start.19 = (bf16[4,2,16,1024]{3,2,1,0:T(8,128)(2,1)S(1)}, bf16[4,2,16,1024]{3,2,1,0:T(8,128)(2,1)S(1)}, u32[]{:S(2)}, u32[]{:S(2)}) collective-permute-start(bf16[4,2,16,1024]{3,2,1,0:T(8,128)(2,1)S(1)} %collective-permute-done.6.rest_0_), channel_id=1, source_target_pairs={{0,2},{2,0},{1,3},{3,1},{4,6},{6,4},{5,7},{7,5},{8,10},{10,8},{9,1... | collective-permute-start | bytes 786440 | tf_op jit(solution)/shard_map/ppermute | solution.py:397
  59.7 2.7 %collective-permute-start.20 = (bf16[4,2,16,1024]{3,2,1,0:T(8,128)(2,1)S(1)}, bf16[4,2,16,1024]{3,2,1,0:T(8,128)(2,1)S(1)}, u32[]{:S(2)}, u32[]{:S(2)}) collective-permute-start(bf16[4,2,16,1024]{3,2,1,0:T(8,128)(2,1)S(1)} %collective-permute-done.10.rest_1_), channel_id=1, source_target_pairs={{0,2},{2,0},{1,3},{3,1},{4,6},{6,4},{5,7},{7,5},{8,10},{10,8},{9,1... | collective-permute-start | bytes 786440 | tf_op jit(solution)/shard_map/ppermute | solution.py:397
  59.7 10.5 %collective-permute-start.8 = (bf16[4,2,16,1024]{3,2,1,0:T(8,128)(2,1)S(1)}, bf16[4,2,16,1024]{3,2,1,0:T(8,128)(2,1)S(1)}, u32[]{:S(2)}, u32[]{:S(2)}) collective-permute-start(bf16[4,2,16,1024]{3,2,1,0:T(8,128)(2,1)S(1)} %collective-permute-done.7.rest_0_), channel_id=1, source_target_pairs={{0,4},{4,8},{8,12},{12,16},{16,20},{20,24},{24,28},{28,0},{1,5},{5... | collective-permute-start | bytes 786440 | tf_op jit(solution)/shard_map/ppermute | solution.py:397
  60.2 11.4 %collective-permute-start.12 = (bf16[4,2,16,1024]{3,2,1,0:T(8,128)(2,1)S(1)}, bf16[4,2,16,1024]{3,2,1,0:T(8,128)(2,1)S(1)}, u32[]{:S(2)}, u32[]{:S(2)}) collective-permute-start(bf16[4,2,16,1024]{3,2,1,0:T(8,128)(2,1)S(1)} %collective-permute-done.11.rest_1_), channel_id=1, source_target_pairs={{0,28},{4,0},{8,4},{12,8},{16,12},{20,16},{24,20},{28,24},{1,29},{... | collective-permute-start | bytes 786440 | tf_op jit(solution)/shard_map/ppermute | solution.py:397
  65.2 6.5 %collective-permute-start.21 = (bf16[4,2,16,1024]{3,2,1,0:T(8,128)(2,1)S(1)}, bf16[4,2,16,1024]{3,2,1,0:T(8,128)(2,1)S(1)}, u32[]{:S(2)}, u32[]{:S(2)}) collective-permute-start(bf16[4,2,16,1024]{3,2,1,0:T(8,128)(2,1)S(1)} %collective-permute-done.7.rest_0_), channel_id=1, source_target_pairs={{0,2},{2,0},{1,3},{3,1},{4,6},{6,4},{5,7},{7,5},{8,10},{10,8},{9,1... | collective-permute-start | bytes 786440 | tf_op jit(solution)/shard_map/ppermute | solution.py:397
  70.2 4.7 %collective-permute-start.22 = (bf16[4,2,16,1024]{3,2,1,0:T(8,128)(2,1)S(1)}, bf16[4,2,16,1024]{3,2,1,0:T(8,128)(2,1)S(1)}, u32[]{:S(2)}, u32[]{:S(2)}) collective-permute-start(bf16[4,2,16,1024]{3,2,1,0:T(8,128)(2,1)S(1)} %collective-permute-done.11.rest_1_), channel_id=1, source_target_pairs={{0,2},{2,0},{1,3},{3,1},{4,6},{6,4},{5,7},{7,5},{8,10},{10,8},{9,1... | collective-permute-start | bytes 786440 | tf_op jit(solution)/shard_map/ppermute | solution.py:397
  70.2 9.0 %collective-permute-start.16 = (bf16[4,2,16,1024]{3,2,1,0:T(8,128)(2,1)S(1)}, bf16[4,2,16,1024]{3,2,1,0:T(8,128)(2,1)S(1)}, u32[]{:S(2)}, u32[]{:S(2)}) collective-permute-start(bf16[4,2,16,1024]{3,2,1,0:T(8,128)(2,1)S(1)} %collective-permute-done.8.rest_0_), channel_id=1, source_target_pairs={{0,2},{2,0},{1,3},{3,1},{4,6},{6,4},{5,7},{7,5},{8,10},{10,8},{9,1... | collective-permute-start | bytes 786440 | tf_op jit(solution)/shard_map/ppermute | solution.py:397
  71.6 7.5 %collective-permute-start.17 = (bf16[4,2,16,1024]{3,2,1,0:T(8,128)(2,1)S(1)}, bf16[4,2,16,1024]{3,2,1,0:T(8,128)(2,1)S(1)}, u32[]{:S(2)}, u32[]{:S(2)}) collective-permute-start(bf16[4,2,16,1024]{3,2,1,0:T(8,128)(2,1)S(1)} %collective-permute-done.12.rest_1_), channel_id=1, source_target_pairs={{0,2},{2,0},{1,3},{3,1},{4,6},{6,4},{5,7},{7,5},{8,10},{10,8},{9,1... | collective-permute-start | bytes 786440 | tf_op jit(solution)/shard_map/ppermute | solution.py:397
  71.7 6.4 %collective-permute-start.9 = (bf16[2,2,16,1024]{3,2,1,0:T(8,128)(2,1)S(1)}, bf16[2,2,16,1024]{3,2,1,0:T(8,128)(2,1)S(1)}, u32[]{:S(2)}, u32[]{:S(2)}) collective-permute-start(bf16[2,2,16,1024]{3,2,1,0:T(8,128)(2,1)S(1)} %slice.8), channel_id=1, source_target_pairs={{0,4},{4,8},{8,12},{12,16},{16,20},{20,24},{24,28},{28,0},{1,5},{5... | collective-permute-start | bytes 393224 | tf_op jit(solution)/shard_map/ppermute | solution.py:397
  71.8 7.4 %collective-permute-start.13 = (bf16[2,2,16,1024]{3,2,1,0:T(8,128)(2,1)S(1)}, bf16[2,2,16,1024]{3,2,1,0:T(8,128)(2,1)S(1)}, u32[]{:S(2)}, u32[]{:S(2)}) collective-permute-start(bf16[2,2,16,1024]{3,2,1,0:T(8,128)(2,1)S(1)} %slice.9), channel_id=1, source_target_pairs={{0,28},{4,0},{8,4},{12,8},{16,12},{20,16},{24,20},{28,24},{1,29},{... | collective-permute-start | bytes 393224 | tf_op jit(solution)/shard_map/ppermute | solution.py:397
  78.1 3.9 %collective-permute-start.14 = (bf16[2,2,16,1024]{3,2,1,0:T(8,128)(2,1)S(1)}, bf16[2,2,16,1024]{3,2,1,0:T(8,128)(2,1)S(1)}, u32[]{:S(2)}, u32[]{:S(2)}) collective-permute-start(bf16[2,2,16,1024]{3,2,1,0:T(8,128)(2,1)S(1)} %collective-permute-done.9.rest_0_), channel_id=1, source_target_pairs={{0,2},{2,0},{1,3},{3,1},{4,6},{6,4},{5,7},{7,5},{8,10},{10,8},{9,1... | collective-permute-start | bytes 393224 | tf_op jit(solution)/shard_map/ppermute | solution.py:397
  79.2 2.9 %collective-permute-start.15 = (bf16[2,2,16,1024]{3,2,1,0:T(8,128)(2,1)S(1)}, bf16[2,2,16,1024]{3,2,1,0:T(8,128)(2,1)S(1)}, u32[]{:S(2)}, u32[]{:S(2)}) collective-permute-start(bf16[2,2,16,1024]{3,2,1,0:T(8,128)(2,1)S(1)} %collective-permute-done.13.rest_1_), channel_id=1, source_target_pairs={{0,2},{2,0},{1,3},{3,1},{4,6},{6,4},{5,7},{7,5},{8,10},{10,8},{9,1... | collective-permute-start | bytes 393224 | tf_op jit(solution)/shard_map/ppermute | solution.py:397

commit v4 on v3

--- a/solution.py
+++ b/solution.py
@@ -401,12 +401,9 @@
     ylo, yhi = lax.axis_index("ylo"), lax.axis_index("yhi")
     place = jnp.stack([lax.axis_index(name) for name in ("x", "core", "z", "yhi")])
     white = whiten(fir_taps.reshape(1, TAPS), raw_traces[0])
-    white, lag = lax.optimization_barrier((white, lag_start))
     received = lax.all_to_all(white, STA, split_axis=0, concat_axis=0, tiled=True)
     slots = jnp.where(present != 0, source_slot, -1)
-    received, place, slots, turns, table = lax.optimization_barrier(
-        (received, place, slots, *phases(place, lag))
-    )
+    received, slots = lax.optimization_barrier((received, slots))
     mine = select(slots, received)
 
     ring = lax.ppermute(mine, ("ylo", "yhi"), [(0, 2), (2, 3), (3, 1), (1, 0)])
@@ -419,7 +416,8 @@
     other = shift(mine, "yhi", 2, 1)
     blocks = [block] + [shift(block, "x", 4, -by) for by in (1, 2, 3)]
     blocks, other = lax.optimization_barrier((blocks, other))
-    line = jnp.stack(blocks)
+    line, place, lag_start = lax.optimization_barrier((jnp.stack(blocks), place, lag_start))
+    turns, table = phases(place, lag_start)
     weights = pair_weights(yhi.reshape(1), mine, other)
 
     across = lambda value: shift(value, "core", 2, 1)

time: 84.6 us -> 85.8 us (1.014)
  waiting for transfers between devices: 11.8 us -> 18.8 us
  starting transfers between devices: 48.4 us -> 42.6 us
    ppermute x21, starting transfers between devices: 29.3 us -> 23.5 us  [shift(): lax.ppermute(value, axis, [(at, (at + by) % size) for at in range(size)])]
    ppermute x21, waiting for transfers between devices: 3.33 us -> 7.27 us  [shift(): lax.ppermute(value, axis, [(at, (at + by) % size) for at in range(size)])]
    all_to_all x1, waiting for transfers between devices: 6.78 us -> 9.86 us  [per_device(): lax.all_to_all(white, STA, split_axis=0, concat_axis=0, tiled=True)]
  transfers between devices with their start and end apart: 24 -> 24, of which waited for: 4 -> 5; matrix products, arithmetic and copies ran while one was open for 1% -> 1% of each run, Pallas kernels for 15% -> 14%
where the time goes in v4:
time: 85.8 us; the launch traced here: 85.5 us
  starting transfers between devices  42.6 us (50%)
  Pallas kernels  21.5 us (25%)
  waiting for transfers between devices  18.8 us (22%)
  local copies, waits for them, and re-layouts  1.68 us (2%)
    ppermute x21, starting transfers between devices, shift(): lax.ppermute(value, axis, [(at, (at + by) % size) for at in range(size)])  23.5 us
    all_to_all x1, starting transfers between devices, per_device(): lax.all_to_all(white, STA, split_axis=0, concat_axis=0, tiled=True)  14.8 us
    pallas_call x5, Pallas kernels, correlate(): pl.pallas_call(functools.partial(correlate_kernel, layout), grid_spec=plt...  13.1 us
    all_to_all x1, waiting for transfers between devices, per_device(): lax.all_to_all(white, STA, split_axis=0, concat_axis=0, tiled=True)  9.86 us
    ppermute x21, waiting for transfers between devices, shift(): lax.ppermute(value, axis, [(at, (at + by) % size) for at in range(size)])  7.27 us
    pallas_call x1, Pallas kernels, whiten(): pl.pallas_call(whiten_kernel, out_shape=jax.ShapeDtypeStruct((256, 128),...  6.5 us
    ppermute x1, starting transfers between devices, per_device(): ring = lax.ppermute(mine, ('ylo', 'yhi'), [(0, 2), (2, 3), (3, 1), (1, 0)])  3.62 us
  transfers between devices with their start and end apart: 24, of which 5 were waited for; matrix products, arithmetic and copies ran while one was open for 1% of the time, Pallas kernels for 14%

profile of v4, /device:TPU:1, one launch (start us, length us, event | category | flops | bytes accessed | tf_op | source)
XLA Modules:
  0.0 85.5 jit_solution(4141250016596838217)
XLA Ops:
  0.0 6.5 %whiten.1 = bf16[256,128]{1,0:T(8,128)(2,1)} custom-call(bf16[1,127]{1,0:T(2,128)(2,1)} %bitcast.24, bf16[256,4096]{1,0:T(8,128)(2,1)} %bitcast.18, bf16[4096,128]{1,0:T(8,128)(2,1)} %constant.39.clone.basis_hbm, f32[128,128]{1,0:T(8,128)} %constant.40.clone.band_ref, f32[1,128]{1,0:T(1,128)} %constant.41.clone.inverse_ref), custom_call_target="tpu_custom_call" | custom-call | tf_op jit(solution)/shard_map/whiten/pallas_call | solution.py:139
  6.5 14.8 %all-to-all-start = ((bf16[128,2,128]{2,1,0:T(2,128)(2,1)}), bf16[128,2,128]{2,1,0:T(2,128)(2,1)S(1)}, u32[]{:S(2)}, u32[]{:S(2)}) async-start(bf16[128,2,128]{2,1,0:T(2,128)(2,1)} %bitcast.19), calls=%async_computation | async-start | bytes 131072 | tf_op jit(solution)/shard_map/all_to_all | solution.py:404
  21.3 0.7 compare_select_fusion.slot_ref
  22.0 9.9 %all-to-all-done = bf16[128,2,128]{2,1,0:T(2,128)(2,1)S(1)} async-done(((bf16[128,2,128]{2,1,0:T(2,128)(2,1)}), bf16[128,2,128]{2,1,0:T(2,128)(2,1)S(1)}, u32[]{:S(2)}, u32[]{:S(2)}) %all-to-all-start) | async-done | bytes 65568 | tf_op jit(solution)/shard_map/all_to_all | solution.py:404
  31.9 0.4 select.1.mine_ref
  32.3 0.7 collective-permute-start
  32.9 3.6 %collective-permute-start.1 = (bf16[16,1024]{1,0:T(8,128)(2,1)S(1)}, bf16[16,1024]{1,0:T(8,128)(2,1)S(1)}, u32[]{:S(2)}, u32[]{:S(2)}) collective-permute-start(bf16[16,1024]{1,0:T(8,128)(2,1)S(1)} %select.1.mine_ref), channel_id=1, source_target_pairs={{0,128},{128,129},{129,1},{1,0},{2,130},{130,131},{131,3},{3,2},{4... | collective-permute-start | bytes 98312 | tf_op jit(solution)/shard_map/ppermute | solution.py:409
  36.6 1.6 %collective-permute-done.1 = bf16[16,1024]{1,0:T(8,128)(2,1)S(1)} collective-permute-done((bf16[16,1024]{1,0:T(8,128)(2,1)S(1)}, bf16[16,1024]{1,0:T(8,128)(2,1)S(1)}, u32[]{:S(2)}, u32[]{:S(2)}) %collective-permute-start.1) | collective-permute-done | bytes 32800 | tf_op jit(solution)/shard_map/ppermute | solution.py:409
  38.2 0.9 %collective-permute-start.2 = (bf16[2,16,1024]{2,1,0:T(8,128)(2,1)S(1)}, bf16[2,16,1024]{2,1,0:T(8,128)(2,1)S(1)}, u32[]{:S(2)}, u32[]{:S(2)}) collective-permute-start(bf16[2,16,1024]{2,1,0:T(8,128)(2,1)S(1)} %pad_maximum_fusion.1), channel_id=1, source_target_pairs={{0,96},{32,0},{64,32},{96,64},{1,97},{33,1},{65,33},{97,65},{2,98}... | collective-permute-start | bytes 196616 | tf_op jit(solution)/shard_map/ppermute | solution.py:397
  39.1 1.4 %collective-permute-start.3 = (bf16[2,16,1024]{2,1,0:T(8,128)(2,1)S(1)}, bf16[2,16,1024]{2,1,0:T(8,128)(2,1)S(1)}, u32[]{:S(2)}, u32[]{:S(2)}) collective-permute-start(bf16[2,16,1024]{2,1,0:T(8,128)(2,1)S(1)} %pad_maximum_fusion.1), channel_id=1, source_target_pairs={{0,64},{32,96},{64,0},{96,32},{1,65},{33,97},{65,1},{97,33},{2,66}... | collective-permute-start | bytes 196616 | tf_op jit(solution)/shard_map/ppermute | solution.py:397
  40.5 1.5 %collective-permute-start.5 = (bf16[16,1024]{1,0:T(8,128)(2,1)S(1)}, bf16[16,1024]{1,0:T(8,128)(2,1)S(1)}, u32[]{:S(2)}, u32[]{:S(2)}) collective-permute-start(bf16[16,1024]{1,0:T(8,128)(2,1)S(1)} %select.1.mine_ref), channel_id=1, source_target_pairs={{0,1},{1,0},{2,3},{3,2},{4,5},{5,4},{6,7},{7,6},{8,9},{9,8},{10,11... | collective-permute-start | bytes 98312 | tf_op jit(solution)/shard_map/ppermute | solution.py:397
  42.0 2.7 %collective-permute-done.5.other_ref = bf16[16,1024]{1,0:T(8,128)(2,1)S(1)} collective-permute-done((bf16[16,1024]{1,0:T(8,128)(2,1)S(1)}, bf16[16,1024]{1,0:T(8,128)(2,1)S(1)}, u32[]{:S(2)}, u32[]{:S(2)}) %collective-permute-start.5) | collective-permute-done | bytes 32800 | tf_op jit(solution)/shard_map/ppermute | solution.py:397
  44.8 0.5 collective-permute-start.10
  45.3 1.1 %collective-permute-start.6 = (bf16[4,2,16,1024]{3,2,1,0:T(8,128)(2,1)S(1)}, bf16[4,2,16,1024]{3,2,1,0:T(8,128)(2,1)S(1)}, u32[]{:S(2)}, u32[]{:S(2)}) collective-permute-start(bf16[4,2,16,1024]{3,2,1,0:T(8,128)(2,1)S(1)} %pad_maximum_fusion.rest_0_), channel_id=1, source_target_pairs={{0,4},{4,8},{8,12},{12,16},{16,20},{20,24},{24,28},{28,0},{1,5},{5... | collective-permute-start | bytes 786440 | tf_op jit(solution)/shard_map/ppermute | solution.py:397
  46.4 3.9 %collective-permute-start.18 = (bf16[4,2,16,1024]{3,2,1,0:T(8,128)(2,1)S(1)}, bf16[4,2,16,1024]{3,2,1,0:T(8,128)(2,1)S(1)}, u32[]{:S(2)}, u32[]{:S(2)}) collective-permute-start(bf16[4,2,16,1024]{3,2,1,0:T(8,128)(2,1)S(1)} %pad_maximum_fusion.rest_0_), channel_id=1, source_target_pairs={{0,2},{2,0},{1,3},{3,1},{4,6},{6,4},{5,7},{7,5},{8,10},{10,8},{9,1... | collective-permute-start | bytes 786440 | tf_op jit(solution)/shard_map/ppermute | solution.py:397
  50.3 0.2 pair_weights.1.weight_ref
  50.5 0.9 %copy-done = s32[16,2048]{1,0:T(8,128)S(1)} copy-done((s32[16,2048]{1,0:T(8,128)S(1)}, s32[16,2048]{1,0:T(8,128)}, u32[]{:S(2)}) %copy-start) | copy-done | bytes 131096
  51.4 0.8 copy-done.1
  52.2 1.3 %phases.1 = (f32[8,288,128]{2,1,0:T(8,128)S(1)}, bf16[128,128]{1,0:T(8,128)(2,1)S(1)}) custom-call(s32[4]{0:T(128)S(1)} %pad_add_fusion.place_ref, s32[16,2048]{1,0:T(8,128)S(1)} %copy-done, bf16[128,128]{1,0:T(8,128)(2,1)S(1)} %copy-done.1), custom_call_target="tpu_custom_call" | custom-call | flops 1048576 | bytes 65536 | tf_op jit(solution)/shard_map/phases/pallas_call | solution.py:230
  53.5 1.8 %collective-permute-start.11 = (bf16[4,2,16,1024]{3,2,1,0:T(8,128)(2,1)S(1)}, bf16[4,2,16,1024]{3,2,1,0:T(8,128)(2,1)S(1)}, u32[]{:S(2)}, u32[]{:S(2)}) collective-permute-start(bf16[4,2,16,1024]{3,2,1,0:T(8,128)(2,1)S(1)} %collective-permute-done.10.rest_1_), channel_id=1, source_target_pairs={{0,28},{4,0},{8,4},{12,8},{16,12},{20,16},{24,20},{28,24},{1,29},{... | collective-permute-start | bytes 786440 | tf_op jit(solution)/shard_map/ppermute | solution.py:397
  55.3 2.2 %correlate.5.rest_4_ = f32[16,4,8,32,128]{4,3,2,1,0:T(8,128)} custom-call(s32[4]{0:T(128)S(1)} %pad_add_fusion.place_ref, bf16[8,256,256]{2,1,0:T(8,128)(2,1)S(1)} %pair_weights.1.weight_ref, bf16[128,128]{1,0:T(8,128)(2,1)S(1)} %get-tuple-element.36.table_ref, f32[8,288,128]{2,1,0:T(8,128)S(1)} %get-tuple-element.37.turn_ref, ...), custom_call_target="tpu_custom_call" | custom-call | flops 2147483648 | bytes 65536 | tf_op jit(solution)/shard_map/correlate/pallas_call | solution.py:373
  57.6 1.3 %collective-permute-start.19 = (bf16[4,2,16,1024]{3,2,1,0:T(8,128)(2,1)S(1)}, bf16[4,2,16,1024]{3,2,1,0:T(8,128)(2,1)S(1)}, u32[]{:S(2)}, u32[]{:S(2)}) collective-permute-start(bf16[4,2,16,1024]{3,2,1,0:T(8,128)(2,1)S(1)} %collective-permute-done.6.rest_0_), channel_id=1, source_target_pairs={{0,2},{2,0},{1,3},{3,1},{4,6},{6,4},{5,7},{7,5},{8,10},{10,8},{9,1... | collective-permute-start | bytes 786440 | tf_op jit(solution)/shard_map/ppermute | solution.py:397
  58.9 4.3 %collective-permute-done.7.rest_0_ = bf16[4,2,16,1024]{3,2,1,0:T(8,128)(2,1)S(1)} collective-permute-done((bf16[4,2,16,1024]{3,2,1,0:T(8,128)(2,1)S(1)}, bf16[4,2,16,1024]{3,2,1,0:T(8,128)(2,1)S(1)}, u32[]{:S(2)}, u32[]{:S(2)}) %collective-permute-start.7) | collective-permute-done | bytes 262176 | tf_op jit(solution)/shard_map/ppermute | solution.py:397
  63.2 2.7 %collective-permute-start.12 = (bf16[4,2,16,1024]{3,2,1,0:T(8,128)(2,1)S(1)}, bf16[4,2,16,1024]{3,2,1,0:T(8,128)(2,1)S(1)}, u32[]{:S(2)}, u32[]{:S(2)}) collective-permute-start(bf16[4,2,16,1024]{3,2,1,0:T(8,128)(2,1)S(1)} %collective-permute-done.11.rest_1_), channel_id=1, source_target_pairs={{0,28},{4,0},{8,4},{12,8},{16,12},{20,16},{24,20},{28,24},{1,29},{... | collective-permute-start | bytes 786440 | tf_op jit(solution)/shard_map/ppermute | solution.py:397
  65.9 2.9 %correlate.6.rest_4_ = f32[16,4,8,32,128]{4,3,2,1,0:T(8,128)} custom-call(s32[4]{0:T(128)S(1)} %pad_add_fusion.place_ref, bf16[8,256,256]{2,1,0:T(8,128)(2,1)S(1)} %pair_weights.1.weight_ref, bf16[128,128]{1,0:T(8,128)(2,1)S(1)} %get-tuple-element.36.table_ref, f32[8,288,128]{2,1,0:T(8,128)S(1)} %get-tuple-element.37.turn_ref, ...), custom_call_target="tpu_custom_call", output_to_operand_aliasing={{}: (8, {})} | custom-call | flops 1073741824 | bytes 65536 | tf_op jit(solution)/shard_map/correlate/pallas_call | solution.py:373
  68.8 2.6 %collective-permute-start.21 = (bf16[4,2,16,1024]{3,2,1,0:T(8,128)(2,1)S(1)}, bf16[4,2,16,1024]{3,2,1,0:T(8,128)(2,1)S(1)}, u32[]{:S(2)}, u32[]{:S(2)}) collective-permute-start(bf16[4,2,16,1024]{3,2,1,0:T(8,128)(2,1)S(1)} %collective-permute-done.7.rest_0_), channel_id=1, source_target_pairs={{0,2},{2,0},{1,3},{3,1},{4,6},{6,4},{5,7},{7,5},{8,10},{10,8},{9,1... | collective-permute-start | bytes 786440 | tf_op jit(solution)/shard_map/ppermute | solution.py:397
  71.4 1.7 %collective-permute-start.16 = (bf16[4,2,16,1024]{3,2,1,0:T(8,128)(2,1)S(1)}, bf16[4,2,16,1024]{3,2,1,0:T(8,128)(2,1)S(1)}, u32[]{:S(2)}, u32[]{:S(2)}) collective-permute-start(bf16[4,2,16,1024]{3,2,1,0:T(8,128)(2,1)S(1)} %collective-permute-done.8.rest_0_), channel_id=1, source_target_pairs={{0,2},{2,0},{1,3},{3,1},{4,6},{6,4},{5,7},{7,5},{8,10},{10,8},{9,1... | collective-permute-start | bytes 786440 | tf_op jit(solution)/shard_map/ppermute | solution.py:397
  73.3 2.7 %collective-permute-start.13 = (bf16[2,2,16,1024]{3,2,1,0:T(8,128)(2,1)S(1)}, bf16[2,2,16,1024]{3,2,1,0:T(8,128)(2,1)S(1)}, u32[]{:S(2)}, u32[]{:S(2)}) collective-permute-start(bf16[2,2,16,1024]{3,2,1,0:T(8,128)(2,1)S(1)} %slice.9), channel_id=1, source_target_pairs={{0,28},{4,0},{8,4},{12,8},{16,12},{20,16},{24,20},{28,24},{1,29},{... | collective-permute-start | bytes 393224 | tf_op jit(solution)/shard_map/ppermute | solution.py:397
  76.0 2.9 %correlate.7.rest_4_ = f32[16,4,8,32,128]{4,3,2,1,0:T(8,128)} custom-call(s32[4]{0:T(128)S(1)} %pad_add_fusion.place_ref, bf16[8,256,256]{2,1,0:T(8,128)(2,1)S(1)} %pair_weights.1.weight_ref, bf16[128,128]{1,0:T(8,128)(2,1)S(1)} %get-tuple-element.36.table_ref, f32[8,288,128]{2,1,0:T(8,128)S(1)} %get-tuple-element.37.turn_ref, ...), custom_call_target="tpu_custom_call", output_to_operand_aliasing={{}: (8, {})} | custom-call | flops 268435456 | bytes 65536 | tf_op jit(solution)/shard_map/correlate/pallas_call | solution.py:373
  79.0 1.4 %collective-permute-start.14 = (bf16[2,2,16,1024]{3,2,1,0:T(8,128)(2,1)S(1)}, bf16[2,2,16,1024]{3,2,1,0:T(8,128)(2,1)S(1)}, u32[]{:S(2)}, u32[]{:S(2)}) collective-permute-start(bf16[2,2,16,1024]{3,2,1,0:T(8,128)(2,1)S(1)} %collective-permute-done.9.rest_0_), channel_id=1, source_target_pairs={{0,2},{2,0},{1,3},{3,1},{4,6},{6,4},{5,7},{7,5},{8,10},{10,8},{9,1... | collective-permute-start | bytes 393224 | tf_op jit(solution)/shard_map/ppermute | solution.py:397
  80.4 2.9 %correlate.8.rest_4_ = f32[16,4,8,32,128]{4,3,2,1,0:T(8,128)} custom-call(s32[4]{0:T(128)S(1)} %pad_add_fusion.place_ref, bf16[8,256,256]{2,1,0:T(8,128)(2,1)S(1)} %pair_weights.1.weight_ref, bf16[128,128]{1,0:T(8,128)(2,1)S(1)} %get-tuple-element.36.table_ref, f32[8,288,128]{2,1,0:T(8,128)S(1)} %get-tuple-element.37.turn_ref, ...), custom_call_target="tpu_custom_call", output_to_operand_aliasing={{}: (8, {})} | custom-call | flops 2147483648 | bytes 65536 | tf_op jit(solution)/shard_map/correlate/pallas_call | solution.py:373
  83.3 2.2 %correlate.9 = f32[16,4,8,32,128]{4,3,2,1,0:T(8,128)} custom-call(s32[4]{0:T(128)S(1)} %pad_add_fusion.place_ref, bf16[8,256,256]{2,1,0:T(8,128)(2,1)S(1)} %pair_weights.1.weight_ref, bf16[128,128]{1,0:T(8,128)(2,1)S(1)} %get-tuple-element.36.table_ref, f32[8,288,128]{2,1,0:T(8,128)S(1)} %get-tuple-element.37.turn_ref, ...), custom_call_target="tpu_custom_call", output_to_operand_aliasing={{}: (8, {})} | custom-call | flops 1073741824 | bytes 65536 | tf_op jit(solution)/shard_map/correlate/pallas_call | solution.py:373
  (36 shorter events, 0.5 us)
Async XLA Ops:
  6.5 25.4 %all-to-all-start = ((bf16[128,2,128]{2,1,0:T(2,128)(2,1)}), bf16[128,2,128]{2,1,0:T(2,128)(2,1)S(1)}, u32[]{:S(2)}, u32[]{:S(2)}) async-start(bf16[128,2,128]{2,1,0:T(2,128)(2,1)} %bitcast.19), calls=%async_computation | async-start | bytes 131072 | tf_op jit(solution)/shard_map/all_to_all | solution.py:404
  32.3 4.3 %collective-permute-start = (bf16[16,1024]{1,0:T(8,128)(2,1)S(1)}, bf16[16,1024]{1,0:T(8,128)(2,1)S(1)}, u32[]{:S(2)}, u32[]{:S(2)}) collective-permute-start(bf16[16,1024]{1,0:T(8,128)(2,1)S(1)} %select.1.mine_ref), channel_id=1, source_target_pairs={{1,128},{128,1},{3,130},{130,3},{5,132},{132,5},{7,134},{134,7},{9... | collective-permute-start | bytes 98312 | tf_op jit(solution)/shard_map/ppermute | solution.py:410
  32.9 5.3 %collective-permute-start.1 = (bf16[16,1024]{1,0:T(8,128)(2,1)S(1)}, bf16[16,1024]{1,0:T(8,128)(2,1)S(1)}, u32[]{:S(2)}, u32[]{:S(2)}) collective-permute-start(bf16[16,1024]{1,0:T(8,128)(2,1)S(1)} %select.1.mine_ref), channel_id=1, source_target_pairs={{0,128},{128,129},{129,1},{1,0},{2,130},{130,131},{131,3},{3,2},{4... | collective-permute-start | bytes 98312 | tf_op jit(solution)/shard_map/ppermute | solution.py:409
  38.2 6.5 %collective-permute-start.2 = (bf16[2,16,1024]{2,1,0:T(8,128)(2,1)S(1)}, bf16[2,16,1024]{2,1,0:T(8,128)(2,1)S(1)}, u32[]{:S(2)}, u32[]{:S(2)}) collective-permute-start(bf16[2,16,1024]{2,1,0:T(8,128)(2,1)S(1)} %pad_maximum_fusion.1), channel_id=1, source_target_pairs={{0,96},{32,0},{64,32},{96,64},{1,97},{33,1},{65,33},{97,65},{2,98}... | collective-permute-start | bytes 196616 | tf_op jit(solution)/shard_map/ppermute | solution.py:397
  39.1 5.6 %collective-permute-start.3 = (bf16[2,16,1024]{2,1,0:T(8,128)(2,1)S(1)}, bf16[2,16,1024]{2,1,0:T(8,128)(2,1)S(1)}, u32[]{:S(2)}, u32[]{:S(2)}) collective-permute-start(bf16[2,16,1024]{2,1,0:T(8,128)(2,1)S(1)} %pad_maximum_fusion.1), channel_id=1, source_target_pairs={{0,64},{32,96},{64,0},{96,32},{1,65},{33,97},{65,1},{97,33},{2,66}... | collective-permute-start | bytes 196616 | tf_op jit(solution)/shard_map/ppermute | solution.py:397
  40.5 4.3 %collective-permute-start.4 = (bf16[2,16,1024]{2,1,0:T(8,128)(2,1)S(1)}, bf16[2,16,1024]{2,1,0:T(8,128)(2,1)S(1)}, u32[]{:S(2)}, u32[]{:S(2)}) collective-permute-start(bf16[2,16,1024]{2,1,0:T(8,128)(2,1)S(1)} %pad_maximum_fusion.1), channel_id=1, source_target_pairs={{0,32},{32,64},{64,96},{96,0},{1,33},{33,65},{65,97},{97,1},{2,34}... | collective-permute-start | bytes 196616 | tf_op jit(solution)/shard_map/ppermute | solution.py:397
  40.5 4.3 %collective-permute-start.5 = (bf16[16,1024]{1,0:T(8,128)(2,1)S(1)}, bf16[16,1024]{1,0:T(8,128)(2,1)S(1)}, u32[]{:S(2)}, u32[]{:S(2)}) collective-permute-start(bf16[16,1024]{1,0:T(8,128)(2,1)S(1)} %select.1.mine_ref), channel_id=1, source_target_pairs={{0,1},{1,0},{2,3},{3,2},{4,5},{5,4},{6,7},{7,6},{8,9},{9,8},{10,11... | collective-permute-start | bytes 98312 | tf_op jit(solution)/shard_map/ppermute | solution.py:397
  44.8 8.6 %collective-permute-start.10 = (bf16[4,2,16,1024]{3,2,1,0:T(8,128)(2,1)S(1)}, bf16[4,2,16,1024]{3,2,1,0:T(8,128)(2,1)S(1)}, u32[]{:S(2)}, u32[]{:S(2)}) collective-permute-start(bf16[4,2,16,1024]{3,2,1,0:T(8,128)(2,1)S(1)} %pad_maximum_fusion.rest_0_), channel_id=1, source_target_pairs={{0,28},{4,0},{8,4},{12,8},{16,12},{20,16},{24,20},{28,24},{1,29},{... | collective-permute-start | bytes 786440 | tf_op jit(solution)/shard_map/ppermute | solution.py:397
  45.3 10.0 %collective-permute-start.6 = (bf16[4,2,16,1024]{3,2,1,0:T(8,128)(2,1)S(1)}, bf16[4,2,16,1024]{3,2,1,0:T(8,128)(2,1)S(1)}, u32[]{:S(2)}, u32[]{:S(2)}) collective-permute-start(bf16[4,2,16,1024]{3,2,1,0:T(8,128)(2,1)S(1)} %pad_maximum_fusion.rest_0_), channel_id=1, source_target_pairs={{0,4},{4,8},{8,12},{12,16},{16,20},{20,24},{24,28},{28,0},{1,5},{5... | collective-permute-start | bytes 786440 | tf_op jit(solution)/shard_map/ppermute | solution.py:397
  46.4 9.0 %collective-permute-start.18 = (bf16[4,2,16,1024]{3,2,1,0:T(8,128)(2,1)S(1)}, bf16[4,2,16,1024]{3,2,1,0:T(8,128)(2,1)S(1)}, u32[]{:S(2)}, u32[]{:S(2)}) collective-permute-start(bf16[4,2,16,1024]{3,2,1,0:T(8,128)(2,1)S(1)} %pad_maximum_fusion.rest_0_), channel_id=1, source_target_pairs={{0,2},{2,0},{1,3},{3,1},{4,6},{6,4},{5,7},{7,5},{8,10},{10,8},{9,1... | collective-permute-start | bytes 786440 | tf_op jit(solution)/shard_map/ppermute | solution.py:397
  50.5 0.9 %copy-start = (s32[16,2048]{1,0:T(8,128)S(1)}, s32[16,2048]{1,0:T(8,128)}, u32[]{:S(2)}) copy-start(s32[16,2048]{1,0:T(8,128)} %lag_ref) | copy-start | bytes 393220
  51.4 0.8 copy-start.1
  53.5 9.7 %collective-permute-start.11 = (bf16[4,2,16,1024]{3,2,1,0:T(8,128)(2,1)S(1)}, bf16[4,2,16,1024]{3,2,1,0:T(8,128)(2,1)S(1)}, u32[]{:S(2)}, u32[]{:S(2)}) collective-permute-start(bf16[4,2,16,1024]{3,2,1,0:T(8,128)(2,1)S(1)} %collective-permute-done.10.rest_1_), channel_id=1, source_target_pairs={{0,28},{4,0},{8,4},{12,8},{16,12},{20,16},{24,20},{28,24},{1,29},{... | collective-permute-start | bytes 786440 | tf_op jit(solution)/shard_map/ppermute | solution.py:397
  55.3 7.9 %collective-permute-start.7 = (bf16[4,2,16,1024]{3,2,1,0:T(8,128)(2,1)S(1)}, bf16[4,2,16,1024]{3,2,1,0:T(8,128)(2,1)S(1)}, u32[]{:S(2)}, u32[]{:S(2)}) collective-permute-start(bf16[4,2,16,1024]{3,2,1,0:T(8,128)(2,1)S(1)} %collective-permute-done.6.rest_0_), channel_id=1, source_target_pairs={{0,4},{4,8},{8,12},{12,16},{16,20},{20,24},{24,28},{28,0},{1,5},{5... | collective-permute-start | bytes 786440 | tf_op jit(solution)/shard_map/ppermute | solution.py:397
  57.6 8.3 %collective-permute-start.19 = (bf16[4,2,16,1024]{3,2,1,0:T(8,128)(2,1)S(1)}, bf16[4,2,16,1024]{3,2,1,0:T(8,128)(2,1)S(1)}, u32[]{:S(2)}, u32[]{:S(2)}) collective-permute-start(bf16[4,2,16,1024]{3,2,1,0:T(8,128)(2,1)S(1)} %collective-permute-done.6.rest_0_), channel_id=1, source_target_pairs={{0,2},{2,0},{1,3},{3,1},{4,6},{6,4},{5,7},{7,5},{8,10},{10,8},{9,1... | collective-permute-start | bytes 786440 | tf_op jit(solution)/shard_map/ppermute | solution.py:397
  58.9 7.0 %collective-permute-start.20 = (bf16[4,2,16,1024]{3,2,1,0:T(8,128)(2,1)S(1)}, bf16[4,2,16,1024]{3,2,1,0:T(8,128)(2,1)S(1)}, u32[]{:S(2)}, u32[]{:S(2)}) collective-permute-start(bf16[4,2,16,1024]{3,2,1,0:T(8,128)(2,1)S(1)} %collective-permute-done.10.rest_1_), channel_id=1, source_target_pairs={{0,2},{2,0},{1,3},{3,1},{4,6},{6,4},{5,7},{7,5},{8,10},{10,8},{9,1... | collective-permute-start | bytes 786440 | tf_op jit(solution)/shard_map/ppermute | solution.py:397
  63.2 8.2 %collective-permute-start.8 = (bf16[4,2,16,1024]{3,2,1,0:T(8,128)(2,1)S(1)}, bf16[4,2,16,1024]{3,2,1,0:T(8,128)(2,1)S(1)}, u32[]{:S(2)}, u32[]{:S(2)}) collective-permute-start(bf16[4,2,16,1024]{3,2,1,0:T(8,128)(2,1)S(1)} %collective-permute-done.7.rest_0_), channel_id=1, source_target_pairs={{0,4},{4,8},{8,12},{12,16},{16,20},{20,24},{24,28},{28,0},{1,5},{5... | collective-permute-start | bytes 786440 | tf_op jit(solution)/shard_map/ppermute | solution.py:397
  63.2 9.9 %collective-permute-start.12 = (bf16[4,2,16,1024]{3,2,1,0:T(8,128)(2,1)S(1)}, bf16[4,2,16,1024]{3,2,1,0:T(8,128)(2,1)S(1)}, u32[]{:S(2)}, u32[]{:S(2)}) collective-permute-start(bf16[4,2,16,1024]{3,2,1,0:T(8,128)(2,1)S(1)} %collective-permute-done.11.rest_1_), channel_id=1, source_target_pairs={{0,28},{4,0},{8,4},{12,8},{16,12},{20,16},{24,20},{28,24},{1,29},{... | collective-permute-start | bytes 786440 | tf_op jit(solution)/shard_map/ppermute | solution.py:397
  68.8 4.5 %collective-permute-start.21 = (bf16[4,2,16,1024]{3,2,1,0:T(8,128)(2,1)S(1)}, bf16[4,2,16,1024]{3,2,1,0:T(8,128)(2,1)S(1)}, u32[]{:S(2)}, u32[]{:S(2)}) collective-permute-start(bf16[4,2,16,1024]{3,2,1,0:T(8,128)(2,1)S(1)} %collective-permute-done.7.rest_0_), channel_id=1, source_target_pairs={{0,2},{2,0},{1,3},{3,1},{4,6},{6,4},{5,7},{7,5},{8,10},{10,8},{9,1... | collective-permute-start | bytes 786440 | tf_op jit(solution)/shard_map/ppermute | solution.py:397
  71.4 4.6 %collective-permute-start.22 = (bf16[4,2,16,1024]{3,2,1,0:T(8,128)(2,1)S(1)}, bf16[4,2,16,1024]{3,2,1,0:T(8,128)(2,1)S(1)}, u32[]{:S(2)}, u32[]{:S(2)}) collective-permute-start(bf16[4,2,16,1024]{3,2,1,0:T(8,128)(2,1)S(1)} %collective-permute-done.11.rest_1_), channel_id=1, source_target_pairs={{0,2},{2,0},{1,3},{3,1},{4,6},{6,4},{5,7},{7,5},{8,10},{10,8},{9,1... | collective-permute-start | bytes 786440 | tf_op jit(solution)/shard_map/ppermute | solution.py:397
  71.4 9.0 %collective-permute-start.16 = (bf16[4,2,16,1024]{3,2,1,0:T(8,128)(2,1)S(1)}, bf16[4,2,16,1024]{3,2,1,0:T(8,128)(2,1)S(1)}, u32[]{:S(2)}, u32[]{:S(2)}) collective-permute-start(bf16[4,2,16,1024]{3,2,1,0:T(8,128)(2,1)S(1)} %collective-permute-done.8.rest_0_), channel_id=1, source_target_pairs={{0,2},{2,0},{1,3},{3,1},{4,6},{6,4},{5,7},{7,5},{8,10},{10,8},{9,1... | collective-permute-start | bytes 786440 | tf_op jit(solution)/shard_map/ppermute | solution.py:397
  73.1 7.2 %collective-permute-start.17 = (bf16[4,2,16,1024]{3,2,1,0:T(8,128)(2,1)S(1)}, bf16[4,2,16,1024]{3,2,1,0:T(8,128)(2,1)S(1)}, u32[]{:S(2)}, u32[]{:S(2)}) collective-permute-start(bf16[4,2,16,1024]{3,2,1,0:T(8,128)(2,1)S(1)} %collective-permute-done.12.rest_1_), channel_id=1, source_target_pairs={{0,2},{2,0},{1,3},{3,1},{4,6},{6,4},{5,7},{7,5},{8,10},{10,8},{9,1... | collective-permute-start | bytes 786440 | tf_op jit(solution)/shard_map/ppermute | solution.py:397
  73.2 5.8 %collective-permute-start.9 = (bf16[2,2,16,1024]{3,2,1,0:T(8,128)(2,1)S(1)}, bf16[2,2,16,1024]{3,2,1,0:T(8,128)(2,1)S(1)}, u32[]{:S(2)}, u32[]{:S(2)}) collective-permute-start(bf16[2,2,16,1024]{3,2,1,0:T(8,128)(2,1)S(1)} %slice.8), channel_id=1, source_target_pairs={{0,4},{4,8},{8,12},{12,16},{16,20},{20,24},{24,28},{28,0},{1,5},{5... | collective-permute-start | bytes 393224 | tf_op jit(solution)/shard_map/ppermute | solution.py:397
  73.3 7.1 %collective-permute-start.13 = (bf16[2,2,16,1024]{3,2,1,0:T(8,128)(2,1)S(1)}, bf16[2,2,16,1024]{3,2,1,0:T(8,128)(2,1)S(1)}, u32[]{:S(2)}, u32[]{:S(2)}) collective-permute-start(bf16[2,2,16,1024]{3,2,1,0:T(8,128)(2,1)S(1)} %slice.9), channel_id=1, source_target_pairs={{0,28},{4,0},{8,4},{12,8},{16,12},{20,16},{24,20},{28,24},{1,29},{... | collective-permute-start | bytes 393224 | tf_op jit(solution)/shard_map/ppermute | solution.py:397
  79.0 4.3 %collective-permute-start.14 = (bf16[2,2,16,1024]{3,2,1,0:T(8,128)(2,1)S(1)}, bf16[2,2,16,1024]{3,2,1,0:T(8,128)(2,1)S(1)}, u32[]{:S(2)}, u32[]{:S(2)}) collective-permute-start(bf16[2,2,16,1024]{3,2,1,0:T(8,128)(2,1)S(1)} %collective-permute-done.9.rest_0_), channel_id=1, source_target_pairs={{0,2},{2,0},{1,3},{3,1},{4,6},{6,4},{5,7},{7,5},{8,10},{10,8},{9,1... | collective-permute-start | bytes 393224 | tf_op jit(solution)/shard_map/ppermute | solution.py:397
  80.4 2.9 %collective-permute-start.15 = (bf16[2,2,16,1024]{3,2,1,0:T(8,128)(2,1)S(1)}, bf16[2,2,16,1024]{3,2,1,0:T(8,128)(2,1)S(1)}, u32[]{:S(2)}, u32[]{:S(2)}) collective-permute-start(bf16[2,2,16,1024]{3,2,1,0:T(8,128)(2,1)S(1)} %collective-permute-done.13.rest_1_), channel_id=1, source_target_pairs={{0,2},{2,0},{1,3},{3,1},{4,6},{6,4},{5,7},{7,5},{8,10},{10,8},{9,1... | collective-permute-start | bytes 393224 | tf_op jit(solution)/shard_map/ppermute | solution.py:397

commit v5 on v3

--- a/solution.py
+++ b/solution.py
@@ -112,12 +112,12 @@
         filtered = filtered.astype(jnp.bfloat16)
         if group == 0:
             basis_copy.wait()
-        for number, tile in enumerate(tiles):
-            spectrum += jnp.dot(
-                filtered[256 * number : 256 * (number + 1)],
-                basis_ref[256 * tile : 256 * (tile + 1), :],
-                preferred_element_type=jnp.float32,
-            )
+        samples = [filtered[256 * number : 256 * (number + 1)] for number in range(4)]
+        spectrum += jnp.dot(
+            jnp.concatenate(samples, axis=1),
+            basis_ref[1024 * group : 1024 * (group + 1), :],
+            preferred_element_type=jnp.float32,
+        )
     square = spectrum * spectrum
     magnitude = jnp.sqrt(square + swap_parts(square))
     amplitude = (

time: 84.6 us -> 84.3 us (level)
  no operation moved by 1% of the time
where the time goes in v5:
time: 84.3 us; the launch traced here: 84 us
  starting transfers between devices  48.4 us (57%)
  Pallas kernels  21.2 us (25%)
  waiting for transfers between devices  11.7 us (14%)
  local copies, waits for them, and re-layouts  1.68 us (2%)
    ppermute x21, starting transfers between devices, shift(): lax.ppermute(value, axis, [(at, (at + by) % size) for at in range(size)])  29.3 us
    all_to_all x1, starting transfers between devices, per_device(): lax.all_to_all(white, STA, split_axis=0, concat_axis=0, tiled=True)  14.8 us
    pallas_call x5, Pallas kernels, correlate(): pl.pallas_call(functools.partial(correlate_kernel, layout), grid_spec=plt...  13 us
    all_to_all x1, waiting for transfers between devices, per_device(): lax.all_to_all(white, STA, split_axis=0, concat_axis=0, tiled=True)  6.78 us
    pallas_call x1, Pallas kernels, whiten(): pl.pallas_call(whiten_kernel, out_shape=jax.ShapeDtypeStruct((256, 128),...  6.28 us
    ppermute x1, starting transfers between devices, per_device(): ring = lax.ppermute(mine, ('ylo', 'yhi'), [(0, 2), (2, 3), (3, 1), (1, 0)])  3.62 us
    ppermute x21, waiting for transfers between devices, shift(): lax.ppermute(value, axis, [(at, (at + by) % size) for at in range(size)])  3.33 us
  transfers between devices with their start and end apart: 24, of which 4 were waited for; matrix products, arithmetic and copies ran while one was open for 1% of the time, Pallas kernels for 15%

profile of v5, /device:TPU:1, one launch (start us, length us, event | category | flops | bytes accessed | tf_op | source)
XLA Modules:
  0.0 84.0 jit_solution(5530159142541300999)
XLA Ops:
  0.0 6.3 %whiten.1 = bf16[256,128]{1,0:T(8,128)(2,1)} custom-call(bf16[1,127]{1,0:T(2,128)(2,1)} %bitcast.24, bf16[256,4096]{1,0:T(8,128)(2,1)} %bitcast.18, bf16[4096,128]{1,0:T(8,128)(2,1)} %constant.39.clone.basis_hbm, f32[128,128]{1,0:T(8,128)} %constant.40.clone.band_ref, f32[1,128]{1,0:T(1,128)} %constant.41.clone.inverse_ref), custom_call_target="tpu_custom_call" | custom-call | tf_op jit(solution)/shard_map/whiten/pallas_call | solution.py:139
  6.3 14.8 %all-to-all-start = ((bf16[128,2,128]{2,1,0:T(2,128)(2,1)}), bf16[128,2,128]{2,1,0:T(2,128)(2,1)S(1)}, u32[]{:S(2)}, u32[]{:S(2)}) async-start(bf16[128,2,128]{2,1,0:T(2,128)(2,1)} %bitcast.19), calls=%async_computation | async-start | bytes 131072 | tf_op jit(solution)/shard_map/all_to_all | solution.py:405
  21.2 0.9 %copy-done = s32[16,2048]{1,0:T(8,128)S(1)} copy-done((s32[16,2048]{1,0:T(8,128)S(1)}, s32[16,2048]{1,0:T(8,128)}, u32[]{:S(2)}) %copy-start) | copy-done | bytes 131096
  22.1 0.8 copy-done.1
  22.8 1.3 %phases.1 = (f32[8,288,128]{2,1,0:T(8,128)S(1)}, bf16[128,128]{1,0:T(8,128)(2,1)S(1)}) custom-call(s32[4]{0:T(128)S(1)} %pad_add_fusion.place_ref, s32[16,2048]{1,0:T(8,128)S(1)} %copy-done, bf16[128,128]{1,0:T(8,128)(2,1)S(1)} %copy-done.1), custom_call_target="tpu_custom_call" | custom-call | flops 1048576 | bytes 65536 | tf_op jit(solution)/shard_map/phases/pallas_call | solution.py:230
  24.2 0.7 compare_select_fusion.slot_ref
  24.9 6.8 %all-to-all-done = bf16[128,2,128]{2,1,0:T(2,128)(2,1)S(1)} async-done(((bf16[128,2,128]{2,1,0:T(2,128)(2,1)}), bf16[128,2,128]{2,1,0:T(2,128)(2,1)S(1)}, u32[]{:S(2)}, u32[]{:S(2)}) %all-to-all-start) | async-done | bytes 65568 | tf_op jit(solution)/shard_map/all_to_all | solution.py:405
  31.7 0.4 select.1.mine_ref
  32.0 0.7 collective-permute-start
  32.7 3.6 %collective-permute-start.1 = (bf16[16,1024]{1,0:T(8,128)(2,1)S(1)}, bf16[16,1024]{1,0:T(8,128)(2,1)S(1)}, u32[]{:S(2)}, u32[]{:S(2)}) collective-permute-start(bf16[16,1024]{1,0:T(8,128)(2,1)S(1)} %select.1.mine_ref), channel_id=1, source_target_pairs={{0,128},{128,129},{129,1},{1,0},{2,130},{130,131},{131,3},{3,2},{4... | collective-permute-start | bytes 98312 | tf_op jit(solution)/shard_map/ppermute | solution.py:412
  36.3 1.6 %collective-permute-done.1 = bf16[16,1024]{1,0:T(8,128)(2,1)S(1)} collective-permute-done((bf16[16,1024]{1,0:T(8,128)(2,1)S(1)}, bf16[16,1024]{1,0:T(8,128)(2,1)S(1)}, u32[]{:S(2)}, u32[]{:S(2)}) %collective-permute-start.1) | collective-permute-done | bytes 32800 | tf_op jit(solution)/shard_map/ppermute | solution.py:412
  38.0 0.9 %collective-permute-start.2 = (bf16[2,16,1024]{2,1,0:T(8,128)(2,1)S(1)}, bf16[2,16,1024]{2,1,0:T(8,128)(2,1)S(1)}, u32[]{:S(2)}, u32[]{:S(2)}) collective-permute-start(bf16[2,16,1024]{2,1,0:T(8,128)(2,1)S(1)} %pad_maximum_fusion.1), channel_id=1, source_target_pairs={{0,96},{32,0},{64,32},{96,64},{1,97},{33,1},{65,33},{97,65},{2,98}... | collective-permute-start | bytes 196616 | tf_op jit(solution)/shard_map/ppermute | solution.py:397
  38.9 1.4 %collective-permute-start.3 = (bf16[2,16,1024]{2,1,0:T(8,128)(2,1)S(1)}, bf16[2,16,1024]{2,1,0:T(8,128)(2,1)S(1)}, u32[]{:S(2)}, u32[]{:S(2)}) collective-permute-start(bf16[2,16,1024]{2,1,0:T(8,128)(2,1)S(1)} %pad_maximum_fusion.1), channel_id=1, source_target_pairs={{0,64},{32,96},{64,0},{96,32},{1,65},{33,97},{65,1},{97,33},{2,66}... | collective-permute-start | bytes 196616 | tf_op jit(solution)/shard_map/ppermute | solution.py:397
  40.3 1.5 %collective-permute-start.5 = (bf16[16,1024]{1,0:T(8,128)(2,1)S(1)}, bf16[16,1024]{1,0:T(8,128)(2,1)S(1)}, u32[]{:S(2)}, u32[]{:S(2)}) collective-permute-start(bf16[16,1024]{1,0:T(8,128)(2,1)S(1)} %select.1.mine_ref), channel_id=1, source_target_pairs={{0,1},{1,0},{2,3},{3,2},{4,5},{5,4},{6,7},{7,6},{8,9},{9,8},{10,11... | collective-permute-start | bytes 98312 | tf_op jit(solution)/shard_map/ppermute | solution.py:397
  41.7 2.8 %collective-permute-done.5.other_ref = bf16[16,1024]{1,0:T(8,128)(2,1)S(1)} collective-permute-done((bf16[16,1024]{1,0:T(8,128)(2,1)S(1)}, bf16[16,1024]{1,0:T(8,128)(2,1)S(1)}, u32[]{:S(2)}, u32[]{:S(2)}) %collective-permute-start.5) | collective-permute-done | bytes 32800 | tf_op jit(solution)/shard_map/ppermute | solution.py:397
  44.6 0.5 collective-permute-start.10
  45.1 1.1 %collective-permute-start.6 = (bf16[4,2,16,1024]{3,2,1,0:T(8,128)(2,1)S(1)}, bf16[4,2,16,1024]{3,2,1,0:T(8,128)(2,1)S(1)}, u32[]{:S(2)}, u32[]{:S(2)}) collective-permute-start(bf16[4,2,16,1024]{3,2,1,0:T(8,128)(2,1)S(1)} %pad_maximum_fusion.rest_0_), channel_id=1, source_target_pairs={{0,4},{4,8},{8,12},{12,16},{16,20},{20,24},{24,28},{28,0},{1,5},{5... | collective-permute-start | bytes 786440 | tf_op jit(solution)/shard_map/ppermute | solution.py:397
  46.2 3.9 %collective-permute-start.18 = (bf16[4,2,16,1024]{3,2,1,0:T(8,128)(2,1)S(1)}, bf16[4,2,16,1024]{3,2,1,0:T(8,128)(2,1)S(1)}, u32[]{:S(2)}, u32[]{:S(2)}) collective-permute-start(bf16[4,2,16,1024]{3,2,1,0:T(8,128)(2,1)S(1)} %pad_maximum_fusion.rest_0_), channel_id=1, source_target_pairs={{0,2},{2,0},{1,3},{3,1},{4,6},{6,4},{5,7},{7,5},{8,10},{10,8},{9,1... | collective-permute-start | bytes 786440 | tf_op jit(solution)/shard_map/ppermute | solution.py:397
  50.3 1.8 %collective-permute-start.11 = (bf16[4,2,16,1024]{3,2,1,0:T(8,128)(2,1)S(1)}, bf16[4,2,16,1024]{3,2,1,0:T(8,128)(2,1)S(1)}, u32[]{:S(2)}, u32[]{:S(2)}) collective-permute-start(bf16[4,2,16,1024]{3,2,1,0:T(8,128)(2,1)S(1)} %collective-permute-done.10.rest_1_), channel_id=1, source_target_pairs={{0,28},{4,0},{8,4},{12,8},{16,12},{20,16},{24,20},{28,24},{1,29},{... | collective-permute-start | bytes 786440 | tf_op jit(solution)/shard_map/ppermute | solution.py:397
  52.1 2.2 %correlate.5.rest_4_ = f32[16,4,8,32,128]{4,3,2,1,0:T(8,128)} custom-call(s32[4]{0:T(128)S(1)} %pad_add_fusion.place_ref, bf16[8,256,256]{2,1,0:T(8,128)(2,1)S(1)} %pair_weights.1.weight_ref, bf16[128,128]{1,0:T(8,128)(2,1)S(1)} %get-tuple-element.37.table_ref, f32[8,288,128]{2,1,0:T(8,128)S(1)} %get-tuple-element.38.turn_ref, ...), custom_call_target="tpu_custom_call" | custom-call | flops 2147483648 | bytes 65536 | tf_op jit(solution)/shard_map/correlate/pallas_call | solution.py:373
  54.4 5.1 %collective-permute-start.19 = (bf16[4,2,16,1024]{3,2,1,0:T(8,128)(2,1)S(1)}, bf16[4,2,16,1024]{3,2,1,0:T(8,128)(2,1)S(1)}, u32[]{:S(2)}, u32[]{:S(2)}) collective-permute-start(bf16[4,2,16,1024]{3,2,1,0:T(8,128)(2,1)S(1)} %collective-permute-done.6.rest_0_), channel_id=1, source_target_pairs={{0,2},{2,0},{1,3},{3,1},{4,6},{6,4},{5,7},{7,5},{8,10},{10,8},{9,1... | collective-permute-start | bytes 786440 | tf_op jit(solution)/shard_map/ppermute | solution.py:397
  59.5 0.5 collective-permute-start.8
  60.0 2.2 %collective-permute-start.12 = (bf16[4,2,16,1024]{3,2,1,0:T(8,128)(2,1)S(1)}, bf16[4,2,16,1024]{3,2,1,0:T(8,128)(2,1)S(1)}, u32[]{:S(2)}, u32[]{:S(2)}) collective-permute-start(bf16[4,2,16,1024]{3,2,1,0:T(8,128)(2,1)S(1)} %collective-permute-done.11.rest_1_), channel_id=1, source_target_pairs={{0,28},{4,0},{8,4},{12,8},{16,12},{20,16},{24,20},{28,24},{1,29},{... | collective-permute-start | bytes 786440 | tf_op jit(solution)/shard_map/ppermute | solution.py:397
  62.2 2.9 %correlate.6.rest_4_ = f32[16,4,8,32,128]{4,3,2,1,0:T(8,128)} custom-call(s32[4]{0:T(128)S(1)} %pad_add_fusion.place_ref, bf16[8,256,256]{2,1,0:T(8,128)(2,1)S(1)} %pair_weights.1.weight_ref, bf16[128,128]{1,0:T(8,128)(2,1)S(1)} %get-tuple-element.37.table_ref, f32[8,288,128]{2,1,0:T(8,128)S(1)} %get-tuple-element.38.turn_ref, ...), custom_call_target="tpu_custom_call", output_to_operand_aliasing={{}: (8, {})} | custom-call | flops 1073741824 | bytes 65536 | tf_op jit(solution)/shard_map/correlate/pallas_call | solution.py:373
  65.0 4.9 %collective-permute-start.21 = (bf16[4,2,16,1024]{3,2,1,0:T(8,128)(2,1)S(1)}, bf16[4,2,16,1024]{3,2,1,0:T(8,128)(2,1)S(1)}, u32[]{:S(2)}, u32[]{:S(2)}) collective-permute-start(bf16[4,2,16,1024]{3,2,1,0:T(8,128)(2,1)S(1)} %collective-permute-done.7.rest_0_), channel_id=1, source_target_pairs={{0,2},{2,0},{1,3},{3,1},{4,6},{6,4},{5,7},{7,5},{8,10},{10,8},{9,1... | collective-permute-start | bytes 786440 | tf_op jit(solution)/shard_map/ppermute | solution.py:397
  70.0 1.5 %collective-permute-start.16 = (bf16[4,2,16,1024]{3,2,1,0:T(8,128)(2,1)S(1)}, bf16[4,2,16,1024]{3,2,1,0:T(8,128)(2,1)S(1)}, u32[]{:S(2)}, u32[]{:S(2)}) collective-permute-start(bf16[4,2,16,1024]{3,2,1,0:T(8,128)(2,1)S(1)} %collective-permute-done.8.rest_0_), channel_id=1, source_target_pairs={{0,2},{2,0},{1,3},{3,1},{4,6},{6,4},{5,7},{7,5},{8,10},{10,8},{9,1... | collective-permute-start | bytes 786440 | tf_op jit(solution)/shard_map/ppermute | solution.py:397
  71.6 3.0 %collective-permute-start.13 = (bf16[2,2,16,1024]{3,2,1,0:T(8,128)(2,1)S(1)}, bf16[2,2,16,1024]{3,2,1,0:T(8,128)(2,1)S(1)}, u32[]{:S(2)}, u32[]{:S(2)}) collective-permute-start(bf16[2,2,16,1024]{3,2,1,0:T(8,128)(2,1)S(1)} %slice.9), channel_id=1, source_target_pairs={{0,28},{4,0},{8,4},{12,8},{16,12},{20,16},{24,20},{28,24},{1,29},{... | collective-permute-start | bytes 393224 | tf_op jit(solution)/shard_map/ppermute | solution.py:397
  74.6 2.9 %correlate.7.rest_4_ = f32[16,4,8,32,128]{4,3,2,1,0:T(8,128)} custom-call(s32[4]{0:T(128)S(1)} %pad_add_fusion.place_ref, bf16[8,256,256]{2,1,0:T(8,128)(2,1)S(1)} %pair_weights.1.weight_ref, bf16[128,128]{1,0:T(8,128)(2,1)S(1)} %get-tuple-element.37.table_ref, f32[8,288,128]{2,1,0:T(8,128)S(1)} %get-tuple-element.38.turn_ref, ...), custom_call_target="tpu_custom_call", output_to_operand_aliasing={{}: (8, {})} | custom-call | flops 268435456 | bytes 65536 | tf_op jit(solution)/shard_map/correlate/pallas_call | solution.py:373
  77.5 0.4 collective-permute-done.9.rest_0_
  77.9 1.0 %collective-permute-start.14 = (bf16[2,2,16,1024]{3,2,1,0:T(8,128)(2,1)S(1)}, bf16[2,2,16,1024]{3,2,1,0:T(8,128)(2,1)S(1)}, u32[]{:S(2)}, u32[]{:S(2)}) collective-permute-start(bf16[2,2,16,1024]{3,2,1,0:T(8,128)(2,1)S(1)} %collective-permute-done.9.rest_0_), channel_id=1, source_target_pairs={{0,2},{2,0},{1,3},{3,1},{4,6},{6,4},{5,7},{7,5},{8,10},{10,8},{9,1... | collective-permute-start | bytes 393224 | tf_op jit(solution)/shard_map/ppermute | solution.py:397
  79.0 2.9 %correlate.8.rest_4_ = f32[16,4,8,32,128]{4,3,2,1,0:T(8,128)} custom-call(s32[4]{0:T(128)S(1)} %pad_add_fusion.place_ref, bf16[8,256,256]{2,1,0:T(8,128)(2,1)S(1)} %pair_weights.1.weight_ref, bf16[128,128]{1,0:T(8,128)(2,1)S(1)} %get-tuple-element.37.table_ref, f32[8,288,128]{2,1,0:T(8,128)S(1)} %get-tuple-element.38.turn_ref, ...), custom_call_target="tpu_custom_call", output_to_operand_aliasing={{}: (8, {})} | custom-call | flops 2147483648 | bytes 65536 | tf_op jit(solution)/shard_map/correlate/pallas_call | solution.py:373
  81.8 2.2 %correlate.9 = f32[16,4,8,32,128]{4,3,2,1,0:T(8,128)} custom-call(s32[4]{0:T(128)S(1)} %pad_add_fusion.place_ref, bf16[8,256,256]{2,1,0:T(8,128)(2,1)S(1)} %pair_weights.1.weight_ref, bf16[128,128]{1,0:T(8,128)(2,1)S(1)} %get-tuple-element.37.table_ref, f32[8,288,128]{2,1,0:T(8,128)S(1)} %get-tuple-element.38.turn_ref, ...), custom_call_target="tpu_custom_call", output_to_operand_aliasing={{}: (8, {})} | custom-call | flops 1073741824 | bytes 65536 | tf_op jit(solution)/shard_map/correlate/pallas_call | solution.py:373
  (36 shorter events, 0.6 us)
Async XLA Ops:
  6.3 25.4 %all-to-all-start = ((bf16[128,2,128]{2,1,0:T(2,128)(2,1)}), bf16[128,2,128]{2,1,0:T(2,128)(2,1)S(1)}, u32[]{:S(2)}, u32[]{:S(2)}) async-start(bf16[128,2,128]{2,1,0:T(2,128)(2,1)} %bitcast.19), calls=%async_computation | async-start | bytes 131072 | tf_op jit(solution)/shard_map/all_to_all | solution.py:405
  21.2 0.9 %copy-start = (s32[16,2048]{1,0:T(8,128)S(1)}, s32[16,2048]{1,0:T(8,128)}, u32[]{:S(2)}) copy-start(s32[16,2048]{1,0:T(8,128)} %lag_ref) | copy-start | bytes 393220
  22.1 0.8 copy-start.1
  32.0 4.3 %collective-permute-start = (bf16[16,1024]{1,0:T(8,128)(2,1)S(1)}, bf16[16,1024]{1,0:T(8,128)(2,1)S(1)}, u32[]{:S(2)}, u32[]{:S(2)}) collective-permute-start(bf16[16,1024]{1,0:T(8,128)(2,1)S(1)} %select.1.mine_ref), channel_id=1, source_target_pairs={{1,128},{128,1},{3,130},{130,3},{5,132},{132,5},{7,134},{134,7},{9... | collective-permute-start | bytes 98312 | tf_op jit(solution)/shard_map/ppermute | solution.py:413
  32.7 5.3 %collective-permute-start.1 = (bf16[16,1024]{1,0:T(8,128)(2,1)S(1)}, bf16[16,1024]{1,0:T(8,128)(2,1)S(1)}, u32[]{:S(2)}, u32[]{:S(2)}) collective-permute-start(bf16[16,1024]{1,0:T(8,128)(2,1)S(1)} %select.1.mine_ref), channel_id=1, source_target_pairs={{0,128},{128,129},{129,1},{1,0},{2,130},{130,131},{131,3},{3,2},{4... | collective-permute-start | bytes 98312 | tf_op jit(solution)/shard_map/ppermute | solution.py:412
  38.0 6.5 %collective-permute-start.2 = (bf16[2,16,1024]{2,1,0:T(8,128)(2,1)S(1)}, bf16[2,16,1024]{2,1,0:T(8,128)(2,1)S(1)}, u32[]{:S(2)}, u32[]{:S(2)}) collective-permute-start(bf16[2,16,1024]{2,1,0:T(8,128)(2,1)S(1)} %pad_maximum_fusion.1), channel_id=1, source_target_pairs={{0,96},{32,0},{64,32},{96,64},{1,97},{33,1},{65,33},{97,65},{2,98}... | collective-permute-start | bytes 196616 | tf_op jit(solution)/shard_map/ppermute | solution.py:397
  38.9 5.6 %collective-permute-start.3 = (bf16[2,16,1024]{2,1,0:T(8,128)(2,1)S(1)}, bf16[2,16,1024]{2,1,0:T(8,128)(2,1)S(1)}, u32[]{:S(2)}, u32[]{:S(2)}) collective-permute-start(bf16[2,16,1024]{2,1,0:T(8,128)(2,1)S(1)} %pad_maximum_fusion.1), channel_id=1, source_target_pairs={{0,64},{32,96},{64,0},{96,32},{1,65},{33,97},{65,1},{97,33},{2,66}... | collective-permute-start | bytes 196616 | tf_op jit(solution)/shard_map/ppermute | solution.py:397
  40.3 4.3 %collective-permute-start.4 = (bf16[2,16,1024]{2,1,0:T(8,128)(2,1)S(1)}, bf16[2,16,1024]{2,1,0:T(8,128)(2,1)S(1)}, u32[]{:S(2)}, u32[]{:S(2)}) collective-permute-start(bf16[2,16,1024]{2,1,0:T(8,128)(2,1)S(1)} %pad_maximum_fusion.1), channel_id=1, source_target_pairs={{0,32},{32,64},{64,96},{96,0},{1,33},{33,65},{65,97},{97,1},{2,34}... | collective-permute-start | bytes 196616 | tf_op jit(solution)/shard_map/ppermute | solution.py:397
  40.3 4.3 %collective-permute-start.5 = (bf16[16,1024]{1,0:T(8,128)(2,1)S(1)}, bf16[16,1024]{1,0:T(8,128)(2,1)S(1)}, u32[]{:S(2)}, u32[]{:S(2)}) collective-permute-start(bf16[16,1024]{1,0:T(8,128)(2,1)S(1)} %select.1.mine_ref), channel_id=1, source_target_pairs={{0,1},{1,0},{2,3},{3,2},{4,5},{5,4},{6,7},{7,6},{8,9},{9,8},{10,11... | collective-permute-start | bytes 98312 | tf_op jit(solution)/shard_map/ppermute | solution.py:397
  44.6 5.6 %collective-permute-start.10 = (bf16[4,2,16,1024]{3,2,1,0:T(8,128)(2,1)S(1)}, bf16[4,2,16,1024]{3,2,1,0:T(8,128)(2,1)S(1)}, u32[]{:S(2)}, u32[]{:S(2)}) collective-permute-start(bf16[4,2,16,1024]{3,2,1,0:T(8,128)(2,1)S(1)} %pad_maximum_fusion.rest_0_), channel_id=1, source_target_pairs={{0,28},{4,0},{8,4},{12,8},{16,12},{20,16},{24,20},{28,24},{1,29},{... | collective-permute-start | bytes 786440 | tf_op jit(solution)/shard_map/ppermute | solution.py:397
  45.1 7.0 %collective-permute-start.6 = (bf16[4,2,16,1024]{3,2,1,0:T(8,128)(2,1)S(1)}, bf16[4,2,16,1024]{3,2,1,0:T(8,128)(2,1)S(1)}, u32[]{:S(2)}, u32[]{:S(2)}) collective-permute-start(bf16[4,2,16,1024]{3,2,1,0:T(8,128)(2,1)S(1)} %pad_maximum_fusion.rest_0_), channel_id=1, source_target_pairs={{0,4},{4,8},{8,12},{12,16},{16,20},{20,24},{24,28},{28,0},{1,5},{5... | collective-permute-start | bytes 786440 | tf_op jit(solution)/shard_map/ppermute | solution.py:397
  46.2 6.0 %collective-permute-start.18 = (bf16[4,2,16,1024]{3,2,1,0:T(8,128)(2,1)S(1)}, bf16[4,2,16,1024]{3,2,1,0:T(8,128)(2,1)S(1)}, u32[]{:S(2)}, u32[]{:S(2)}) collective-permute-start(bf16[4,2,16,1024]{3,2,1,0:T(8,128)(2,1)S(1)} %pad_maximum_fusion.rest_0_), channel_id=1, source_target_pairs={{0,2},{2,0},{1,3},{3,1},{4,6},{6,4},{5,7},{7,5},{8,10},{10,8},{9,1... | collective-permute-start | bytes 786440 | tf_op jit(solution)/shard_map/ppermute | solution.py:397
  50.3 9.7 %collective-permute-start.11 = (bf16[4,2,16,1024]{3,2,1,0:T(8,128)(2,1)S(1)}, bf16[4,2,16,1024]{3,2,1,0:T(8,128)(2,1)S(1)}, u32[]{:S(2)}, u32[]{:S(2)}) collective-permute-start(bf16[4,2,16,1024]{3,2,1,0:T(8,128)(2,1)S(1)} %collective-permute-done.10.rest_1_), channel_id=1, source_target_pairs={{0,28},{4,0},{8,4},{12,8},{16,12},{20,16},{24,20},{28,24},{1,29},{... | collective-permute-start | bytes 786440 | tf_op jit(solution)/shard_map/ppermute | solution.py:397
  52.1 7.3 %collective-permute-start.7 = (bf16[4,2,16,1024]{3,2,1,0:T(8,128)(2,1)S(1)}, bf16[4,2,16,1024]{3,2,1,0:T(8,128)(2,1)S(1)}, u32[]{:S(2)}, u32[]{:S(2)}) collective-permute-start(bf16[4,2,16,1024]{3,2,1,0:T(8,128)(2,1)S(1)} %collective-permute-done.6.rest_0_), channel_id=1, source_target_pairs={{0,4},{4,8},{8,12},{12,16},{16,20},{20,24},{24,28},{28,0},{1,5},{5... | collective-permute-start | bytes 786440 | tf_op jit(solution)/shard_map/ppermute | solution.py:397
  54.4 7.8 %collective-permute-start.19 = (bf16[4,2,16,1024]{3,2,1,0:T(8,128)(2,1)S(1)}, bf16[4,2,16,1024]{3,2,1,0:T(8,128)(2,1)S(1)}, u32[]{:S(2)}, u32[]{:S(2)}) collective-permute-start(bf16[4,2,16,1024]{3,2,1,0:T(8,128)(2,1)S(1)} %collective-permute-done.6.rest_0_), channel_id=1, source_target_pairs={{0,2},{2,0},{1,3},{3,1},{4,6},{6,4},{5,7},{7,5},{8,10},{10,8},{9,1... | collective-permute-start | bytes 786440 | tf_op jit(solution)/shard_map/ppermute | solution.py:397
  59.5 2.7 %collective-permute-start.20 = (bf16[4,2,16,1024]{3,2,1,0:T(8,128)(2,1)S(1)}, bf16[4,2,16,1024]{3,2,1,0:T(8,128)(2,1)S(1)}, u32[]{:S(2)}, u32[]{:S(2)}) collective-permute-start(bf16[4,2,16,1024]{3,2,1,0:T(8,128)(2,1)S(1)} %collective-permute-done.10.rest_1_), channel_id=1, source_target_pairs={{0,2},{2,0},{1,3},{3,1},{4,6},{6,4},{5,7},{7,5},{8,10},{10,8},{9,1... | collective-permute-start | bytes 786440 | tf_op jit(solution)/shard_map/ppermute | solution.py:397
  59.5 10.5 %collective-permute-start.8 = (bf16[4,2,16,1024]{3,2,1,0:T(8,128)(2,1)S(1)}, bf16[4,2,16,1024]{3,2,1,0:T(8,128)(2,1)S(1)}, u32[]{:S(2)}, u32[]{:S(2)}) collective-permute-start(bf16[4,2,16,1024]{3,2,1,0:T(8,128)(2,1)S(1)} %collective-permute-done.7.rest_0_), channel_id=1, source_target_pairs={{0,4},{4,8},{8,12},{12,16},{16,20},{20,24},{24,28},{28,0},{1,5},{5... | collective-permute-start | bytes 786440 | tf_op jit(solution)/shard_map/ppermute | solution.py:397
  60.0 11.4 %collective-permute-start.12 = (bf16[4,2,16,1024]{3,2,1,0:T(8,128)(2,1)S(1)}, bf16[4,2,16,1024]{3,2,1,0:T(8,128)(2,1)S(1)}, u32[]{:S(2)}, u32[]{:S(2)}) collective-permute-start(bf16[4,2,16,1024]{3,2,1,0:T(8,128)(2,1)S(1)} %collective-permute-done.11.rest_1_), channel_id=1, source_target_pairs={{0,28},{4,0},{8,4},{12,8},{16,12},{20,16},{24,20},{28,24},{1,29},{... | collective-permute-start | bytes 786440 | tf_op jit(solution)/shard_map/ppermute | solution.py:397
  65.0 6.5 %collective-permute-start.21 = (bf16[4,2,16,1024]{3,2,1,0:T(8,128)(2,1)S(1)}, bf16[4,2,16,1024]{3,2,1,0:T(8,128)(2,1)S(1)}, u32[]{:S(2)}, u32[]{:S(2)}) collective-permute-start(bf16[4,2,16,1024]{3,2,1,0:T(8,128)(2,1)S(1)} %collective-permute-done.7.rest_0_), channel_id=1, source_target_pairs={{0,2},{2,0},{1,3},{3,1},{4,6},{6,4},{5,7},{7,5},{8,10},{10,8},{9,1... | collective-permute-start | bytes 786440 | tf_op jit(solution)/shard_map/ppermute | solution.py:397
  69.9 4.7 %collective-permute-start.22 = (bf16[4,2,16,1024]{3,2,1,0:T(8,128)(2,1)S(1)}, bf16[4,2,16,1024]{3,2,1,0:T(8,128)(2,1)S(1)}, u32[]{:S(2)}, u32[]{:S(2)}) collective-permute-start(bf16[4,2,16,1024]{3,2,1,0:T(8,128)(2,1)S(1)} %collective-permute-done.11.rest_1_), channel_id=1, source_target_pairs={{0,2},{2,0},{1,3},{3,1},{4,6},{6,4},{5,7},{7,5},{8,10},{10,8},{9,1... | collective-permute-start | bytes 786440 | tf_op jit(solution)/shard_map/ppermute | solution.py:397
  70.0 9.0 %collective-permute-start.16 = (bf16[4,2,16,1024]{3,2,1,0:T(8,128)(2,1)S(1)}, bf16[4,2,16,1024]{3,2,1,0:T(8,128)(2,1)S(1)}, u32[]{:S(2)}, u32[]{:S(2)}) collective-permute-start(bf16[4,2,16,1024]{3,2,1,0:T(8,128)(2,1)S(1)} %collective-permute-done.8.rest_0_), channel_id=1, source_target_pairs={{0,2},{2,0},{1,3},{3,1},{4,6},{6,4},{5,7},{7,5},{8,10},{10,8},{9,1... | collective-permute-start | bytes 786440 | tf_op jit(solution)/shard_map/ppermute | solution.py:397
  71.4 7.5 %collective-permute-start.17 = (bf16[4,2,16,1024]{3,2,1,0:T(8,128)(2,1)S(1)}, bf16[4,2,16,1024]{3,2,1,0:T(8,128)(2,1)S(1)}, u32[]{:S(2)}, u32[]{:S(2)}) collective-permute-start(bf16[4,2,16,1024]{3,2,1,0:T(8,128)(2,1)S(1)} %collective-permute-done.12.rest_1_), channel_id=1, source_target_pairs={{0,2},{2,0},{1,3},{3,1},{4,6},{6,4},{5,7},{7,5},{8,10},{10,8},{9,1... | collective-permute-start | bytes 786440 | tf_op jit(solution)/shard_map/ppermute | solution.py:397
  71.4 6.4 %collective-permute-start.9 = (bf16[2,2,16,1024]{3,2,1,0:T(8,128)(2,1)S(1)}, bf16[2,2,16,1024]{3,2,1,0:T(8,128)(2,1)S(1)}, u32[]{:S(2)}, u32[]{:S(2)}) collective-permute-start(bf16[2,2,16,1024]{3,2,1,0:T(8,128)(2,1)S(1)} %slice.8), channel_id=1, source_target_pairs={{0,4},{4,8},{8,12},{12,16},{16,20},{20,24},{24,28},{28,0},{1,5},{5... | collective-permute-start | bytes 393224 | tf_op jit(solution)/shard_map/ppermute | solution.py:397
  71.6 7.4 %collective-permute-start.13 = (bf16[2,2,16,1024]{3,2,1,0:T(8,128)(2,1)S(1)}, bf16[2,2,16,1024]{3,2,1,0:T(8,128)(2,1)S(1)}, u32[]{:S(2)}, u32[]{:S(2)}) collective-permute-start(bf16[2,2,16,1024]{3,2,1,0:T(8,128)(2,1)S(1)} %slice.9), channel_id=1, source_target_pairs={{0,28},{4,0},{8,4},{12,8},{16,12},{20,16},{24,20},{28,24},{1,29},{... | collective-permute-start | bytes 393224 | tf_op jit(solution)/shard_map/ppermute | solution.py:397
  77.9 3.9 %collective-permute-start.14 = (bf16[2,2,16,1024]{3,2,1,0:T(8,128)(2,1)S(1)}, bf16[2,2,16,1024]{3,2,1,0:T(8,128)(2,1)S(1)}, u32[]{:S(2)}, u32[]{:S(2)}) collective-permute-start(bf16[2,2,16,1024]{3,2,1,0:T(8,128)(2,1)S(1)} %collective-permute-done.9.rest_0_), channel_id=1, source_target_pairs={{0,2},{2,0},{1,3},{3,1},{4,6},{6,4},{5,7},{7,5},{8,10},{10,8},{9,1... | collective-permute-start | bytes 393224 | tf_op jit(solution)/shard_map/ppermute | solution.py:397
  78.9 2.9 %collective-permute-start.15 = (bf16[2,2,16,1024]{3,2,1,0:T(8,128)(2,1)S(1)}, bf16[2,2,16,1024]{3,2,1,0:T(8,128)(2,1)S(1)}, u32[]{:S(2)}, u32[]{:S(2)}) collective-permute-start(bf16[2,2,16,1024]{3,2,1,0:T(8,128)(2,1)S(1)} %collective-permute-done.13.rest_1_), channel_id=1, source_target_pairs={{0,2},{2,0},{1,3},{3,1},{4,6},{6,4},{5,7},{7,5},{8,10},{10,8},{9,1... | collective-permute-start | bytes 393224 | tf_op jit(solution)/shard_map/ppermute | solution.py:397
